TPU v7x, 256 devices: a whole 4x4x8 slice. The times are simulated.
256 devices in a mesh: dp: 16 (over z, y_hi), head: 16 (over x, y_lo, core).
Axes of the slice: x: 4, y: 4 (y_hi: 2, y_lo: 2; y = y_hi * 2 + y_lo), z: 8, core: 2. Of those that a mesh axis runs over, the one named last changes fastest.
Arguments:
- q_latent: bfloat16 [4096, 1536], P('dp'), may hold values from -6 to 6
- kv_latent: bfloat16 [4096, 576], P('dp'), may hold values from -6 to 6
- q_up: bfloat16 [1536, 24576], P('dp', 'head'), may hold values from -0.15625 to 0.15625
- kv_up: bfloat16 [512, 32768], P('dp', 'head'), may hold values from -0.25 to 0.25
- out_grad: bfloat16 [4096, 16384], P('dp', 'head'), may hold values from -6 to 6
Outputs:
- d_q_latent: bfloat16 [4096, 1536], P('dp', 'head')
- d_kv_latent: bfloat16 [4096, 576], P('dp', 'head')
- grad_blocks: float32 [256, 512, 512], P(('head', 'dp'))
- left_gram: float32 [256, 512, 512], P(('head', 'dp'))
- right_gram: float32 [256, 512, 512], P(('head', 'dp'))
All inputs are finite; a program needn't handle non-finite values.
Results may differ from a plain program's by a relative error of at most 0.024.
Values may be sent and summed in bfloat16 or wider, within the bound.
No kernel may reach another device: no remote copies, remote signals or barrier semaphores. Data moves between devices by JAX's collectives and lax.ppermute only.
A program may use at most 128 MiB of HBM per device.

v0:
```python
import math

import jax
import jax.numpy as jnp
from jax import lax
from jax.sharding import PartitionSpec as P

KVL = 512
NOPE = 128
ROPE = 64
VD = 128
BLK = 512


def square_blocks(matrix):
    rows, cols = matrix.shape
    pieces = matrix.reshape(rows // BLK, BLK, cols // BLK, BLK)
    return jnp.transpose(pieces, (0, 2, 1, 3)).reshape(rows // BLK * (cols // BLK), BLK, BLK)


def per_device(q_latent, kv_latent, q_up, kv_up, out_grad):
    qk_size = NOPE + ROPE
    kv_size = NOPE + VD
    scale = 1.0 / math.sqrt(qk_size)
    w_query, w_keyval = (
        lax.all_gather(q_up, "dp", axis=0, tiled=True),
        lax.all_gather(kv_up, "dp", axis=0, tiled=True),
    )
    length = q_latent.shape[0]
    heads = w_query.shape[1] // qk_size
    kv_lat = kv_latent[:, :KVL]
    rope_key = kv_latent[:, KVL:]
    query = jnp.dot(q_latent, w_query, preferred_element_type=jnp.float32).astype(jnp.bfloat16)
    query = query.reshape(length, heads, qk_size)
    keyval = jnp.dot(kv_lat, w_keyval, preferred_element_type=jnp.float32).astype(jnp.bfloat16)
    keyval = keyval.reshape(length, heads, kv_size)
    shared = jnp.broadcast_to(rope_key[:, None, :], (length, heads, ROPE))
    key = jnp.concatenate([keyval[:, :, :NOPE], shared], axis=2)
    value = keyval[:, :, NOPE:]
    grad = out_grad.reshape(length, heads, VD)
    positions = jnp.arange(length)
    causal = positions[:, None] >= positions[None, :]
    scores = jnp.einsum("qhd,khd->hqk", query, key, preferred_element_type=jnp.float32) * scale
    scores = jnp.where(causal[None], scores, -jnp.inf)
    weights = jnp.exp(scores)
    weights = weights / jnp.sum(weights, axis=-1, keepdims=True)
    probs = weights.astype(jnp.bfloat16)
    attn_out = jnp.einsum("hqk,khd->qhd", probs, value, preferred_element_type=jnp.float32)
    delta = jnp.sum(grad.astype(jnp.float32) * attn_out, axis=-1)
    delta = jnp.transpose(delta)[:, :, None]
    dvalue = jnp.einsum("hqk,qhd->khd", probs, grad, preferred_element_type=jnp.float32).astype(
        jnp.bfloat16
    )
    dprob = jnp.einsum("qhd,khd->hqk", grad, value, preferred_element_type=jnp.float32)
    dscore = (weights * (dprob - delta) * scale).astype(jnp.bfloat16)
    dquery = jnp.einsum("hqk,khd->qhd", dscore, key, preferred_element_type=jnp.float32).astype(
        jnp.bfloat16
    )
    dkey = jnp.einsum("hqk,qhd->khd", dscore, query, preferred_element_type=jnp.float32).astype(
        jnp.bfloat16
    )
    dq_flat = dquery.reshape(length, heads * qk_size)
    dkv_flat = jnp.concatenate([dkey[:, :, :NOPE], dvalue], axis=2).reshape(length, heads * kv_size)
    q_term = jnp.dot(dq_flat, w_query.T, preferred_element_type=jnp.float32)
    rope_term = jnp.sum(dkey[:, :, NOPE:].astype(jnp.float32), axis=1)
    kv_term = jnp.concatenate(
        [jnp.dot(dkv_flat, w_keyval.T, preferred_element_type=jnp.float32), rope_term], axis=1
    )
    d_query_lat, d_keyval_lat = (
        lax.psum_scatter(
            q_term.astype(jnp.bfloat16), "head", scatter_dimension=1, tiled=True
        ).astype(jnp.float32),
        lax.psum_scatter(
            kv_term.astype(jnp.bfloat16), "head", scatter_dimension=1, tiled=True
        ).astype(jnp.float32),
    )
    wq_grad = jnp.dot(q_latent.T, dq_flat, preferred_element_type=jnp.float32)
    wkv_grad = jnp.dot(kv_lat.T, dkv_flat, preferred_element_type=jnp.float32)
    local_blocks = jnp.concatenate([square_blocks(wq_grad), square_blocks(wkv_grad)], axis=0)
    block_count = local_blocks.shape[0]
    owners = lax.axis_size("dp")
    slots = (block_count + owners - 1) // owners
    spare = owners * slots - block_count
    filler = jnp.zeros((spare, BLK, BLK), jnp.float32)
    owned = lax.psum_scatter(
        jnp.concatenate([local_blocks, filler], axis=0).astype(jnp.bfloat16),
        "dp",
        scatter_dimension=0,
        tiled=True,
    ).astype(jnp.float32)
    left_gram = jnp.einsum("sic,sjc->sij", owned, owned, precision=lax.Precision.HIGHEST)
    right_gram = jnp.einsum("sci,scj->sij", owned, owned, precision=lax.Precision.HIGHEST)
    return (
        d_query_lat.astype(jnp.bfloat16),
        d_keyval_lat.astype(jnp.bfloat16),
        owned,
        left_gram,
        right_gram,
    )


def solution(mesh):
    return jax.shard_map(
        per_device,
        mesh=mesh,
        in_specs=(P("dp", None), P("dp", None), P("dp", "head"), P("dp", "head"), P("dp", "head")),
        out_specs=(
            P("dp", "head"),
            P("dp", "head"),
            P(("head", "dp"), None, None),
            P(("head", "dp"), None, None),
            P(("head", "dp"), None, None),
        ),
        check_vma=False,
    )
```

profile of v0, /device:TPU:6, one launch (start us, length us, event | category | flops | bytes accessed | tf_op | source)
XLA Modules:
  0.0 622.6 jit_solution(10591723139238853662)
XLA Ops:
  7.2 0.0 copy-start
  7.2 0.0 all-gather.3.cloned.1.call-start
  7.2 0.7 all-gather.3.cloned.1.call-update
  7.9 0.0 all-gather.5.cloned.1.call-start
  8.0 0.7 all-gather.5.cloned.1.call-update
  8.7 0.0 all-reduce.3.cloned.1.call-start
  8.7 1.2 copy.54
  10.0 0.1 pad.2.clone
  10.1 89.0 %all-gather.3.cloned.1.call-done = bf16[512,2048]{1,0:T(8,128)(2,1)} async-done(((bf16[32,2048]{1,0:T(8,128)(2,1)}), bf16[512,2048]{1,0:T(8,128)(2,1)}) %all-gather.3.cloned.1.call-update) | async-done | bytes 2097168 | tf_op jit(solution)/shard_map/all_gather | solution.py:27
  99.1 2.4 convolution_convert_fusion.2
  101.5 0.3 copy.76
  101.8 0.9 fusion.22
  102.7 0.3 copy.74
  103.0 0.0 slice-start
  103.0 99.4 %all-gather.5.cloned.1.call-done = bf16[1536,1536]{1,0:T(8,128)(2,1)} async-done(((bf16[96,1536]{1,0:T(8,128)(2,1)}), bf16[1536,1536]{1,0:T(8,128)(2,1)}) %all-gather.5.cloned.1.call-update) | async-done | bytes 4718608 | tf_op jit(solution)/shard_map/all_gather | solution.py:26
  202.4 0.0 copy-done
  202.4 3.7 convolution_convert_fusion.4
  206.1 0.3 copy.52
  206.4 0.0 slice-done
  206.4 0.7 fusion.4
  207.1 0.0 copy-start.6
  207.1 1.5 fusion.8
  208.6 0.0 copy-done.6
  208.6 0.7 fusion.7
  209.3 0.8 fusion.2
  210.1 0.5 fusion.6
  210.6 0.0 copy-start.7
  210.6 1.3 convolution_convert_fusion.6
  211.9 0.0 copy-start.5
  212.0 0.1 copy.61
  212.1 0.0 copy-done.7
  212.1 0.1 pad_maximum_fusion
  212.2 0.0 copy-start.3
  212.2 0.7 copy-done.5
  212.8 0.7 convolution_convert_fusion.1
  213.6 0.2 copy-done.3
  213.8 0.8 convolution_convert_fusion.8
  214.5 0.8 pad_maximum_fusion.4
  215.3 0.0 all-reduce.3.cloned.1.call-update
  215.3 0.0 reduce-scatter.6.cloned.1.call-start
  215.4 2.4 copy.64
  217.8 4.7 fusion
  222.5 6.6 %copy.62 = bf16[1536,1536]{1,0:T(8,128)(2,1)} copy(bf16[1536,1536]{0,1:T(8,128)(2,1)} %fusion) | data formatting | bytes 9437184 | tf_op jit(solution)/shard_map/dot_general | solution.py:77
  229.1 11.9 %reshape.69 = bf16[3,512,3,512]{3,2,1,0:T(4,128)(2,1)} reshape(bf16[1536,1536]{1,0:T(8,128)(2,1)} %copy.62) | data formatting | bytes 9437184 | tf_op jit(solution)/shard_map/reshape | solution.py:17
  241.0 4.1 copy.63
  245.1 0.0 copy-done.1
  245.1 3.8 maximum_maximum_fusion
  249.0 0.0 reduce-scatter.6.cloned.1.call-update
  249.0 0.0 copy-start.8
  249.0 0.0 reduce-scatter.4.cloned.1.call-start
  249.1 1.0 copy-done.4
  250.1 4.6 convolution_convert_fusion.3
  254.8 0.0 reduce-scatter.4.cloned.1.call-update
  254.8 0.0 copy-done.8
  254.8 0.6 dynamic-slice
  256.0 70.5 %all-reduce.3.cloned.1.call-done = bf16[256,576]{1,0:T(8,128)(2,1)} async-done(((bf16[256,576]{1,0:T(8,128)(2,1)}), bf16[256,576]{1,0:T(8,128)(2,1)}) %all-reduce.3.cloned.1.call-update) | async-done | bytes 294928
  326.6 1.0 constant_dynamic-slice_fusion
  327.6 0.7 copy.65
  328.3 229.2 %reduce-scatter.6.cloned.1.call-done = bf16[1,512,512]{2,1,0:T(8,128)(2,1)} async-done(((bf16[16,512,512]{2,1,0:T(8,128)(2,1)}), bf16[1,512,512]{2,1,0:T(8,128)(2,1)}) %reduce-scatter.6.cloned.1.call-update) | async-done | bytes 524304 | tf_op jit(solution)/shard_map/reduce_scatter | solution.py:85
  557.5 2.2 convert_element_type.61
  559.7 2.6 convolution_bitcast_fusion
  562.4 0.0 copy-done.2
  562.4 1.4 convolution_bitcast_fusion.1
  563.8 52.3 %reduce-scatter.4.cloned.1.call-done = bf16[256,96]{0,1:T(8,128)(2,1)} async-done(((bf16[256,1536]{0,1:T(8,128)(2,1)}), bf16[256,96]{0,1:T(8,128)(2,1)}) %reduce-scatter.4.cloned.1.call-update) | async-done | bytes 49168 | tf_op jit(solution)/shard_map/reduce_scatter | solution.py:70
  (8 shorter events, 0.1 us)
Async XLA Ops:
  7.2 195.2 %copy-start = (bf16[256,1536]{1,0:T(8,128)(2,1)S(1)}, bf16[256,1536]{1,0:T(8,128)(2,1)}, u32[]{:S(2)}) copy-start(bf16[256,1536]{1,0:T(8,128)(2,1)} %param.5) | copy-start | bytes 2359300
  7.2 91.9 %all-gather.3.cloned.1.call-start = ((), (), s32[]{:S(2)}) async-start(), calls=%async_computation.2 | async-start | bytes 2228224 | tf_op jit(solution)/shard_map/all_gather | solution.py:27
  7.9 194.4 %all-gather.5.cloned.1.call-start = ((), (), s32[]{:S(2)}) async-start(), calls=%async_computation.3 | async-start | bytes 5013504 | tf_op jit(solution)/shard_map/all_gather | solution.py:26
  8.7 317.9 %all-reduce.3.cloned.1.call-start = ((), (), s32[]{:S(2)}) async-start(), calls=%async_computation.6 | async-start | bytes 655360
  103.0 103.4 %slice-start = ((bf16[256,576]{0,1:T(8,128)(2,1)}), bf16[256,64]{0,1:T(8,128)(2,1)S(1)}, s32[]{:S(2)}) async-start(bf16[256,576]{0,1:T(8,128)(2,1)} %param.6), calls=%async_computation.7 | async-start | bytes 65536 | tf_op jit(solution)/shard_map/slice | solution.py:32
  207.1 1.5 copy-start.6
  210.6 1.5 copy-start.7
  211.9 1.0 copy-start.5
  212.2 1.6 copy-start.3
  215.3 342.2 %reduce-scatter.6.cloned.1.call-start = ((), (), s32[]{:S(2)}) async-start(), calls=%async_computation.5 | async-start | bytes 8912896 | tf_op jit(solution)/shard_map/reduce_scatter | solution.py:85
  241.0 4.1 copy-start.1
  249.0 1.1 copy-start.4
  249.0 5.8 copy-start.8
  249.0 367.1 %reduce-scatter.4.cloned.1.call-start = ((), (), s32[]{:S(2)}) async-start(), calls=%async_computation.4 | async-start | bytes 835584 | tf_op jit(solution)/shard_map/reduce_scatter | solution.py:70
  557.5 4.9 copy-start.2
Sparse Core Ops, SparseCore 0:
  10.6 88.4 all-gather.2
  101.6 100.6 all-gather.4
  215.4 111.0 all-reduce.2
  331.1 226.3 reduce-scatter.5
  560.6 55.4 reduce-scatter.3
where the time goes:
time: 630 us; the launch traced here: 623 us
  waiting for transfers between devices  542 us (86%)
  local copies, waits for them, and re-layouts  32.6 us (5%)
  matrix products  26.4 us (4%)
  between operations  14.7 us (2%)
  other arithmetic  6.93 us (1%)
    reduce_scatter x1, waiting for transfers between devices, per_device(): lax.psum_scatter(jnp.concatenate([local_blocks, filler], axis=0).astype(j...  229 us
    all_gather x1, waiting for transfers between devices, per_device(): lax.all_gather(q_up, 'dp', axis=0, tiled=True)  99.4 us
    all_gather x1, waiting for transfers between devices, per_device(): lax.all_gather(kv_up, 'dp', axis=0, tiled=True)  89 us
    unnamed x6, waiting for transfers between devices  72 us
    reduce_scatter x1, waiting for transfers between devices, per_device(): lax.psum_scatter(q_term.astype(jnp.bfloat16), 'head', scatter_dimension=1...  52.3 us
    reshape x2, local copies, waits for them, and re-layouts, square_blocks(): pieces = matrix.reshape(rows // BLK, BLK, cols // BLK, BLK)  14.3 us
  transfers between devices with their start and end apart: 5, of which 5 were waited for; matrix products, arithmetic and copies ran while one was open for 8% of the time, Pallas kernels for 0%

commit v1 on v0

v1 whole, which is shorter than its diff:
```python
import math

import jax
import jax.numpy as jnp
from jax import lax
from jax.experimental import pallas as pl
from jax.experimental.pallas import tpu as pltpu
from jax.sharding import PartitionSpec as P

KVL = 512
NOPE = 128
ROPE = 64
VD = 128
BLK = 512
QK = NOPE + ROPE
SCALE = 1.0 / math.sqrt(QK)
LOG2E = math.log2(math.e)

F32 = jnp.float32
BF16 = jnp.bfloat16


def dot(a, b, ca, cb):
    return lax.dot_general(a, b, (((ca,), (cb,)), ((), ())), preferred_element_type=F32)


def main_kernel(pos, ql, kl, lat0, lat1, og, w, dl, out_a, out_b, out_c, wq, wkv, lq, lk, rope, dq, dkv, kvt):
    member, group, core = pos[0], pos[1], pos[2]
    for d in range(16):
        for t in range(3):
            wq[96 * d : 96 * d + 96, 128 * t : 128 * t + 128] = w[d, 96 * t : 96 * t + 96, :]
        for t in range(4):
            wkv[32 * d : 32 * d + 32, 128 * t : 128 * t + 128] = w[d, 288 + 32 * t : 320 + 32 * t, :]
    lq[0:256, :] = ql[...]
    lk[0:256, :] = kl[:, :KVL]
    rope[0:256, :] = kl[:, KVL:]
    for i, lat in enumerate((lat0, lat1)):
        base = 128 * (core ^ i)
        for chip in range(8):
            for s in range(3):
                rows = pl.ds(pl.multiple_of(256 * (s + 1) + base + 16 * chip, 16), 16)
                at = 272 * s
                for t in range(12):
                    lq[rows, 128 * t : 128 * t + 128] = lat[chip, at + 16 * t : at + 16 * t + 16, :]
                for t in range(4):
                    lk[rows, 128 * t : 128 * t + 128] = lat[chip, at + 192 + 16 * t : at + 208 + 16 * t, :]
                rope[rows, :] = lat[chip, at + 256 : at + 272, :ROPE]

    causal = lax.broadcasted_iota(jnp.int32, (256, 256), 0) >= lax.broadcasted_iota(jnp.int32, (256, 256), 1)

    def sequence(s, carry):
        rows = pl.ds(pl.multiple_of(256 * s, 256), 256)
        who = member ^ s
        query = dot(lq[rows, :], wq[...], 1, 0)
        keyval = dot(lk[rows, :], wkv[...], 1, 0).astype(BF16)
        rope_key = rope[rows, :]
        rope_sum = jnp.zeros((256, ROPE), F32)
        dq_parts = []
        for h in range(2):
            q_h = query[:, QK * h : QK * h + QK].astype(BF16)
            key = jnp.concatenate([keyval[:, 256 * h : 256 * h + 128], rope_key], axis=1)
            value = keyval[:, 256 * h + 128 : 256 * h + 256]
            grad = og[who, :, 128 * h : 128 * h + 128]
            weights = jnp.where(causal, jnp.exp2(dot(q_h, key, 1, 1) * (SCALE * LOG2E)), 0.0)
            weights = weights / jnp.sum(weights, axis=1, keepdims=True)
            probs = weights.astype(BF16)
            dprob = dot(grad, value, 1, 1)
            delta = jnp.sum(probs.astype(F32) * dprob, axis=1, keepdims=True)
            dscore = (weights * (dprob - delta) * SCALE).astype(BF16)
            dvalue = dot(probs, grad, 0, 0).astype(BF16)
            dq_parts.append(dot(dscore, key, 1, 0))
            dkey = dot(dscore, q_h, 0, 0)
            dkv[rows, 256 * h : 256 * h + 128] = dkey[:, :NOPE].astype(BF16)
            dkv[rows, 256 * h + 128 : 256 * h + 256] = dvalue
            rope_sum = rope_sum + dkey[:, NOPE:].astype(BF16).astype(F32)
        dq[rows, :] = jnp.concatenate(dq_parts, axis=1).astype(BF16)
        q_term = dot(wq[...], dq[rows, :], 1, 1).astype(BF16)
        kvt[0:KVL, :] = dot(wkv[...], dkv[rows, :], 1, 1)
        kvt[KVL:, :] = rope_sum.T
        for h in range(16):
            side = (h % 2) ^ core
            dl[side, h // 2, who, 0:96, :] = q_term[96 * h : 96 * h + 96, :]
            piece = jnp.concatenate([kvt[36 * h : 36 * h + 36, :], jnp.zeros((12, 256), F32)], axis=0)
            dl[side, h // 2, who, 96:144, :] = piece.astype(BF16)
        return carry

    lax.fori_loop(0, 4, sequence, 0)

    for block in range(4):
        turn = (block - group + 4) % 4
        if block == 3:
            term = dot(lk[...], dkv[...], 0, 0).astype(BF16)
            out_a[turn] = term[:, :384]
            out_c[turn] = term[:, 384:]
            continue
        term = dot(lq[:, 512 * block : 512 * block + 512], dq[...], 0, 0).astype(BF16)

        @pl.when((member == 0) | (member == 3))
        def _():
            out_a[turn] = term

        @pl.when(member == 1)
        def _():
            out_a[turn, :, 0:256] = term[:, 128:]
            out_c[turn] = term[:, :128]

        @pl.when(member == 2)
        def _():
            out_b[turn] = term[:, :256]
            out_c[turn] = term[:, 256:]


def main_call(pos, ql, kl, lat0, lat1, og, w):
    vmem = pl.BlockSpec(memory_space=pltpu.VMEM)
    return pl.pallas_call(
        main_kernel,
        out_shape=(
            jax.ShapeDtypeStruct((2, 8, 4, 144, 256), BF16),
            jax.ShapeDtypeStruct((4, 512, 384), BF16),
            jax.ShapeDtypeStruct((4, 512, 256), BF16),
            jax.ShapeDtypeStruct((4, 512, 128), BF16),
        ),
        in_specs=[pl.BlockSpec(memory_space=pltpu.SMEM)] + [vmem] * 6,
        out_specs=(vmem,) * 4,
        scratch_shapes=[
            pltpu.VMEM((1536, 384), BF16),
            pltpu.VMEM((512, 512), BF16),
            pltpu.VMEM((1024, 1536), BF16),
            pltpu.VMEM((1024, 512), BF16),
            pltpu.VMEM((1024, ROPE), BF16),
            pltpu.VMEM((1024, 384), BF16),
            pltpu.VMEM((1024, 512), BF16),
            pltpu.VMEM((576, 256), F32),
        ],
        compiler_params=pltpu.CompilerParams(vmem_limit_bytes=48 * 1024 * 1024),
        cost_estimate=pl.CostEstimate(flops=6_300_000_000, bytes_accessed=16_000_000, transcendentals=524288),
        name="mla_backward",
    )(pos, ql, kl, lat0, lat1, og, w)


def gram_kernel(pos, *refs):
    terms, (grad, left, right) = refs[:12], refs[12:]
    owner = pos[0]
    is_q = owner < 9
    column = owner % 3

    def total(k):
        return sum(terms[3 * turn + k][...].astype(F32) for turn in range(4))

    @pl.when((is_q & (column == 0)) | ((owner >= 9) & (owner < 13)))
    def _():
        grad[:, 0:384] = total(0)
        grad[:, 384:512] = total(2)

    @pl.when(is_q & (column == 1))
    def _():
        grad[:, 0:256] = sum(terms[3 * turn][:, 0:256].astype(F32) for turn in range(4))
        grad[:, 256:512] = total(1)

    @pl.when(is_q & (column == 2))
    def _():
        grad[:, 0:128] = total(2)
        grad[:, 128:512] = total(0)

    @pl.when(owner >= 13)
    def _():
        grad[...] = jnp.zeros_like(grad)

    g = grad[...]
    highest = lax.Precision.HIGHEST
    left[...] = lax.dot_general(g, g, (((1,), (1,)), ((), ())), precision=highest, preferred_element_type=F32)
    right[...] = lax.dot_general(g, g, (((0,), (0,)), ((), ())), precision=highest, preferred_element_type=F32)


def gram_call(pos, terms):
    vmem = pl.BlockSpec(memory_space=pltpu.VMEM)
    block = jax.ShapeDtypeStruct((BLK, BLK), F32)
    return pl.pallas_call(
        gram_kernel,
        out_shape=(block, block, block),
        in_specs=[pl.BlockSpec(memory_space=pltpu.SMEM)] + [vmem] * 12,
        out_specs=(vmem,) * 3,
        compiler_params=pltpu.CompilerParams(vmem_limit_bytes=32 * 1024 * 1024),
        cost_estimate=pl.CostEstimate(flops=3_200_000_000, bytes_accessed=8_000_000, transcendentals=0),
        name="owner_grams",
    )(pos, *terms)


GROUPS = [[4 * a + m for m in range(4)] for a in range(4)]
SAME_CORE = [[2 * i + c for i in range(8)] for c in range(2)]


def term_routes(turn):
    route_a, route_b, route_c = [], [], []
    for a in range(4):
        block = (a + turn) % 4
        for m in range(4):
            here = 4 * a + m
            if block == 3:
                route_a.append((here, 9 + m))
                route_c.append((here, 9 + m))
                continue
            first = 3 * block
            if m == 0:
                route_a.append((here, first))
            elif m == 1:
                route_a.append((here, first + 1))
                route_c.append((here, first))
            elif m == 2:
                route_b.append((here, first + 1))
                route_c.append((here, first + 2))
            else:
                route_a.append((here, first + 2))
    return route_a, route_b, route_c


def per_device(q_latent, kv_latent, q_up, kv_up, out_grad):
    dp, head = lax.axis_index("dp"), lax.axis_index("head")
    member, group = dp % 4, dp // 4
    core, chip = head % 2, head // 2
    pos = jnp.stack([member, group, core, dp]).astype(jnp.int32)

    wq = q_up.reshape(96, 12, 128).transpose(1, 0, 2).reshape(4, 288, 128)
    wk = kv_up.reshape(32, 16, 128).transpose(1, 0, 2).reshape(4, 128, 128)
    w = jnp.concatenate([wq, wk], axis=1)
    w = jnp.broadcast_to(w[None], (4, 4, 416, 128)).reshape(16, 416, 128)

    row = 16 * (8 * core + chip)
    q_rows = lax.dynamic_slice_in_dim(q_latent, row, 16, 0)
    kv_rows = jnp.pad(lax.dynamic_slice_in_dim(kv_latent, row, 16, 0), ((0, 0), (0, 64)))
    piece = jnp.concatenate([q_rows, kv_rows], axis=1).reshape(16, 17, 128).transpose(1, 0, 2).reshape(272, 128)
    others = [lax.ppermute(piece, "dp", [(i, i ^ s) for i in range(16)]) for s in (1, 2, 3)]
    others = jnp.broadcast_to(jnp.concatenate(others, axis=0)[None], (8, 816, 128))
    lat0 = lax.all_to_all(others, "head", 0, 0, tiled=True, axis_index_groups=SAME_CORE)
    lat1 = lax.ppermute(lat0, "head", [(i, i ^ 1) for i in range(16)])

    og = out_grad.reshape(256, 4, 256).transpose(1, 0, 2)
    og = lax.all_to_all(og, "dp", 0, 0, tiled=True, axis_index_groups=GROUPS)

    w = lax.all_to_all(w, "dp", 0, 0, tiled=True)

    dl, out_a, out_b, out_c = main_call(pos, q_latent, kv_latent, lat0, lat1, og, w)

    terms = []
    for turn in range(4):
        for out, route in zip((out_a, out_b, out_c), term_routes(turn)):
            terms.append(lax.ppermute(out[turn], "dp", route))

    given = lax.ppermute(dl[1], "head", [(i, i ^ 1) for i in range(16)])
    dl = (dl[0].astype(F32) + given.astype(F32)).astype(BF16)
    dl = lax.all_to_all(dl, "head", 0, 0, tiled=True, axis_index_groups=SAME_CORE)
    dl = jnp.sum(dl.astype(F32), axis=0).astype(BF16)
    dl = lax.all_to_all(dl, "dp", 0, 0, tiled=True, axis_index_groups=GROUPS)
    dl = jnp.sum(dl.astype(F32), axis=0)
    d_q = dl[:96].T.astype(BF16)
    d_kv = dl[96:132].T.astype(BF16)

    owned, left, right = gram_call(pos[3:], terms)
    return d_q, d_kv, owned[None], left[None], right[None]


def solution(mesh):
    return jax.shard_map(
        per_device,
        mesh=mesh,
        in_specs=(P("dp", None), P("dp", None), P("dp", "head"), P("dp", "head"), P("dp", "head")),
        out_specs=(
            P("dp", "head"),
            P("dp", "head"),
            P(("head", "dp"), None, None),
            P(("head", "dp"), None, None),
            P(("head", "dp"), None, None),
        ),
        check_vma=False,
    )
```

time: 630 us -> 235 us (0.37)
  the two profiles are of different devices: /device:TPU:6 before, /device:TPU:89 now
where the time goes in v1:
time: 235 us; the launch traced here: 234 us
  waiting for transfers between devices  106 us (45%)
  starting transfers between devices  84.8 us (36%)
  Pallas kernels  22.7 us (10%)
  local copies, waits for them, and re-layouts  14.9 us (6%)
  other arithmetic  5.11 us (2%)
    ppermute x12, waiting for transfers between devices, per_device(): terms.append(lax.ppermute(out[turn], 'dp', route))  45.3 us
    ppermute x12, starting transfers between devices, per_device(): terms.append(lax.ppermute(out[turn], 'dp', route))  35.5 us
    all_to_all x1, waiting for transfers between devices, per_device(): w = lax.all_to_all(w, 'dp', 0, 0, tiled=True)  32.9 us
    all_to_all x1, waiting for transfers between devices, per_device(): lax.all_to_all(others, 'head', 0, 0, tiled=True, axis_index_groups=SAME_C...  19.1 us
    pallas_call x1, Pallas kernels, main_call(): pl.pallas_call(main_kernel, out_shape=(jax.ShapeDtypeStruct((2, 8, 4, 144...  18 us
    all_to_all x1, starting transfers between devices, per_device(): dl = lax.all_to_all(dl, 'dp', 0, 0, tiled=True, axis_index_groups=GROUPS)  9.58 us
    all_to_all x1, starting transfers between devices, per_device(): w = lax.all_to_all(w, 'dp', 0, 0, tiled=True)  9.08 us
    all_to_all x1, starting transfers between devices, per_device(): lax.all_to_all(dl, 'head', 0, 0, tiled=True, axis_index_groups=SAME_CORE)  7.8 us
  transfers between devices with their start and end apart: 22, of which 9 were waited for; matrix products, arithmetic and copies ran while one was open for 3% of the time, Pallas kernels for 2%

profile of v1, /device:TPU:89, one launch (start us, length us, event | category | flops | bytes accessed | tf_op | source)
XLA Modules:
  0.0 234.4 jit_solution(16427580830198738956)
XLA Ops:
  0.6 0.0 copy-start.6
  0.6 1.3 copy.27
  1.9 1.0 copy.28
  2.9 5.6 %all-to-all-start.1 = ((bf16[4,256,256]{2,1,0:T(8,128)(2,1)}), bf16[4,256,256]{2,1,0:T(8,128)(2,1)S(1)}, u32[]{:S(2)}, u32[]{:S(2)}) async-start(bf16[4,256,256]{2,1,0:T(8,128)(2,1)} %bitcast.7), calls=%async_computation.1 | async-start | bytes 1048576 | tf_op jit(solution)/shard_map/all_to_all | solution.py:238
  8.5 0.1 constant_dynamic-slice_fusion
  8.6 0.1 copy.32
  8.8 0.8 constant_dynamic-slice_fusion.1
  9.7 1.3 collective-permute-start.2
  10.9 0.1 collective-permute-start.1
  11.0 2.9 %collective-permute-start = (bf16[272,128]{1,0:T(8,128)(2,1)S(1)}, bf16[272,128]{1,0:T(8,128)(2,1)S(1)}, u32[]{:S(2)}, u32[]{:S(2)}) collective-permute-start(bf16[272,128]{1,0:T(8,128)(2,1)S(1)} %bitcast.61), channel_id=1, source_target_pairs={{0,16},{16,0},{32,48},{48,32},{64,80},{80,64},{96,112},{112,96},{1... | collective-permute-start | bytes 208904 | tf_op jit(solution)/shard_map/ppermute | solution.py:232
  13.9 2.7 %collective-permute-done.2 = bf16[272,128]{1,0:T(8,128)(2,1)S(1)} collective-permute-done((bf16[272,128]{1,0:T(8,128)(2,1)S(1)}, bf16[272,128]{1,0:T(8,128)(2,1)S(1)}, u32[]{:S(2)}, u32[]{:S(2)}) %collective-permute-start.2) | collective-permute-done | bytes 69664 | tf_op jit(solution)/shard_map/ppermute | solution.py:232
  16.6 1.8 collective-permute-done.1
  18.4 0.0 collective-permute-done
  18.4 0.0 copy-start.9
  18.4 0.0 all-to-all-done.1.og
  18.4 1.4 broadcast_in_dim.10
  19.8 5.3 %all-to-all-start = ((bf16[8,816,128]{2,1,0:T(8,128)(2,1)}), bf16[8,816,128]{2,1,0:T(8,128)(2,1)S(1)}, u32[]{:S(2)}, u32[]{:S(2)}) async-start(bf16[8,816,128]{2,1,0:T(8,128)(2,1)} %broadcast_in_dim.10), calls=%async_computation | async-start | bytes 3342336 | tf_op jit(solution)/shard_map/all_to_all | solution.py:234
  25.3 0.2 reshape.41
  25.5 0.1 copy.29
  25.6 0.0 copy-start.7
  25.6 19.1 %all-to-all-done.lat0 = bf16[8,816,128]{2,1,0:T(8,128)(2,1)S(1)} async-done(((bf16[8,816,128]{2,1,0:T(8,128)(2,1)}), bf16[8,816,128]{2,1,0:T(8,128)(2,1)S(1)}, u32[]{:S(2)}, u32[]{:S(2)}) %all-to-all-start) | async-done | bytes 1671200 | tf_op jit(solution)/shard_map/all_to_all | solution.py:234
  44.7 1.6 broadcast_in_dim.22
  46.3 0.2 copy-done.5
  46.5 9.1 %all-to-all-start.2 = ((bf16[16,416,128]{2,1,0:T(8,128)(2,1)}), bf16[16,416,128]{2,1,0:T(8,128)(2,1)S(1)}, u32[]{:S(2)}, u32[]{:S(2)}) async-start(bf16[16,416,128]{2,1,0:T(8,128)(2,1)} %bitcast.12), calls=%async_computation.2 | async-start | bytes 3407872 | tf_op jit(solution)/shard_map/all_to_all | solution.py:240
  55.5 3.5 %collective-permute-start.3 = (bf16[8,816,128]{2,1,0:T(8,128)(2,1)}, bf16[8,816,128]{2,1,0:T(8,128)(2,1)}, u32[]{:S(2)}, u32[]{:S(2)}) collective-permute-start(bf16[8,816,128]{2,1,0:T(8,128)(2,1)} %copy-done.5), channel_id=1, source_target_pairs={{0,1},{1,0},{2,3},{3,2},{4,5},{5,4},{6,7},{7,6},{8,9},{9,8},{10,11... | collective-permute-start | bytes 5013512 | tf_op jit(solution)/shard_map/ppermute | solution.py:235
  59.1 0.2 copy.31.kl
  59.3 0.1 pad_add_fusion.pos
  59.4 32.9 %all-to-all-done.2.w = bf16[16,416,128]{2,1,0:T(8,128)(2,1)S(1)} async-done(((bf16[16,416,128]{2,1,0:T(8,128)(2,1)}), bf16[16,416,128]{2,1,0:T(8,128)(2,1)S(1)}, u32[]{:S(2)}, u32[]{:S(2)}) %all-to-all-start.2) | async-done | bytes 1703968 | tf_op jit(solution)/shard_map/all_to_all | solution.py:240
  92.3 1.2 copy-done.4
  93.6 1.1 copy-done.2
  94.7 18.0 %mla_backward.1 = (bf16[2,8,4,144,256]{4,3,2,1,0:T(8,128)(2,1)}, bf16[4,512,384]{2,1,0:T(8,128)(2,1)S(1)}, bf16[4,512,256]{2,1,0:T(8,128)(2,1)S(1)}, bf16[4,512,128]{2,1,0:T(8,128)(2,1)S(1)}) custom-call(s32[4]{0:T(128)S(1)} %pad_add_fusion.pos, bf16[256,1536]{1,0:T(8,128)(2,1)S(1)} %copy-done.2, bf16[256,576]{1,0:T(8,128)(2,1)S(1)} %copy.31.kl, ...), custom_call_target="tpu_custom_call" | custom-call | flops 6300000256 | bytes 16000000 | tf_op jit(solution)/shard_map/mla_backward/pallas_call | solution.py:115
  112.7 2.1 slice_bitcast_fusion
  114.8 4.1 %collective-permute-start.4 = (bf16[8,4,144,256]{3,2,1,0:T(8,128)(2,1)S(1)}, bf16[8,4,144,256]{3,2,1,0:T(8,128)(2,1)S(1)}, u32[]{:S(2)}, u32[]{:S(2)}) collective-permute-start(bf16[8,4,144,256]{3,2,1,0:T(8,128)(2,1)S(1)} %slice_bitcast_fusion), channel_id=1, source_target_pairs={{0,1},{1,0},{2,3},{3,2},{4,5},{5,4},{6,7},{7,6},{8,9},{9,8},{10,11... | collective-permute-start | bytes 7077896 | tf_op jit(solution)/shard_map/ppermute | solution.py:249
  118.9 4.2 %collective-permute-done.4 = bf16[8,4,144,256]{3,2,1,0:T(8,128)(2,1)S(1)} collective-permute-done((bf16[8,4,144,256]{3,2,1,0:T(8,128)(2,1)S(1)}, bf16[8,4,144,256]{3,2,1,0:T(8,128)(2,1)S(1)}, u32[]{:S(2)}, u32[]{:S(2)}) %collective-permute-start.4) | collective-permute-done | bytes 2359328 | tf_op jit(solution)/shard_map/ppermute | solution.py:249
  123.1 2.1 fusion
  125.2 7.8 %all-to-all-start.3 = ((bf16[8,4,144,256]{3,2,1,0:T(8,128)(2,1)}), bf16[8,4,144,256]{3,2,1,0:T(8,128)(2,1)}, u32[]{:S(2)}, u32[]{:S(2)}) async-start(bf16[8,4,144,256]{3,2,1,0:T(8,128)(2,1)} %fusion), calls=%async_computation.3 | async-start | bytes 4718592 | tf_op jit(solution)/shard_map/all_to_all | solution.py:251
  133.1 5.6 %collective-permute-start.16 = (bf16[512,128]{1,0:T(8,128)(2,1)S(1)}, bf16[512,128]{1,0:T(8,128)(2,1)S(1)}, u32[]{:S(2)}, u32[]{:S(2)}) collective-permute-start(bf16[512,128]{1,0:T(8,128)(2,1)S(1)} %get-tuple-element.27), channel_id=1, source_target_pairs={{0,144},{16,160},{32,176},{48,192},{80,0},{96,32},{144,48},{160,80... | collective-permute-start | bytes 393224 | tf_op jit(solution)/shard_map/ppermute | solution.py:247
  138.7 5.1 %collective-permute-start.13 = (bf16[512,128]{1,0:T(8,128)(2,1)S(1)}, bf16[512,128]{1,0:T(8,128)(2,1)S(1)}, u32[]{:S(2)}, u32[]{:S(2)}) collective-permute-start(bf16[512,128]{1,0:T(8,128)(2,1)S(1)} %get-tuple-element.28), channel_id=1, source_target_pairs={{16,96},{32,128},{64,144},{80,160},{96,176},{112,192},{144,0},{160... | collective-permute-start | bytes 393224 | tf_op jit(solution)/shard_map/ppermute | solution.py:247
  143.8 1.9 collective-permute-start.10
  145.7 1.9 collective-permute-start.7
  147.7 0.8 slice_bitcast_fusion.5
  148.5 0.7 collective-permute-start.15
  149.1 0.9 collective-permute-start.12
  150.0 0.7 collective-permute-done.13.refs_8_
  150.7 0.7 collective-permute-start.9
  151.4 1.2 slice_bitcast_fusion.1
  152.6 14.7 %collective-permute-done.10.refs_5_ = bf16[512,128]{1,0:T(8,128)(2,1)S(1)} collective-permute-done((bf16[512,128]{1,0:T(8,128)(2,1)S(1)}, bf16[512,128]{1,0:T(8,128)(2,1)S(1)}, u32[]{:S(2)}, u32[]{:S(2)}) %collective-permute-start.10) | collective-permute-done | bytes 131104 | tf_op jit(solution)/shard_map/ppermute | solution.py:247
  167.2 1.9 collective-permute-start.14
  169.2 0.0 collective-permute-done.7.refs_2_
  169.2 7.7 %collective-permute-start.11 = (bf16[512,384]{1,0:T(8,128)(2,1)}, bf16[512,384]{1,0:T(8,128)(2,1)S(1)}, u32[]{:S(2)}, u32[]{:S(2)}) collective-permute-start(bf16[512,384]{1,0:T(8,128)(2,1)} %get-tuple-element.20), channel_id=1, source_target_pairs={{0,96},{16,112},{48,128},{64,144},{80,160},{96,176},{112,192},{128... | collective-permute-start | bytes 1179656 | tf_op jit(solution)/shard_map/ppermute | solution.py:247
  176.9 1.9 collective-permute-start.8
  178.8 0.0 collective-permute-done.12.refs_7_
  178.8 6.6 %collective-permute-start.5 = (bf16[512,384]{1,0:T(8,128)(2,1)}, bf16[512,384]{1,0:T(8,128)(2,1)S(1)}, u32[]{:S(2)}, u32[]{:S(2)}) collective-permute-start(bf16[512,384]{1,0:T(8,128)(2,1)} %get-tuple-element.22), channel_id=1, source_target_pairs={{0,0},{16,16},{48,32},{64,48},{80,64},{112,80},{128,96},{144,112},... | collective-permute-start | bytes 1179656 | tf_op jit(solution)/shard_map/ppermute | solution.py:247
  185.4 0.0 collective-permute-done.9.refs_4_
  185.4 0.7 collective-permute-start.6
  186.1 2.8 %reduce_sum.21 = bf16[4,144,256]{2,1,0:T(8,128)(2,1)} reduce(bf16[8,4,144,256]{3,2,1,0:T(8,128)(2,1)} %all-to-all-done.3, bf16[]{:T(256)} %constant.59.clone.1), dimensions={0}, to_apply=%region_0.1 | reduce | flops 1032192 | bytes 2654210 | tf_op jit(solution)/shard_map/reduce_sum | solution.py:252
  188.9 9.6 %all-to-all-start.4 = ((bf16[4,144,256]{2,1,0:T(8,128)(2,1)}), bf16[4,144,256]{2,1,0:T(8,128)(2,1)S(1)}, u32[]{:S(2)}, u32[]{:S(2)}) async-start(bf16[4,144,256]{2,1,0:T(8,128)(2,1)} %reduce_sum.21), calls=%async_computation.4 | async-start | bytes 589824 | tf_op jit(solution)/shard_map/all_to_all | solution.py:253
  198.5 0.0 collective-permute-done.14.refs_9_
  198.5 10.0 %collective-permute-done.11.refs_6_ = bf16[512,384]{1,0:T(8,128)(2,1)S(1)} collective-permute-done((bf16[512,384]{1,0:T(8,128)(2,1)}, bf16[512,384]{1,0:T(8,128)(2,1)S(1)}, u32[]{:S(2)}, u32[]{:S(2)}) %collective-permute-start.11) | collective-permute-done | bytes 393248 | tf_op jit(solution)/shard_map/ppermute | solution.py:247
  208.6 19.9 %collective-permute-done.8.refs_3_ = bf16[512,384]{1,0:T(8,128)(2,1)S(1)} collective-permute-done((bf16[512,384]{1,0:T(8,128)(2,1)}, bf16[512,384]{1,0:T(8,128)(2,1)S(1)}, u32[]{:S(2)}, u32[]{:S(2)}) %collective-permute-start.8) | collective-permute-done | bytes 393248 | tf_op jit(solution)/shard_map/ppermute | solution.py:247
  228.5 0.0 collective-permute-done.5.refs_0_
  228.5 4.7 %owner_grams.1 = (f32[512,512]{1,0:T(8,128)}, f32[512,512]{1,0:T(8,128)}, f32[512,512]{1,0:T(8,128)}) custom-call(s32[1]{0:T(128)} %bitcast.3.pos, bf16[512,384]{1,0:T(8,128)(2,1)S(1)} %collective-permute-done.5.refs_0_, bf16[512,256]{1,0:T(8,128)(2,1)S(1)} %collective-permute-done.6.refs_1_, bf16[512,128]{1,0:T(8,128)(2,1)S(1)} %collective-permute-done.7.refs_2_, ...), custom_call_target="tpu_custom_call" | custom-call | flops 3200000000 | bytes 8000000 | tf_op jit(solution)/shard_map/owner_grams/pallas_call | solution.py:178
  233.2 0.6 slice_bitcast_fusion.14
  233.8 0.6 slice_bitcast_fusion.13
  (29 shorter events, 0.3 us)
Async XLA Ops:
  0.6 7.9 %copy-start.6 = (bf16[256,576]{0,1:T(8,128)(2,1)S(1)}, bf16[256,576]{0,1:T(8,128)(2,1)}, u32[]{:S(2)}) copy-start(bf16[256,576]{0,1:T(8,128)(2,1)} %param.6) | copy-start | bytes 884740
  2.9 15.5 %all-to-all-start.1 = ((bf16[4,256,256]{2,1,0:T(8,128)(2,1)}), bf16[4,256,256]{2,1,0:T(8,128)(2,1)S(1)}, u32[]{:S(2)}, u32[]{:S(2)}) async-start(bf16[4,256,256]{2,1,0:T(8,128)(2,1)} %bitcast.7), calls=%async_computation.1 | async-start | bytes 1048576 | tf_op jit(solution)/shard_map/all_to_all | solution.py:238
  9.7 6.9 %collective-permute-start.2 = (bf16[272,128]{1,0:T(8,128)(2,1)S(1)}, bf16[272,128]{1,0:T(8,128)(2,1)S(1)}, u32[]{:S(2)}, u32[]{:S(2)}) collective-permute-start(bf16[272,128]{1,0:T(8,128)(2,1)S(1)} %bitcast.59), channel_id=1, source_target_pairs={{0,48},{16,32},{32,16},{48,0},{64,112},{80,96},{96,80},{112,64},{1... | collective-permute-start | bytes 208904 | tf_op jit(solution)/shard_map/ppermute | solution.py:232
  10.9 7.4 %collective-permute-start.1 = (bf16[272,128]{1,0:T(8,128)(2,1)S(1)}, bf16[272,128]{1,0:T(8,128)(2,1)S(1)}, u32[]{:S(2)}, u32[]{:S(2)}) collective-permute-start(bf16[272,128]{1,0:T(8,128)(2,1)S(1)} %bitcast.60), channel_id=1, source_target_pairs={{0,32},{16,48},{32,0},{48,16},{64,96},{80,112},{96,64},{112,80},{1... | collective-permute-start | bytes 208904 | tf_op jit(solution)/shard_map/ppermute | solution.py:232
  11.0 7.4 %collective-permute-start = (bf16[272,128]{1,0:T(8,128)(2,1)S(1)}, bf16[272,128]{1,0:T(8,128)(2,1)S(1)}, u32[]{:S(2)}, u32[]{:S(2)}) collective-permute-start(bf16[272,128]{1,0:T(8,128)(2,1)S(1)} %bitcast.61), channel_id=1, source_target_pairs={{0,16},{16,0},{32,48},{48,32},{64,80},{80,64},{96,112},{112,96},{1... | collective-permute-start | bytes 208904 | tf_op jit(solution)/shard_map/ppermute | solution.py:232
  18.4 6.8 %copy-start.9 = (bf16[32,2048]{1,0:T(8,128)(2,1)S(1)}, bf16[32,2048]{1,0:T(8,128)(2,1)}, u32[]{:S(2)}) copy-start(bf16[32,2048]{1,0:T(8,128)(2,1)} %param.8) | copy-start | bytes 393220
  19.8 5.4 %copy-start.8 = (bf16[96,1536]{1,0:T(8,128)(2,1)S(1)}, bf16[96,1536]{1,0:T(8,128)(2,1)}, u32[]{:S(2)}) copy-start(bf16[96,1536]{1,0:T(8,128)(2,1)} %param.7) | copy-start | bytes 884740
  19.8 24.8 %all-to-all-start = ((bf16[8,816,128]{2,1,0:T(8,128)(2,1)}), bf16[8,816,128]{2,1,0:T(8,128)(2,1)S(1)}, u32[]{:S(2)}, u32[]{:S(2)}) async-start(bf16[8,816,128]{2,1,0:T(8,128)(2,1)} %broadcast_in_dim.10), calls=%async_computation | async-start | bytes 3342336 | tf_op jit(solution)/shard_map/all_to_all | solution.py:234
  25.6 33.5 %copy-start.7 = (bf16[256,576]{0,1:T(8,128)(2,1)S(1)}, bf16[256,576]{0,1:T(8,128)(2,1)}, u32[]{:S(2)}) copy-start(bf16[256,576]{0,1:T(8,128)(2,1)} %param.6) | copy-start | bytes 884740
  44.7 1.8 copy-start.5
  46.5 45.9 %all-to-all-start.2 = ((bf16[16,416,128]{2,1,0:T(8,128)(2,1)}), bf16[16,416,128]{2,1,0:T(8,128)(2,1)S(1)}, u32[]{:S(2)}, u32[]{:S(2)}) async-start(bf16[16,416,128]{2,1,0:T(8,128)(2,1)} %bitcast.12), calls=%async_computation.2 | async-start | bytes 3407872 | tf_op jit(solution)/shard_map/all_to_all | solution.py:240
  55.5 38.0 %collective-permute-start.3 = (bf16[8,816,128]{2,1,0:T(8,128)(2,1)}, bf16[8,816,128]{2,1,0:T(8,128)(2,1)}, u32[]{:S(2)}, u32[]{:S(2)}) collective-permute-start(bf16[8,816,128]{2,1,0:T(8,128)(2,1)} %copy-done.5), channel_id=1, source_target_pairs={{0,1},{1,0},{2,3},{3,2},{4,5},{5,4},{6,7},{7,6},{8,9},{9,8},{10,11... | collective-permute-start | bytes 5013512 | tf_op jit(solution)/shard_map/ppermute | solution.py:235
  92.3 1.3 copy-start.4
  93.6 1.1 copy-start.2
  112.7 2.1 copy-start
  112.7 10.4 %copy-start.3 = (bf16[2,8,4,144,256]{4,3,2,1,0:T(8,128)(2,1)S(1)}, bf16[2,8,4,144,256]{4,3,2,1,0:T(8,128)(2,1)}, u32[]{:S(2)}) copy-start(bf16[2,8,4,144,256]{4,3,2,1,0:T(8,128)(2,1)} %get-tuple-element.12) | copy-start | bytes 14155780
  114.8 8.3 %collective-permute-start.4 = (bf16[8,4,144,256]{3,2,1,0:T(8,128)(2,1)S(1)}, bf16[8,4,144,256]{3,2,1,0:T(8,128)(2,1)S(1)}, u32[]{:S(2)}, u32[]{:S(2)}) collective-permute-start(bf16[8,4,144,256]{3,2,1,0:T(8,128)(2,1)S(1)} %slice_bitcast_fusion), channel_id=1, source_target_pairs={{0,1},{1,0},{2,3},{3,2},{4,5},{5,4},{6,7},{7,6},{8,9},{9,8},{10,11... | collective-permute-start | bytes 7077896 | tf_op jit(solution)/shard_map/ppermute | solution.py:249
  125.2 7.8 %copy-start.1 = (bf16[4,512,128]{2,1,0:T(8,128)(2,1)S(1)}, bf16[4,512,128]{2,1,0:T(8,128)(2,1)}, u32[]{:S(2)}) copy-start(bf16[4,512,128]{2,1,0:T(8,128)(2,1)} %copy-done) | copy-start | bytes 1572868
  125.2 60.9 %all-to-all-start.3 = ((bf16[8,4,144,256]{3,2,1,0:T(8,128)(2,1)}), bf16[8,4,144,256]{3,2,1,0:T(8,128)(2,1)}, u32[]{:S(2)}, u32[]{:S(2)}) async-start(bf16[8,4,144,256]{3,2,1,0:T(8,128)(2,1)} %fusion), calls=%async_computation.3 | async-start | bytes 4718592 | tf_op jit(solution)/shard_map/all_to_all | solution.py:251
  133.1 16.0 %collective-permute-start.16 = (bf16[512,128]{1,0:T(8,128)(2,1)S(1)}, bf16[512,128]{1,0:T(8,128)(2,1)S(1)}, u32[]{:S(2)}, u32[]{:S(2)}) collective-permute-start(bf16[512,128]{1,0:T(8,128)(2,1)S(1)} %get-tuple-element.27), channel_id=1, source_target_pairs={{0,144},{16,160},{32,176},{48,192},{80,0},{96,32},{144,48},{160,80... | collective-permute-start | bytes 393224 | tf_op jit(solution)/shard_map/ppermute | solution.py:247
  138.7 12.0 %collective-permute-start.13 = (bf16[512,128]{1,0:T(8,128)(2,1)S(1)}, bf16[512,128]{1,0:T(8,128)(2,1)S(1)}, u32[]{:S(2)}, u32[]{:S(2)}) collective-permute-start(bf16[512,128]{1,0:T(8,128)(2,1)S(1)} %get-tuple-element.28), channel_id=1, source_target_pairs={{16,96},{32,128},{64,144},{80,160},{96,176},{112,192},{144,0},{160... | collective-permute-start | bytes 393224 | tf_op jit(solution)/shard_map/ppermute | solution.py:247
  143.8 23.4 %collective-permute-start.10 = (bf16[512,128]{1,0:T(8,128)(2,1)S(1)}, bf16[512,128]{1,0:T(8,128)(2,1)S(1)}, u32[]{:S(2)}, u32[]{:S(2)}) collective-permute-start(bf16[512,128]{1,0:T(8,128)(2,1)S(1)} %get-tuple-element.29), channel_id=1, source_target_pairs={{16,48},{32,80},{80,96},{96,128},{128,144},{144,160},{160,176},{17... | collective-permute-start | bytes 393224 | tf_op jit(solution)/shard_map/ppermute | solution.py:247
  145.7 23.4 %collective-permute-start.7 = (bf16[512,128]{1,0:T(8,128)(2,1)S(1)}, bf16[512,128]{1,0:T(8,128)(2,1)S(1)}, u32[]{:S(2)}, u32[]{:S(2)}) collective-permute-start(bf16[512,128]{1,0:T(8,128)(2,1)S(1)} %get-tuple-element.30), channel_id=1, source_target_pairs={{16,0},{32,32},{80,48},{96,80},{144,96},{160,128},{192,144},{208,1... | collective-permute-start | bytes 393224 | tf_op jit(solution)/shard_map/ppermute | solution.py:247
  148.5 28.4 %collective-permute-start.15 = (bf16[512,256]{1,0:T(8,128)(2,1)S(1)}, bf16[512,256]{1,0:T(8,128)(2,1)S(1)}, u32[]{:S(2)}, u32[]{:S(2)}) collective-permute-start(bf16[512,256]{1,0:T(8,128)(2,1)S(1)} %get-tuple-element.23), channel_id=1, source_target_pairs={{96,16},{160,64},{224,112},{97,17},{161,65},{225,113},{98,18},{162... | collective-permute-start | bytes 786440 | tf_op jit(solution)/shard_map/ppermute | solution.py:247
  149.1 29.6 %collective-permute-start.12 = (bf16[512,256]{1,0:T(8,128)(2,1)S(1)}, bf16[512,256]{1,0:T(8,128)(2,1)S(1)}, u32[]{:S(2)}, u32[]{:S(2)}) collective-permute-start(bf16[512,256]{1,0:T(8,128)(2,1)S(1)} %get-tuple-element.24), channel_id=1, source_target_pairs={{32,112},{160,16},{224,64},{33,113},{161,17},{225,65},{34,114},{16... | collective-permute-start | bytes 786440 | tf_op jit(solution)/shard_map/ppermute | solution.py:247
  150.7 34.7 %collective-permute-start.9 = (bf16[512,256]{1,0:T(8,128)(2,1)S(1)}, bf16[512,256]{1,0:T(8,128)(2,1)S(1)}, u32[]{:S(2)}, u32[]{:S(2)}) collective-permute-start(bf16[512,256]{1,0:T(8,128)(2,1)S(1)} %get-tuple-element.25), channel_id=1, source_target_pairs={{32,64},{96,112},{224,16},{33,65},{97,113},{225,17},{34,66},{98,11... | collective-permute-start | bytes 786440 | tf_op jit(solution)/shard_map/ppermute | solution.py:247
  167.2 31.3 %collective-permute-start.14 = (bf16[512,384]{1,0:T(8,128)(2,1)}, bf16[512,384]{1,0:T(8,128)(2,1)S(1)}, u32[]{:S(2)}, u32[]{:S(2)}) collective-permute-start(bf16[512,384]{1,0:T(8,128)(2,1)} %get-tuple-element.19), channel_id=1, source_target_pairs={{0,144},{16,160},{32,176},{48,192},{64,0},{80,16},{112,32},{128,48... | collective-permute-start | bytes 1179656 | tf_op jit(solution)/shard_map/ppermute | solution.py:247
  169.2 39.4 %collective-permute-start.11 = (bf16[512,384]{1,0:T(8,128)(2,1)}, bf16[512,384]{1,0:T(8,128)(2,1)S(1)}, u32[]{:S(2)}, u32[]{:S(2)}) collective-permute-start(bf16[512,384]{1,0:T(8,128)(2,1)} %get-tuple-element.20), channel_id=1, source_target_pairs={{0,96},{16,112},{48,128},{64,144},{80,160},{96,176},{112,192},{128... | collective-permute-start | bytes 1179656 | tf_op jit(solution)/shard_map/ppermute | solution.py:247
  176.9 51.6 %collective-permute-start.8 = (bf16[512,384]{1,0:T(8,128)(2,1)}, bf16[512,384]{1,0:T(8,128)(2,1)S(1)}, u32[]{:S(2)}, u32[]{:S(2)}) collective-permute-start(bf16[512,384]{1,0:T(8,128)(2,1)} %get-tuple-element.21), channel_id=1, source_target_pairs={{0,48},{16,64},{48,80},{64,96},{80,112},{112,128},{128,144},{144,1... | collective-permute-start | bytes 1179656 | tf_op jit(solution)/shard_map/ppermute | solution.py:247
  178.8 49.7 %collective-permute-start.5 = (bf16[512,384]{1,0:T(8,128)(2,1)}, bf16[512,384]{1,0:T(8,128)(2,1)S(1)}, u32[]{:S(2)}, u32[]{:S(2)}) collective-permute-start(bf16[512,384]{1,0:T(8,128)(2,1)} %get-tuple-element.22), channel_id=1, source_target_pairs={{0,0},{16,16},{48,32},{64,48},{80,64},{112,80},{128,96},{144,112},... | collective-permute-start | bytes 1179656 | tf_op jit(solution)/shard_map/ppermute | solution.py:247
  185.4 13.1 %collective-permute-start.6 = (bf16[512,256]{1,0:T(8,128)(2,1)}, bf16[512,256]{1,0:T(8,128)(2,1)S(1)}, u32[]{:S(2)}, u32[]{:S(2)}) collective-permute-start(bf16[512,256]{1,0:T(8,128)(2,1)} %get-tuple-element.26), channel_id=1, source_target_pairs={{32,16},{96,64},{160,112},{33,17},{97,65},{161,113},{34,18},{98,66... | collective-permute-start | bytes 786440 | tf_op jit(solution)/shard_map/ppermute | solution.py:247
  188.9 44.2 %all-to-all-start.4 = ((bf16[4,144,256]{2,1,0:T(8,128)(2,1)}), bf16[4,144,256]{2,1,0:T(8,128)(2,1)S(1)}, u32[]{:S(2)}, u32[]{:S(2)}) async-start(bf16[4,144,256]{2,1,0:T(8,128)(2,1)} %reduce_sum.21), calls=%async_computation.4 | async-start | bytes 589824 | tf_op jit(solution)/shard_map/all_to_all | solution.py:253

commit v2 on v0

v2 whole, which is shorter than its diff:
```python
import math

import jax
import jax.numpy as jnp
from jax import lax
from jax.experimental import pallas as pl
from jax.experimental.pallas import tpu as pltpu
from jax.sharding import PartitionSpec as P

KVL = 512
NOPE = 128
ROPE = 64
VD = 128
BLK = 512
QK = NOPE + ROPE
SCALE = 1.0 / math.sqrt(QK)
LOG2E = math.log2(math.e)

F32 = jnp.float32
BF16 = jnp.bfloat16
WHOLE = 60


def dot(a, b, ca, cb):
    return lax.dot_general(a, b, (((ca,), (cb,)), ((), ())), preferred_element_type=F32)


def send_kernel(
    pos, ql_in, klt_in, qu_in, ku_in, grad, send1, send2, send3, own_w, og0, og1, og2, og3, kl, ql, klt, qu, ku, sems
):
    core, chip, member = pos[0], pos[1], pos[2]
    rows = pl.ds(pl.multiple_of(128 * core + 16 * chip, 16), 16)
    pairs = [(qu_in, qu), (ku_in, ku), (klt_in, klt), (ql_in.at[rows], ql)]
    copies_in = [pltpu.make_async_copy(x, y, sems.at[i]) for i, (x, y) in enumerate(pairs)]
    copies = []
    for s, out in enumerate((og0, og1, og2, og3)):
        for h in range(2):
            columns = pl.ds(pl.multiple_of(256 * (member ^ s) + 128 * h, 128), 128)
            part = pl.ds(256 * h, 256)
            copies.append(pltpu.make_async_copy(grad.at[:, columns], out.at[part], sems.at[4 + 2 * s + h]))
    for copy in copies_in + copies:
        copy.start()
    for copy in copies_in:
        copy.wait()
    kl[...] = klt[...].T
    for s, out in enumerate((own_w, send1, send2, send3)):
        to = 272 if s else 0
        for t in range(3):
            columns = pl.ds(pl.multiple_of(384 * (member ^ s) + 128 * t, 128), 128)
            out[to + 96 * t : to + 96 * t + 96, :] = qu[:, columns]
        for t in range(4):
            columns = pl.ds(pl.multiple_of(512 * (member ^ s) + 128 * t, 128), 128)
            out[to + 288 + 32 * t : to + 320 + 32 * t, :] = ku[:, columns]
        if s == 0:
            continue
        for t in range(12):
            out[16 * t : 16 * t + 16, :] = ql[:, 128 * t : 128 * t + 128]
        for t in range(4):
            out[192 + 16 * t : 208 + 16 * t, :] = kl[rows, 128 * t : 128 * t + 128]
        out[256:272, :ROPE] = kl[rows, KVL:]
        out[256:272, ROPE:] = jnp.zeros((16, 128 - ROPE), BF16)
    for copy in copies:
        copy.wait()


def latent_kernel(pos, ql, kl, *refs):
    lats, outs, (lq, lk, rope, sems) = refs[:8], refs[8:11], refs[11:]
    core, chip = pos[0], pos[1]
    lq[0:256, :] = ql[...]
    lk[0:256, :] = kl[:, :KVL]
    rope[0:256, :] = kl[:, KVL:]
    copies = []
    for s in range(4):
        for side in range(2 if s else 0):
            base = 128 * (core ^ side)
            for step in range(4):
                lat = lats[4 * side + step]
                for y in range(2):
                    source = 2 * ((chip // 2 - step + 4) % 4) + ((chip % 2) ^ y)
                    rows = pl.ds(pl.multiple_of(256 * s + base + 16 * source, 16), 16)
                    at = 272 * (s - 1)
                    for t in range(12):
                        lq[rows, 128 * t : 128 * t + 128] = lat[y, at + 16 * t : at + 16 * t + 16, :]
                    for t in range(4):
                        lk[rows, 128 * t : 128 * t + 128] = lat[y, at + 192 + 16 * t : at + 208 + 16 * t, :]
                    rope[rows, :] = lat[y, at + 256 : at + 272, :ROPE]
        part = pl.ds(256 * s, 256)
        for i, (source, out) in enumerate(zip((lq, lk, rope), outs)):
            copies.append(pltpu.make_async_copy(source.at[part], out.at[part], sems.at[s, i]))
            copies[-1].start()
    for copy in copies:
        copy.wait()


def call(kernel, name, out_shape, vmem_mib, args, scratch=(), out_specs=None, in_specs=None, flops=0, size=0, scalars=False):
    vmem = pl.BlockSpec(memory_space=pltpu.VMEM)
    specs = [vmem] * len(args)
    if scalars:
        specs[0] = pl.BlockSpec(memory_space=pltpu.SMEM)
    return pl.pallas_call(
        kernel,
        out_shape=out_shape,
        in_specs=specs if in_specs is None else in_specs,
        out_specs=[vmem] * len(out_shape) if out_specs is None else out_specs,
        scratch_shapes=scratch,
        compiler_params=pltpu.CompilerParams(vmem_limit_bytes=vmem_mib * 1024 * 1024),
        cost_estimate=pl.CostEstimate(flops=flops, bytes_accessed=size, transcendentals=0),
        name=name,
    )(*args)


def main_kernel(
    pos, lq_in, lk_in, rope_in, og0, og1, og2, og3, w0, w1, w2, w3, w4, out, given_out, wq_out, wkv_out,
    lq, lk, rope, og, wq3, wkv3, dq, dkv, drope, term, wq2, wkv2, w, row_sems, sems,
):
    core, member, group = pos[0], pos[2], pos[3]
    starts, at = [], 0
    for i, piece in enumerate((w0, w1, w2, w3, w4)):
        starts.append(pltpu.make_async_copy(piece, w.at[pl.ds(at, piece.shape[0])], sems.at[i]))
        at += piece.shape[0]
    for copy in starts:
        copy.start()

    def row_copies(s):
        part = pl.ds(256 * s, 256)
        pairs = [(lq_in, lq), (lk_in, lk), (rope_in, rope)]
        copies = [pltpu.make_async_copy(x.at[part], y.at[part], row_sems.at[s, i]) for i, (x, y) in enumerate(pairs)]
        return copies + [pltpu.make_async_copy((og0, og1, og2, og3)[s], og.at[s], row_sems.at[s, 3])]

    rows_in = [row_copies(s) for s in range(4)]
    for copies in rows_in:
        for copy in copies:
            copy.start()
    for copy in starts:
        copy.wait()
    for copy in rows_in[0]:
        copy.wait()
    for j, a in enumerate((0, 3, 1, 2)):
        for i in range(4):
            d = 4 * ((group + a) % 4) + (member ^ i)
            for t in range(3):
                wq3[d, :, 128 * t : 128 * t + 128] = w[4 * j + i, 96 * t : 96 * t + 96, :]
            for t in range(4):
                wkv3[d, :, 128 * t : 128 * t + 128] = w[4 * j + i, 288 + 32 * t : 320 + 32 * t, :]
    wq, wkv = wq3[...].reshape(1536, 384), wkv3[...].reshape(512, 512)
    wide = wkv.astype(F32)
    for h in range(16):
        side = (h % 2) ^ core
        own = min(max(KVL - 36 * h, 0), 36)
        wq2[side, 96 * (h // 2) : 96 * (h // 2) + 96, :] = wq[96 * h : 96 * h + 96, :]
        piece = jnp.zeros((48, 512), F32)
        if own:
            piece = jnp.concatenate([wide[36 * h : 36 * h + own, :], piece[own:]], axis=0)
        wkv2[side, 48 * (h // 2) : 48 * (h // 2) + 48, :] = piece.astype(BF16)
    ends = [
        pltpu.make_async_copy(wq2.at[0], wq_out, sems.at[7]),
        pltpu.make_async_copy(wkv2.at[0], wkv_out, sems.at[8]),
    ]
    for i, (source, to, tiles) in enumerate(((wq2.at[1], 7680, 3), (wkv2.at[1], 9984, 4))):
        size = source.shape[0]
        for t in range(tiles):
            part = given_out.at[pl.ds(to + size * t, size)]
            ends.append(pltpu.make_async_copy(source.at[:, pl.ds(128 * t, 128)], part, sems.at[16 + 4 * i + t]))
    for copy in ends:
        copy.start()

    causal = lax.broadcasted_iota(jnp.int32, (256, 256), 0) >= lax.broadcasted_iota(jnp.int32, (256, 256), 1)

    for s in range(4):
        if s:
            for copy in rows_in[s]:
                copy.wait()
        rows = pl.ds(256 * s, 256)
        query = dot(lq[rows, :], wq, 1, 0)
        keyval = dot(lk[rows, :], wkv, 1, 0).astype(BF16)
        rope_key = rope[rows, :]
        rope_sum = jnp.zeros((256, ROPE), F32)
        dq_parts = []
        for h in range(2):
            q_h = query[:, QK * h : QK * h + QK].astype(BF16)
            key = jnp.concatenate([keyval[:, 256 * h : 256 * h + 128], rope_key], axis=1)
            value = keyval[:, 256 * h + 128 : 256 * h + 256]
            grad = og[s, 256 * h : 256 * h + 256, :]
            weights = jnp.where(causal, jnp.exp2(dot(q_h, key, 1, 1) * (SCALE * LOG2E)), 0.0)
            weights = weights / jnp.sum(weights, axis=1, keepdims=True)
            probs = weights.astype(BF16)
            dprob = dot(grad, value, 1, 1)
            delta = jnp.sum(probs.astype(F32) * dprob, axis=1, keepdims=True)
            dscore = (weights * (dprob - delta) * SCALE).astype(BF16)
            dvalue = dot(probs, grad, 0, 0).astype(BF16)
            dq_parts.append(dot(dscore, key, 1, 0))
            dkey = dot(dscore, q_h, 0, 0)
            dkv[rows, 256 * h : 256 * h + 128] = dkey[:, :NOPE].astype(BF16)
            dkv[rows, 256 * h + 128 : 256 * h + 256] = dvalue
            rope_sum = rope_sum + dkey[:, NOPE:].astype(BF16).astype(F32)
        dq[rows, :] = jnp.concatenate(dq_parts, axis=1).astype(BF16)
        drope[:, 256 * s : 256 * s + 256] = rope_sum.T.astype(BF16)
        to = 1920 * s
        for i, (source, size, tiles) in enumerate(((dq.at[rows], 256, 3), (dkv.at[rows], 256, 4), (drope, ROPE, 2))):
            for t in range(tiles):
                columns = pl.ds(128 * t if i < 2 else 256 * s + 128 * t, 128)
                part = given_out.at[pl.ds(to, size)]
                ends.append(pltpu.make_async_copy(source.at[:, columns], part, sems.at[24 + 9 * s + 4 * i - min(i, 1) + t]))
                ends[-1].start()
                to += size

    for block in (3, 0, 1, 2):
        if block == 3:
            value = dot(lk[...], dkv[...], 0, 0).astype(BF16)
        else:
            value = dot(lq[:, 512 * block : 512 * block + 512], dq[...], 0, 0).astype(BF16)
        tiles = value.shape[1] // 128
        for d in range(16):
            for t in range(tiles):
                term[d, 3 * block + t] = value[32 * d : 32 * d + 32, 128 * t : 128 * t + 128]
        part = pl.ds(3 * block, tiles)
        ends.append(pltpu.make_async_copy(term.at[:, part], out.at[:, part], sems.at[12 + block]))
        ends[-1].start()
    for copy in ends:
        copy.wait()


def main_call(*args):
    shape = jax.ShapeDtypeStruct
    hbm = pl.BlockSpec(memory_space=pltpu.HBM)
    return call(
        main_kernel,
        "mla_backward",
        (
            shape((16, 13, 32, 128), BF16),
            shape((11520, 128), BF16),
            shape((768, 384), BF16),
            shape((384, 512), BF16),
        ),
        WHOLE,
        args,
        scratch=[
            pltpu.VMEM((1024, 1536), BF16),
            pltpu.VMEM((1024, 512), BF16),
            pltpu.VMEM((1024, ROPE), BF16),
            pltpu.VMEM((4, 512, 128), BF16),
            pltpu.VMEM((16, 96, 384), BF16),
            pltpu.VMEM((16, 32, 512), BF16),
            pltpu.VMEM((1024, 384), BF16),
            pltpu.VMEM((1024, 512), BF16),
            pltpu.VMEM((ROPE, 1024), BF16),
            pltpu.VMEM((16, 13, 32, 128), BF16),
            pltpu.VMEM((2, 768, 384), BF16),
            pltpu.VMEM((2, 384, 512), BF16),
            pltpu.VMEM((16, 416, 128), BF16),
            pltpu.SemaphoreType.DMA((4, 4)),
            pltpu.SemaphoreType.DMA((64,)),
        ],
        in_specs=[pl.BlockSpec(memory_space=pltpu.SMEM)] + [hbm] * 12,
        out_specs=[hbm] * 4,
        flops=4_500_000_000,
        size=12_000_000,
    )


def latent_grad_kernel(pos, mine, other, w_other, wq, wkv, *outs):
    core, chip = pos[0], pos[1]

    def wide(ref, at, size, tiles):
        return jnp.concatenate([ref[at + size * t : at + size * t + size, :] for t in range(tiles)], axis=1)

    wq_other, wkv_other = wide(w_other, 0, 768, 3), wide(w_other, 2304, 384, 4)
    q_term = dot(wq[...], wide(mine, 0, 256, 3), 1, 1) + dot(wq_other, wide(other, 0, 256, 3), 1, 1)
    kv_term = dot(wkv[...], wide(mine, 768, 256, 4), 1, 1) + dot(wkv_other, wide(other, 768, 256, 4), 1, 1)
    rotated = wide(mine, 1792, ROPE, 2).astype(F32) + wide(other, 1792, ROPE, 2).astype(F32)
    tail = jnp.zeros((48, 256), F32)
    on_0 = jnp.concatenate([tail[:8], rotated[:28], tail[36:]], axis=0)
    on_1 = jnp.concatenate([rotated[28:], tail[36:]], axis=0)
    last = kv_term[336:384] + jnp.where(core == 0, on_0, on_1)
    q_term = q_term.astype(BF16)
    kv_term = jnp.concatenate([kv_term[:336], last], axis=0).astype(BF16)
    for x in range(4):
        for y in range(2):
            h = 2 * x + y
            to_x, to_y = (x - chip // 2 + 4) % 4, y ^ (chip % 2)
            for k in range(4):

                @pl.when(to_x == k)
                def _():
                    outs[k][to_y, 0, 0:96, :] = q_term[96 * h : 96 * h + 96, :]
                    outs[k][to_y, 0, 96:144, :] = kv_term[48 * h : 48 * h + 48, :]


def latent_grad_call(pos, mine, other, wq, wkv):
    def whole(x):
        return pl.BlockSpec(x.shape, lambda s: (0, 0))

    sequence = pl.BlockSpec((1920, 128), lambda s: (s, 0))
    return pl.pallas_call(
        latent_grad_kernel,
        out_shape=[jax.ShapeDtypeStruct((2, 4, 144, 256), BF16)] * 4,
        grid=(4,),
        in_specs=[pl.BlockSpec(memory_space=pltpu.SMEM)]
        + [sequence, sequence, pl.BlockSpec((3840, 128), lambda s: (2, 0)), whole(wq), whole(wkv)],
        out_specs=[pl.BlockSpec((2, 1, 144, 256), lambda s: (0, s, 0, 0))] * 4,
        compiler_params=pltpu.CompilerParams(vmem_limit_bytes=WHOLE * 1024 * 1024),
        cost_estimate=pl.CostEstimate(flops=1_800_000_000, bytes_accessed=12_000_000, transcendentals=0),
        name="latent_grads",
    )(pos, mine, other, other, wq, wkv)


def strip_kernel(terms, strips):
    def summed(m, p):
        return sum(terms[4 * a + m, p].astype(F32) for a in range(4)).astype(BF16)

    for block in range(16):
        for u in range(4):
            if block < 9:
                column = 4 * (block % 3) + u
                strips[block, u] = summed(column // 3, 3 * (block // 3) + column % 3)
            elif block < 13:
                strips[block, u] = summed(block - 9, 9 + u)
            else:
                strips[block, u] = jnp.zeros((32, 128), BF16)


def gram_kernel(strips, grad, left, right):
    for d in range(16):
        for u in range(4):
            grad[32 * d : 32 * d + 32, 128 * u : 128 * u + 128] = strips[d, u].astype(F32)
    g = grad[...]
    highest = lax.Precision.HIGHEST
    left[...] = lax.dot_general(g, g, (((1,), (1,)), ((), ())), precision=highest, preferred_element_type=F32)
    right[...] = lax.dot_general(g, g, (((0,), (0,)), ((), ())), precision=highest, preferred_element_type=F32)


PARTNER = [[(i, i ^ s) for i in range(16)] for s in range(4)]
GROUP_UP = [(i, (i + 4) % 16) for i in range(16)]
GROUP_DOWN = [(i, (i + 12) % 16) for i in range(16)]
OTHER_CORE = [(i, i ^ 1) for i in range(16)]
ACROSS_Y = [(i, i ^ 2) for i in range(16)]
ALONG_X = [[(i, (i + 4 * k) % 16) for i in range(16)] for k in range(4)]


def per_device(q_latent, kv_latent, q_up, kv_up, out_grad):
    dp, head = lax.axis_index("dp"), lax.axis_index("head")
    member = dp % 4
    core, chip = head % 2, head // 2
    pos = jnp.stack([core, chip, member, dp // 4]).astype(jnp.int32)
    shape = jax.ShapeDtypeStruct
    vmem, hbm = pl.BlockSpec(memory_space=pltpu.VMEM), pl.BlockSpec(memory_space=pltpu.HBM)

    send, grad = shape((688, 128), BF16), shape((512, 128), BF16)
    *sends, own_w, og0, og1, og2, og3, kl = call(
        send_kernel,
        "send_rows",
        (send,) * 3 + (shape((416, 128), BF16),) + (grad,) * 4 + (shape((256, 576), BF16),),
        WHOLE,
        (pos, q_latent, kv_latent.T, q_up, kv_up, out_grad),
        scratch=[
            pltpu.VMEM((16, 1536), BF16),
            pltpu.VMEM((576, 256), BF16),
            pltpu.VMEM((96, 1536), BF16),
            pltpu.VMEM((32, 2048), BF16),
            pltpu.SemaphoreType.DMA((12,)),
        ],
        in_specs=[pl.BlockSpec(memory_space=pltpu.SMEM)] + [hbm] * 5,
        size=4_000_000,
        scalars=True,
    )
    parts = [lax.ppermute(sends[s - 1], "dp", PARTNER[s]) for s in (1, 2, 3)]
    w = jnp.stack([own_w] + [part[272:] for part in parts])
    from_down = lax.ppermute(w, "dp", GROUP_UP)
    from_up = lax.ppermute(w, "dp", GROUP_DOWN)
    far = [lax.ppermute(from_down[:2], "dp", GROUP_UP), lax.ppermute(from_up[2:], "dp", GROUP_DOWN)]
    ogs, _ = lax.optimization_barrier(((og1, og2, og3), (from_down, from_up)))
    ogs = [og0] + [lax.ppermute(ogs[s - 1], "dp", PARTNER[s]) for s in (1, 2, 3)]
    near = jnp.concatenate([part[:272] for part in parts], axis=0)
    near = jnp.stack([near, lax.ppermute(near, "head", ACROSS_Y)])
    lats = [near] + [lax.ppermute(near, "head", ALONG_X[k]) for k in (1, 2, 3)]
    lats, _ = lax.optimization_barrier((lats, (from_down, from_up)))
    lats = lats + [lax.ppermute(lat, "head", OTHER_CORE) for lat in lats]

    rows = (shape((1024, 1536), BF16), shape((1024, 512), BF16), shape((1024, ROPE), BF16))
    lq, lk, rope = call(
        latent_kernel,
        "latent_rows",
        rows,
        WHOLE,
        (pos, q_latent, kl, *lats),
        scratch=[pltpu.VMEM(x.shape, BF16) for x in rows] + [pltpu.SemaphoreType.DMA((4, 3))],
        out_specs=[hbm] * 3,
        size=9_000_000,
        scalars=True,
    )
    terms, mine, wq, wkv = main_call(pos, lq, lk, rope, *ogs, w, from_down, from_up, *far)
    terms = lax.all_to_all(terms, "dp", 0, 0, tiled=True)

    other = lax.ppermute(mine, "head", OTHER_CORE)
    parts = latent_grad_call(pos, mine, other, wq, wkv)
    parts = [parts[0]] + [lax.ppermute(parts[k], "head", ALONG_X[k]) for k in (1, 2, 3)]
    part = sum(p.astype(F32) for p in parts)
    across = lax.ppermute(part[1].astype(BF16), "head", ACROSS_Y)
    (strips,) = call(strip_kernel, "block_strips", (shape((16, 4, 32, 128), BF16),), 8, (terms,), size=3_000_000)
    part = (part[0] + across.astype(F32)).astype(BF16)
    parts = [part[0]] + [lax.ppermute(part[s], "dp", PARTNER[s]) for s in (1, 2, 3)]
    strips = lax.all_to_all(strips, "dp", 0, 0, tiled=True)
    block = shape((BLK, BLK), F32)
    owned, left, right = call(
        gram_kernel, "owner_grams", (block, block, block), 16, (strips,), flops=3_200_000_000, size=4_000_000
    )
    parts, _ = lax.optimization_barrier((parts, left))
    part = sum(p.astype(F32) for p in parts)
    d_q = part[:96].T.astype(BF16)
    d_kv = part[96:132].T.astype(BF16)
    return d_q, d_kv, owned[None], left[None], right[None]


def solution(mesh):
    return jax.shard_map(
        per_device,
        mesh=mesh,
        in_specs=(P("dp", None), P("dp", None), P("dp", "head"), P("dp", "head"), P("dp", "head")),
        out_specs=(
            P("dp", "head"),
            P("dp", "head"),
            P(("head", "dp"), None, None),
            P(("head", "dp"), None, None),
            P(("head", "dp"), None, None),
        ),
        check_vma=False,
    )
```

time: 630 us -> 170 us (0.27)
  waiting for transfers between devices: 542 us -> 80.8 us
  starting transfers between devices: 0.2 us -> 47.2 us
  Pallas kernels: 0 us -> 35.2 us
  local copies, waits for them, and re-layouts: 32.6 us -> 2.1 us
  matrix products: 26.4 us -> 0 us
  between operations: 14.7 us -> 0.96 us
    reduce_scatter x2 -> x0, waiting for transfers between devices: 282 us -> none  [the longest x1 229 us: per_device(): lax.psum_scatter(jnp.concatenate([local_blocks, filler], axis=0).astype(j...]
    all_gather x2 -> x0, waiting for transfers between devices: 188 us -> none  [the longest x1 99.4 us: per_device(): lax.all_gather(q_up, 'dp', axis=0, tiled=True)]
    unnamed x6 -> x0, waiting for transfers between devices: 72 us -> none
    ppermute x0 -> x26, waiting for transfers between devices: none -> 47.2 us  [the longest x1 10.2 us: per_device(): across = lax.ppermute(part[1].astype(BF16), 'head', ACROSS_Y)]
    ppermute x0 -> x26, starting transfers between devices: none -> 37.4 us  [the longest x3 6.09 us: per_device(): lax.ppermute(part[s], 'dp', PARTNER[s])]
    pallas_call x0 -> x6, Pallas kernels: none -> 35.2 us  [the longest x5 28.1 us: call(): pl.pallas_call(kernel, out_shape=out_shape, in_specs=specs if in_specs is...]
    all_to_all x0 -> x2, waiting for transfers between devices: none -> 33.6 us  [the longest x1 33.6 us: per_device(): terms = lax.all_to_all(terms, 'dp', 0, 0, tiled=True)]
    dot_general x14 -> x0, matrix products: 26.4 us -> none  [the longest x1 4.66 us: per_device(): wq_grad = jnp.dot(q_latent.T, dq_flat, preferred_element_type=jnp.float32)]
  transfers between devices with their start and end apart: 5 -> 28, of which waited for: 5 -> 12; matrix products, arithmetic and copies ran while one was open for 8% -> 1% of each run, Pallas kernels for 0% -> 10%
where the time goes in v2:
time: 170 us; the launch traced here: 168 us
  waiting for transfers between devices  80.8 us (48%)
  starting transfers between devices  47.2 us (28%)
  Pallas kernels  35.2 us (21%)
  other arithmetic  2.23 us (1%)
  local copies, waits for them, and re-layouts  2.1 us (1%)
    all_to_all x1, waiting for transfers between devices, per_device(): terms = lax.all_to_all(terms, 'dp', 0, 0, tiled=True)  33.6 us
    pallas_call x5, Pallas kernels, call(): pl.pallas_call(kernel, out_shape=out_shape, in_specs=specs if in_specs is...  28.1 us
    ppermute x1, waiting for transfers between devices, per_device(): across = lax.ppermute(part[1].astype(BF16), 'head', ACROSS_Y)  10.2 us
    ppermute x1, waiting for transfers between devices, per_device(): from_down = lax.ppermute(w, 'dp', GROUP_UP)  8.87 us
    ppermute x3, waiting for transfers between devices, per_device(): lax.ppermute(ogs[s - 1], 'dp', PARTNER[s])  8.7 us
    ppermute x3, waiting for transfers between devices, per_device(): parts = [lax.ppermute(sends[s - 1], 'dp', PARTNER[s]) for s in (1, 2, 3)]  8.24 us
    pallas_call x1, Pallas kernels, latent_grad_call(): pl.pallas_call(latent_grad_kernel, out_shape=[jax.ShapeDtypeStruct((2, 4,...  7.05 us
    ppermute x1, waiting for transfers between devices, per_device(): from_up = lax.ppermute(w, 'dp', GROUP_DOWN)  6.81 us
  transfers between devices with their start and end apart: 28, of which 12 were waited for; matrix products, arithmetic and copies ran while one was open for 1% of the time, Pallas kernels for 10%

profile of v2, /device:TPU:6, one launch (start us, length us, event | category | flops | bytes accessed | tf_op | source)
XLA Modules:
  0.0 168.5 jit_solution(9605574061188712833)
XLA Ops:
  0.7 0.7 pad_add_fusion.pos
  1.3 3.2 %send_rows.1 = (bf16[688,128]{1,0:T(8,128)(2,1)}, bf16[688,128]{1,0:T(8,128)(2,1)}, bf16[688,128]{1,0:T(8,128)(2,1)}, bf16[416,128]{1,0:T(8,128)(2,1)}, bf16[512...) custom-call(s32[4]{0:T(128)} %pad_add_fusion.pos, ...), custom_call_target="tpu_custom_call" | custom-call | bytes 4000000 | tf_op jit(solution)/shard_map/send_rows/pallas_call | solution.py:100
  4.6 3.3 %collective-permute-start = (bf16[688,128]{1,0:T(8,128)(2,1)}, bf16[688,128]{1,0:T(8,128)(2,1)S(1)}, u32[]{:S(2)}, u32[]{:S(2)}) collective-permute-start(bf16[688,128]{1,0:T(8,128)(2,1)} %get-tuple-element.40), channel_id=1, source_target_pairs={{0,16},{16,0},{32,48},{48,32},{64,80},{80,64},{96,112},{112,96},{1... | collective-permute-start | bytes 528392 | tf_op jit(solution)/shard_map/ppermute | solution.py:366
  7.8 1.9 %collective-permute-start.1 = (bf16[688,128]{1,0:T(8,128)(2,1)}, bf16[688,128]{1,0:T(8,128)(2,1)S(1)}, u32[]{:S(2)}, u32[]{:S(2)}) collective-permute-start(bf16[688,128]{1,0:T(8,128)(2,1)} %get-tuple-element.41), channel_id=1, source_target_pairs={{0,32},{16,48},{32,0},{48,16},{64,96},{80,112},{96,64},{112,80},{1... | collective-permute-start | bytes 528392 | tf_op jit(solution)/shard_map/ppermute | solution.py:366
  9.8 0.0 collective-permute-start.2
  9.8 2.8 %collective-permute-done = bf16[688,128]{1,0:T(8,128)(2,1)S(1)} collective-permute-done((bf16[688,128]{1,0:T(8,128)(2,1)}, bf16[688,128]{1,0:T(8,128)(2,1)S(1)}, u32[]{:S(2)}, u32[]{:S(2)}) %collective-permute-start) | collective-permute-done | bytes 176160 | tf_op jit(solution)/shard_map/ppermute | solution.py:366
  12.6 2.8 %collective-permute-done.1 = bf16[688,128]{1,0:T(8,128)(2,1)S(1)} collective-permute-done((bf16[688,128]{1,0:T(8,128)(2,1)}, bf16[688,128]{1,0:T(8,128)(2,1)S(1)}, u32[]{:S(2)}, u32[]{:S(2)}) %collective-permute-start.1) | collective-permute-done | bytes 176160 | tf_op jit(solution)/shard_map/ppermute | solution.py:366
  15.4 2.6 %collective-permute-done.2 = bf16[688,128]{1,0:T(8,128)(2,1)S(1)} collective-permute-done((bf16[688,128]{1,0:T(8,128)(2,1)}, bf16[688,128]{1,0:T(8,128)(2,1)S(1)}, u32[]{:S(2)}, u32[]{:S(2)}) %collective-permute-start.2) | collective-permute-done | bytes 176160 | tf_op jit(solution)/shard_map/ppermute | solution.py:366
  18.1 1.3 collective-permute-start.3
  19.5 0.1 pad_maximum_fusion.w0
  19.5 0.0 copy-start.2
  19.5 3.3 %collective-permute-start.7 = (bf16[4,416,128]{2,1,0:T(8,128)(2,1)S(1)}, bf16[4,416,128]{2,1,0:T(8,128)(2,1)S(1)}, u32[]{:S(2)}, u32[]{:S(2)}) collective-permute-start(bf16[4,416,128]{2,1,0:T(8,128)(2,1)S(1)} %pad_maximum_fusion.w0), channel_id=1, source_target_pairs={{0,64},{16,80},{32,96},{48,112},{64,128},{80,144},{96,160},{112,17... | collective-permute-start | bytes 1277960 | tf_op jit(solution)/shard_map/ppermute | solution.py:368
  22.9 2.9 %collective-permute-start.8 = (bf16[4,416,128]{2,1,0:T(8,128)(2,1)S(1)}, bf16[4,416,128]{2,1,0:T(8,128)(2,1)S(1)}, u32[]{:S(2)}, u32[]{:S(2)}) collective-permute-start(bf16[4,416,128]{2,1,0:T(8,128)(2,1)S(1)} %pad_maximum_fusion.w0), channel_id=1, source_target_pairs={{0,192},{16,208},{32,224},{48,240},{64,0},{80,16},{96,32},{112,48}... | collective-permute-start | bytes 1277960 | tf_op jit(solution)/shard_map/ppermute | solution.py:369
  25.8 0.0 collective-permute-done.3
  25.9 0.0 copy-start
  25.9 0.6 collective-permute-start.4
  26.5 2.4 %collective-permute-start.5 = (bf16[2,816,128]{2,1,0:T(8,128)(2,1)S(1)}, bf16[2,816,128]{2,1,0:T(8,128)(2,1)S(1)}, u32[]{:S(2)}, u32[]{:S(2)}) collective-permute-start(bf16[2,816,128]{2,1,0:T(8,128)(2,1)S(1)} %pad_maximum_fusion.1.refs_0_), channel_id=1, source_target_pairs={{0,8},{1,9},{2,10},{3,11},{4,12},{5,13},{6,14},{7,15},{8,0},{9,1},... | collective-permute-start | bytes 1253384 | tf_op jit(solution)/shard_map/ppermute | solution.py:375
  28.9 0.0 collective-permute-start.6
  28.9 8.9 %collective-permute-done.7.w1 = bf16[4,416,128]{2,1,0:T(8,128)(2,1)S(1)} collective-permute-done((bf16[4,416,128]{2,1,0:T(8,128)(2,1)S(1)}, bf16[4,416,128]{2,1,0:T(8,128)(2,1)S(1)}, u32[]{:S(2)}, u32[]{:S(2)}) %collective-permute-start.7) | collective-permute-done | bytes 426016 | tf_op jit(solution)/shard_map/ppermute | solution.py:368
  37.8 6.8 %collective-permute-done.8.w2 = bf16[4,416,128]{2,1,0:T(8,128)(2,1)S(1)} collective-permute-done((bf16[4,416,128]{2,1,0:T(8,128)(2,1)S(1)}, bf16[4,416,128]{2,1,0:T(8,128)(2,1)S(1)}, u32[]{:S(2)}, u32[]{:S(2)}) %collective-permute-start.8) | collective-permute-done | bytes 426016 | tf_op jit(solution)/shard_map/ppermute | solution.py:369
  44.6 0.0 collective-permute-done.4.refs_1_
  44.6 0.0 collective-permute-done.5.refs_2_
  44.6 1.8 %collective-permute-done.6.refs_3_ = bf16[2,816,128]{2,1,0:T(8,128)(2,1)S(1)} collective-permute-done((bf16[2,816,128]{2,1,0:T(8,128)(2,1)S(1)}, bf16[2,816,128]{2,1,0:T(8,128)(2,1)S(1)}, u32[]{:S(2)}, u32[]{:S(2)}) %collective-permute-start.6) | collective-permute-done | bytes 417824 | tf_op jit(solution)/shard_map/ppermute | solution.py:375
  46.4 0.0 collective-permute-start.10
  46.5 0.5 collective-permute-start.11
  46.9 0.0 collective-permute-start.12
  47.0 0.5 collective-permute-start.9
  47.5 2.1 %collective-permute-start.16 = (bf16[2,416,128]{2,1,0:T(8,128)(2,1)S(1)}, bf16[2,416,128]{2,1,0:T(8,128)(2,1)}, u32[]{:S(2)}, u32[]{:S(2)}) collective-permute-start(bf16[2,416,128]{2,1,0:T(8,128)(2,1)S(1)} %slice.73), channel_id=1, source_target_pairs={{0,64},{16,80},{32,96},{48,112},{64,128},{80,144},{96,160},{112,17... | collective-permute-start | bytes 638984 | tf_op jit(solution)/shard_map/ppermute | solution.py:370
  49.6 0.7 slice.74
  50.3 0.0 collective-permute-done.10.refs_5_
  50.3 2.1 %collective-permute-start.17 = (bf16[2,416,128]{2,1,0:T(8,128)(2,1)}, bf16[2,416,128]{2,1,0:T(8,128)(2,1)}, u32[]{:S(2)}, u32[]{:S(2)}) collective-permute-start(bf16[2,416,128]{2,1,0:T(8,128)(2,1)} %slice.74), channel_id=1, source_target_pairs={{0,192},{16,208},{32,224},{48,240},{64,0},{80,16},{96,32},{112,48}... | collective-permute-start | bytes 638984 | tf_op jit(solution)/shard_map/ppermute | solution.py:370
  52.4 0.0 collective-permute-done.11.refs_6_
  52.4 2.7 %collective-permute-start.13 = (bf16[512,128]{1,0:T(8,128)(2,1)}, bf16[512,128]{1,0:T(8,128)(2,1)}, u32[]{:S(2)}, u32[]{:S(2)}) collective-permute-start(bf16[512,128]{1,0:T(8,128)(2,1)} %get-tuple-element.55), channel_id=1, source_target_pairs={{0,16},{16,0},{32,48},{48,32},{64,80},{80,64},{96,112},{112,96},{1... | collective-permute-start | bytes 393224 | tf_op jit(solution)/shard_map/ppermute | solution.py:372
  55.1 1.0 collective-permute-start.14
  56.2 1.5 collective-permute-start.15
  57.7 4.5 %latent_rows.1 = (bf16[1024,1536]{1,0:T(8,128)(2,1)}, bf16[1024,512]{1,0:T(8,128)(2,1)}, bf16[1024,64]{1,0:T(8,128)(2,1)}) custom-call(s32[4]{0:T(128)} %pad_add_fusion.pos, bf16[256,1536]{1,0:T(8,128)(2,1)} %ql.1, bf16[256,576]{1,0:T(8,128)(2,1)} %get-tuple-element.39.kl, bf16[2,816,128]{2,1,0:T(8,128)(2,1)} %copy-done, bf16[2,816,128]{2,1,0:T(8,128)(2,1)} %copy-done.3, ...), custom_call_target="tpu_custom_call" | custom-call | bytes 9000000 | tf_op jit(solution)/shard_map/latent_rows/pallas_call | solution.py:100
  62.2 0.0 collective-permute-done.13.og1
  62.2 4.4 %collective-permute-done.14.og2 = bf16[512,128]{1,0:T(8,128)(2,1)} collective-permute-done((bf16[512,128]{1,0:T(8,128)(2,1)}, bf16[512,128]{1,0:T(8,128)(2,1)}, u32[]{:S(2)}, u32[]{:S(2)}) %collective-permute-start.14) | collective-permute-done | bytes 131104 | tf_op jit(solution)/shard_map/ppermute | solution.py:372
  66.7 4.3 %collective-permute-done.15.og3 = bf16[512,128]{1,0:T(8,128)(2,1)} collective-permute-done((bf16[512,128]{1,0:T(8,128)(2,1)S(1)}, bf16[512,128]{1,0:T(8,128)(2,1)}, u32[]{:S(2)}, u32[]{:S(2)}) %collective-permute-start.15) | collective-permute-done | bytes 131104 | tf_op jit(solution)/shard_map/ppermute | solution.py:372
  70.9 0.0 collective-permute-done.17.w4
  71.0 14.9 %mla_backward.1 = (bf16[16,13,32,128]{3,2,1,0:T(8,128)(2,1)}, bf16[11520,128]{1,0:T(8,128)(2,1)}, bf16[768,384]{1,0:T(8,128)(2,1)}, bf16[384,512]{1,0:T(8,128)(2,1)}) custom-call(s32[4]{0:T(128)} %pad_add_fusion.pos, bf16[1024,1536]{1,0:T(8,128)(2,1)} %get-tuple-element.48.lq_in, bf16[1024,512]{1,0:T(8,128)(2,1)} %get-tuple-element.49.lk_in, ...), custom_call_target="tpu_custom_call" | custom-call | flops 4499999744 | bytes 12000000 | tf_op jit(solution)/shard_map/mla_backward/pallas_call | solution.py:100
  85.9 0.1 collective-permute-start.18
  86.0 5.5 %all-to-all-start = ((bf16[16,13,32,128]{3,2,1,0:T(8,128)(2,1)}), bf16[16,13,32,128]{3,2,1,0:T(8,128)(2,1)S(1)}, u32[]{:S(2)}, u32[]{:S(2)}) async-start(bf16[16,13,32,128]{3,2,1,0:T(8,128)(2,1)} %get-tuple-element.65), calls=%async_computation | async-start | bytes 3407872 | tf_op jit(solution)/shard_map/all_to_all | solution.py:392
  91.5 0.2 collective-permute-done.18.other.w_other
  91.7 7.1 %latent_grads.1 = (bf16[2,4,144,256]{3,2,1,0:T(8,128)(2,1)}, bf16[2,4,144,256]{3,2,1,0:T(8,128)(2,1)}, bf16[2,4,144,256]{3,2,1,0:T(8,128)(2,1)}, bf16[2,4,144,256]{3,2,1,0:T(8,128)(2,1)}) custom-call(s32[4]{0:T(128)} %pad_add_fusion.pos, bf16[11520,128]{1,0:T(8,128)(2,1)} %get-tuple-element.58.mine, ...), custom_call_target="tpu_custom_call" | custom-call | flops 1800000000 | bytes 12000000 | tf_op jit(solution)/shard_map/latent_grads/pallas_call | solution.py:294
  98.8 1.2 collective-permute-start.19
  99.9 1.9 %collective-permute-start.20 = (bf16[2,4,144,256]{3,2,1,0:T(8,128)(2,1)}, bf16[2,4,144,256]{3,2,1,0:T(8,128)(2,1)S(1)}, u32[]{:S(2)}, u32[]{:S(2)}) collective-permute-start(bf16[2,4,144,256]{3,2,1,0:T(8,128)(2,1)} %get-tuple-element.63), channel_id=1, source_target_pairs={{0,8},{1,9},{2,10},{3,11},{4,12},{5,13},{6,14},{7,15},{8,0},{9,1},... | collective-permute-start | bytes 1769480 | tf_op jit(solution)/shard_map/ppermute | solution.py:396
  101.8 0.1 collective-permute-start.21
  102.0 33.6 %all-to-all-done.terms = bf16[16,13,32,128]{3,2,1,0:T(8,128)(2,1)S(1)} async-done(((bf16[16,13,32,128]{3,2,1,0:T(8,128)(2,1)}), bf16[16,13,32,128]{3,2,1,0:T(8,128)(2,1)S(1)}, u32[]{:S(2)}, u32[]{:S(2)}) %all-to-all-start) | async-done | bytes 1703968 | tf_op jit(solution)/shard_map/all_to_all | solution.py:392
  135.6 1.0 block_strips.1
  136.6 4.3 %all-to-all-start.1 = ((bf16[16,4,32,128]{3,2,1,0:T(8,128)(2,1)}), bf16[16,4,32,128]{3,2,1,0:T(8,128)(2,1)S(1)}, u32[]{:S(2)}, u32[]{:S(2)}) async-start(bf16[16,4,32,128]{3,2,1,0:T(8,128)(2,1)} %block_strips.1), calls=%async_computation.1 | async-start | bytes 1048576 | tf_op jit(solution)/shard_map/all_to_all | solution.py:402
  140.9 0.0 collective-permute-done.19
  140.9 0.0 collective-permute-done.21
  140.9 1.3 convert_add_fusion
  142.3 1.8 %collective-permute-start.22 = (bf16[4,144,256]{2,1,0:T(8,128)(2,1)S(1)}, bf16[4,144,256]{2,1,0:T(8,128)(2,1)S(1)}, u32[]{:S(2)}, u32[]{:S(2)}) collective-permute-start(bf16[4,144,256]{2,1,0:T(8,128)(2,1)S(1)} %fusion.2), channel_id=1, source_target_pairs={{0,2},{1,3},{2,0},{3,1},{4,6},{5,7},{6,4},{7,5},{8,10},{9,11},{10,... | collective-permute-start | bytes 884744 | tf_op jit(solution)/shard_map/ppermute | solution.py:398
  144.1 10.2 %collective-permute-done.22 = bf16[4,144,256]{2,1,0:T(8,128)(2,1)S(1)} collective-permute-done((bf16[4,144,256]{2,1,0:T(8,128)(2,1)S(1)}, bf16[4,144,256]{2,1,0:T(8,128)(2,1)S(1)}, u32[]{:S(2)}, u32[]{:S(2)}) %collective-permute-start.22) | collective-permute-done | bytes 294944 | tf_op jit(solution)/shard_map/ppermute | solution.py:398
  154.3 0.1 fusion.1
  154.4 4.5 %collective-permute-start.23 = (bf16[144,256]{1,0:T(8,128)(2,1)S(1)}, bf16[144,256]{1,0:T(8,128)(2,1)S(1)}, u32[]{:S(2)}, u32[]{:S(2)}) collective-permute-start(bf16[144,256]{1,0:T(8,128)(2,1)S(1)} %get-tuple-element.75), channel_id=1, source_target_pairs={{0,16},{16,0},{32,48},{48,32},{64,80},{80,64},{96,112},{112,96},{1... | collective-permute-start | bytes 221192 | tf_op jit(solution)/shard_map/ppermute | solution.py:401
  158.9 1.5 collective-permute-start.24
  160.4 0.0 collective-permute-start.25
  160.5 4.5 %owner_grams.1 = (f32[512,512]{1,0:T(8,128)}, f32[512,512]{1,0:T(8,128)}, f32[512,512]{1,0:T(8,128)}) custom-call(bf16[16,4,32,128]{3,2,1,0:T(8,128)(2,1)S(1)} %all-to-all-done.1.strips), custom_call_target="tpu_custom_call" | custom-call | flops 3200000000 | bytes 4000000 | tf_op jit(solution)/shard_map/owner_grams/pallas_call | solution.py:100
  165.0 2.2 %collective-permute-done.25 = bf16[144,256]{1,0:T(8,128)(2,1)S(1)} collective-permute-done((bf16[144,256]{1,0:T(8,128)(2,1)S(1)}, bf16[144,256]{1,0:T(8,128)(2,1)S(1)}, u32[]{:S(2)}, u32[]{:S(2)}) %collective-permute-start.25) | collective-permute-done | bytes 73760 | tf_op jit(solution)/shard_map/ppermute | solution.py:401
  167.2 0.6 slice_bitcast_fusion.8
  167.9 0.6 slice_bitcast_fusion.9
  (45 shorter events, 0.3 us)
Async XLA Ops:
  4.6 14.9 %copy-start.12 = (bf16[416,128]{1,0:T(8,128)(2,1)S(1)}, bf16[416,128]{1,0:T(8,128)(2,1)}, u32[]{:S(2)}) copy-start(bf16[416,128]{1,0:T(8,128)(2,1)} %get-tuple-element.43) | copy-start | bytes 319492
  4.6 8.0 %collective-permute-start = (bf16[688,128]{1,0:T(8,128)(2,1)}, bf16[688,128]{1,0:T(8,128)(2,1)S(1)}, u32[]{:S(2)}, u32[]{:S(2)}) collective-permute-start(bf16[688,128]{1,0:T(8,128)(2,1)} %get-tuple-element.40), channel_id=1, source_target_pairs={{0,16},{16,0},{32,48},{48,32},{64,80},{80,64},{96,112},{112,96},{1... | collective-permute-start | bytes 528392 | tf_op jit(solution)/shard_map/ppermute | solution.py:366
  7.8 7.6 %collective-permute-start.1 = (bf16[688,128]{1,0:T(8,128)(2,1)}, bf16[688,128]{1,0:T(8,128)(2,1)S(1)}, u32[]{:S(2)}, u32[]{:S(2)}) collective-permute-start(bf16[688,128]{1,0:T(8,128)(2,1)} %get-tuple-element.41), channel_id=1, source_target_pairs={{0,32},{16,48},{32,0},{48,16},{64,96},{80,112},{96,64},{112,80},{1... | collective-permute-start | bytes 528392 | tf_op jit(solution)/shard_map/ppermute | solution.py:366
  9.8 8.3 %collective-permute-start.2 = (bf16[688,128]{1,0:T(8,128)(2,1)}, bf16[688,128]{1,0:T(8,128)(2,1)S(1)}, u32[]{:S(2)}, u32[]{:S(2)}) collective-permute-start(bf16[688,128]{1,0:T(8,128)(2,1)} %get-tuple-element.42), channel_id=1, source_target_pairs={{0,48},{16,32},{32,16},{48,0},{64,112},{80,96},{96,80},{112,64},{1... | collective-permute-start | bytes 528392 | tf_op jit(solution)/shard_map/ppermute | solution.py:366
  18.1 7.8 %collective-permute-start.3 = (bf16[816,128]{1,0:T(8,128)(2,1)S(1)}, bf16[816,128]{1,0:T(8,128)(2,1)S(1)}, u32[]{:S(2)}, u32[]{:S(2)}) collective-permute-start(bf16[816,128]{1,0:T(8,128)(2,1)S(1)} %get-tuple-element.78), channel_id=1, source_target_pairs={{0,2},{1,3},{2,0},{3,1},{4,6},{5,7},{6,4},{7,5},{8,10},{9,11},{10,... | collective-permute-start | bytes 626696 | tf_op jit(solution)/shard_map/ppermute | solution.py:374
  19.5 36.7 %copy-start.13 = (bf16[512,128]{1,0:T(8,128)(2,1)S(1)}, bf16[512,128]{1,0:T(8,128)(2,1)}, u32[]{:S(2)}) copy-start(bf16[512,128]{1,0:T(8,128)(2,1)} %get-tuple-element.57) | copy-start | bytes 393220
  19.5 42.7 %copy-start.2 = (bf16[4,416,128]{2,1,0:T(8,128)(2,1)}, bf16[4,416,128]{2,1,0:T(8,128)(2,1)S(1)}, u32[]{:S(2)}) copy-start(bf16[4,416,128]{2,1,0:T(8,128)(2,1)S(1)} %pad_maximum_fusion.w0) | copy-start | bytes 1277956
  19.5 18.2 %collective-permute-start.7 = (bf16[4,416,128]{2,1,0:T(8,128)(2,1)S(1)}, bf16[4,416,128]{2,1,0:T(8,128)(2,1)S(1)}, u32[]{:S(2)}, u32[]{:S(2)}) collective-permute-start(bf16[4,416,128]{2,1,0:T(8,128)(2,1)S(1)} %pad_maximum_fusion.w0), channel_id=1, source_target_pairs={{0,64},{16,80},{32,96},{48,112},{64,128},{80,144},{96,160},{112,17... | collective-permute-start | bytes 1277960 | tf_op jit(solution)/shard_map/ppermute | solution.py:368
  22.9 21.7 %collective-permute-start.8 = (bf16[4,416,128]{2,1,0:T(8,128)(2,1)S(1)}, bf16[4,416,128]{2,1,0:T(8,128)(2,1)S(1)}, u32[]{:S(2)}, u32[]{:S(2)}) collective-permute-start(bf16[4,416,128]{2,1,0:T(8,128)(2,1)S(1)} %pad_maximum_fusion.w0), channel_id=1, source_target_pairs={{0,192},{16,208},{32,224},{48,240},{64,0},{80,16},{96,32},{112,48}... | collective-permute-start | bytes 1277960 | tf_op jit(solution)/shard_map/ppermute | solution.py:369
  25.9 31.8 %copy-start = (bf16[2,816,128]{2,1,0:T(8,128)(2,1)}, bf16[2,816,128]{2,1,0:T(8,128)(2,1)S(1)}, u32[]{:S(2)}) copy-start(bf16[2,816,128]{2,1,0:T(8,128)(2,1)S(1)} %pad_maximum_fusion.1.refs_0_) | copy-start | bytes 1253380
  25.9 18.7 %collective-permute-start.4 = (bf16[2,816,128]{2,1,0:T(8,128)(2,1)S(1)}, bf16[2,816,128]{2,1,0:T(8,128)(2,1)S(1)}, u32[]{:S(2)}, u32[]{:S(2)}) collective-permute-start(bf16[2,816,128]{2,1,0:T(8,128)(2,1)S(1)} %pad_maximum_fusion.1.refs_0_), channel_id=1, source_target_pairs={{0,4},{1,5},{2,6},{3,7},{4,8},{5,9},{6,10},{7,11},{8,12},{9,13},{1... | collective-permute-start | bytes 1253384 | tf_op jit(solution)/shard_map/ppermute | solution.py:375
  26.5 18.1 %collective-permute-start.5 = (bf16[2,816,128]{2,1,0:T(8,128)(2,1)S(1)}, bf16[2,816,128]{2,1,0:T(8,128)(2,1)S(1)}, u32[]{:S(2)}, u32[]{:S(2)}) collective-permute-start(bf16[2,816,128]{2,1,0:T(8,128)(2,1)S(1)} %pad_maximum_fusion.1.refs_0_), channel_id=1, source_target_pairs={{0,8},{1,9},{2,10},{3,11},{4,12},{5,13},{6,14},{7,15},{8,0},{9,1},... | collective-permute-start | bytes 1253384 | tf_op jit(solution)/shard_map/ppermute | solution.py:375
  28.9 17.6 %collective-permute-start.6 = (bf16[2,816,128]{2,1,0:T(8,128)(2,1)S(1)}, bf16[2,816,128]{2,1,0:T(8,128)(2,1)S(1)}, u32[]{:S(2)}, u32[]{:S(2)}) collective-permute-start(bf16[2,816,128]{2,1,0:T(8,128)(2,1)S(1)} %pad_maximum_fusion.1.refs_0_), channel_id=1, source_target_pairs={{0,12},{1,13},{2,14},{3,15},{4,0},{5,1},{6,2},{7,3},{8,4},{9,5},{1... | collective-permute-start | bytes 1253384 | tf_op jit(solution)/shard_map/ppermute | solution.py:375
  37.8 18.4 %copy-start.10 = (bf16[4,416,128]{2,1,0:T(8,128)(2,1)}, bf16[4,416,128]{2,1,0:T(8,128)(2,1)S(1)}, u32[]{:S(2)}) copy-start(bf16[4,416,128]{2,1,0:T(8,128)(2,1)S(1)} %collective-permute-done.7.w1) | copy-start | bytes 1277956
  44.6 13.1 %copy-start.11 = (bf16[4,416,128]{2,1,0:T(8,128)(2,1)}, bf16[4,416,128]{2,1,0:T(8,128)(2,1)S(1)}, u32[]{:S(2)}) copy-start(bf16[4,416,128]{2,1,0:T(8,128)(2,1)S(1)} %collective-permute-done.8.w2) | copy-start | bytes 1277956
  44.6 13.1 %copy-start.3 = (bf16[2,816,128]{2,1,0:T(8,128)(2,1)}, bf16[2,816,128]{2,1,0:T(8,128)(2,1)S(1)}, u32[]{:S(2)}) copy-start(bf16[2,816,128]{2,1,0:T(8,128)(2,1)S(1)} %collective-permute-done.4.refs_1_) | copy-start | bytes 1253380
  44.6 13.1 %copy-start.4 = (bf16[2,816,128]{2,1,0:T(8,128)(2,1)}, bf16[2,816,128]{2,1,0:T(8,128)(2,1)S(1)}, u32[]{:S(2)}) copy-start(bf16[2,816,128]{2,1,0:T(8,128)(2,1)S(1)} %collective-permute-done.5.refs_2_) | copy-start | bytes 1253380
  46.4 11.3 %copy-start.5 = (bf16[2,816,128]{2,1,0:T(8,128)(2,1)}, bf16[2,816,128]{2,1,0:T(8,128)(2,1)S(1)}, u32[]{:S(2)}) copy-start(bf16[2,816,128]{2,1,0:T(8,128)(2,1)S(1)} %collective-permute-done.6.refs_3_) | copy-start | bytes 1253380
  46.4 3.8 %collective-permute-start.10 = (bf16[2,816,128]{2,1,0:T(8,128)(2,1)S(1)}, bf16[2,816,128]{2,1,0:T(8,128)(2,1)S(1)}, u32[]{:S(2)}, u32[]{:S(2)}) collective-permute-start(bf16[2,816,128]{2,1,0:T(8,128)(2,1)S(1)} %collective-permute-done.4.refs_1_), channel_id=1, source_target_pairs={{0,1},{1,0},{2,3},{3,2},{4,5},{5,4},{6,7},{7,6},{8,9},{9,8},{10,11... | collective-permute-start | bytes 1253384 | tf_op jit(solution)/shard_map/ppermute | solution.py:377
  46.5 5.9 %collective-permute-start.11 = (bf16[2,816,128]{2,1,0:T(8,128)(2,1)S(1)}, bf16[2,816,128]{2,1,0:T(8,128)(2,1)S(1)}, u32[]{:S(2)}, u32[]{:S(2)}) collective-permute-start(bf16[2,816,128]{2,1,0:T(8,128)(2,1)S(1)} %collective-permute-done.5.refs_2_), channel_id=1, source_target_pairs={{0,1},{1,0},{2,3},{3,2},{4,5},{5,4},{6,7},{7,6},{8,9},{9,8},{10,11... | collective-permute-start | bytes 1253384 | tf_op jit(solution)/shard_map/ppermute | solution.py:377
  46.9 8.2 %collective-permute-start.12 = (bf16[2,816,128]{2,1,0:T(8,128)(2,1)S(1)}, bf16[2,816,128]{2,1,0:T(8,128)(2,1)S(1)}, u32[]{:S(2)}, u32[]{:S(2)}) collective-permute-start(bf16[2,816,128]{2,1,0:T(8,128)(2,1)S(1)} %collective-permute-done.6.refs_3_), channel_id=1, source_target_pairs={{0,1},{1,0},{2,3},{3,2},{4,5},{5,4},{6,7},{7,6},{8,9},{9,8},{10,11... | collective-permute-start | bytes 1253384 | tf_op jit(solution)/shard_map/ppermute | solution.py:377
  47.0 9.2 %collective-permute-start.9 = (bf16[2,816,128]{2,1,0:T(8,128)(2,1)S(1)}, bf16[2,816,128]{2,1,0:T(8,128)(2,1)S(1)}, u32[]{:S(2)}, u32[]{:S(2)}) collective-permute-start(bf16[2,816,128]{2,1,0:T(8,128)(2,1)S(1)} %pad_maximum_fusion.1.refs_0_), channel_id=1, source_target_pairs={{0,1},{1,0},{2,3},{3,2},{4,5},{5,4},{6,7},{7,6},{8,9},{9,8},{10,11... | collective-permute-start | bytes 1253384 | tf_op jit(solution)/shard_map/ppermute | solution.py:377
  47.5 23.5 %collective-permute-start.16 = (bf16[2,416,128]{2,1,0:T(8,128)(2,1)S(1)}, bf16[2,416,128]{2,1,0:T(8,128)(2,1)}, u32[]{:S(2)}, u32[]{:S(2)}) collective-permute-start(bf16[2,416,128]{2,1,0:T(8,128)(2,1)S(1)} %slice.73), channel_id=1, source_target_pairs={{0,64},{16,80},{32,96},{48,112},{64,128},{80,144},{96,160},{112,17... | collective-permute-start | bytes 638984 | tf_op jit(solution)/shard_map/ppermute | solution.py:370
  50.3 7.4 %copy-start.6 = (bf16[2,816,128]{2,1,0:T(8,128)(2,1)}, bf16[2,816,128]{2,1,0:T(8,128)(2,1)S(1)}, u32[]{:S(2)}) copy-start(bf16[2,816,128]{2,1,0:T(8,128)(2,1)S(1)} %collective-permute-done.10.refs_5_) | copy-start | bytes 1253380
  50.3 20.7 %collective-permute-start.17 = (bf16[2,416,128]{2,1,0:T(8,128)(2,1)}, bf16[2,416,128]{2,1,0:T(8,128)(2,1)}, u32[]{:S(2)}, u32[]{:S(2)}) collective-permute-start(bf16[2,416,128]{2,1,0:T(8,128)(2,1)} %slice.74), channel_id=1, source_target_pairs={{0,192},{16,208},{32,224},{48,240},{64,0},{80,16},{96,32},{112,48}... | collective-permute-start | bytes 638984 | tf_op jit(solution)/shard_map/ppermute | solution.py:370
  52.4 5.3 %copy-start.7 = (bf16[2,816,128]{2,1,0:T(8,128)(2,1)}, bf16[2,816,128]{2,1,0:T(8,128)(2,1)S(1)}, u32[]{:S(2)}) copy-start(bf16[2,816,128]{2,1,0:T(8,128)(2,1)S(1)} %collective-permute-done.11.refs_6_) | copy-start | bytes 1253380
  52.4 9.8 %collective-permute-start.13 = (bf16[512,128]{1,0:T(8,128)(2,1)}, bf16[512,128]{1,0:T(8,128)(2,1)}, u32[]{:S(2)}, u32[]{:S(2)}) collective-permute-start(bf16[512,128]{1,0:T(8,128)(2,1)} %get-tuple-element.55), channel_id=1, source_target_pairs={{0,16},{16,0},{32,48},{48,32},{64,80},{80,64},{96,112},{112,96},{1... | collective-permute-start | bytes 393224 | tf_op jit(solution)/shard_map/ppermute | solution.py:372
  55.1 2.6 %copy-start.8 = (bf16[2,816,128]{2,1,0:T(8,128)(2,1)}, bf16[2,816,128]{2,1,0:T(8,128)(2,1)S(1)}, u32[]{:S(2)}) copy-start(bf16[2,816,128]{2,1,0:T(8,128)(2,1)S(1)} %collective-permute-done.12.refs_7_) | copy-start | bytes 1253380
  55.1 11.5 %collective-permute-start.14 = (bf16[512,128]{1,0:T(8,128)(2,1)}, bf16[512,128]{1,0:T(8,128)(2,1)}, u32[]{:S(2)}, u32[]{:S(2)}) collective-permute-start(bf16[512,128]{1,0:T(8,128)(2,1)} %get-tuple-element.56), channel_id=1, source_target_pairs={{0,32},{16,48},{32,0},{48,16},{64,96},{80,112},{96,64},{112,80},{1... | collective-permute-start | bytes 393224 | tf_op jit(solution)/shard_map/ppermute | solution.py:372
  56.2 1.6 copy-start.9
  56.2 14.8 %collective-permute-start.15 = (bf16[512,128]{1,0:T(8,128)(2,1)S(1)}, bf16[512,128]{1,0:T(8,128)(2,1)}, u32[]{:S(2)}, u32[]{:S(2)}) collective-permute-start(bf16[512,128]{1,0:T(8,128)(2,1)S(1)} %copy-done.13), channel_id=1, source_target_pairs={{0,48},{16,32},{32,16},{48,0},{64,112},{80,96},{96,80},{112,64},{1... | collective-permute-start | bytes 393224 | tf_op jit(solution)/shard_map/ppermute | solution.py:372
  85.9 5.8 %collective-permute-start.18 = (bf16[11520,128]{1,0:T(8,128)(2,1)}, bf16[11520,128]{1,0:T(8,128)(2,1)}, u32[]{:S(2)}, u32[]{:S(2)}) collective-permute-start(bf16[11520,128]{1,0:T(8,128)(2,1)} %get-tuple-element.58.mine), channel_id=1, source_target_pairs={{0,1},{1,0},{2,3},{3,2},{4,5},{5,4},{6,7},{7,6},{8,9},{9,8},{10,11... | collective-permute-start | bytes 8847368 | tf_op jit(solution)/shard_map/ppermute | solution.py:394
  86.0 49.6 %all-to-all-start = ((bf16[16,13,32,128]{3,2,1,0:T(8,128)(2,1)}), bf16[16,13,32,128]{3,2,1,0:T(8,128)(2,1)S(1)}, u32[]{:S(2)}, u32[]{:S(2)}) async-start(bf16[16,13,32,128]{3,2,1,0:T(8,128)(2,1)} %get-tuple-element.65), calls=%async_computation | async-start | bytes 3407872 | tf_op jit(solution)/shard_map/all_to_all | solution.py:392
  98.8 42.1 %collective-permute-start.19 = (bf16[2,4,144,256]{3,2,1,0:T(8,128)(2,1)}, bf16[2,4,144,256]{3,2,1,0:T(8,128)(2,1)S(1)}, u32[]{:S(2)}, u32[]{:S(2)}) collective-permute-start(bf16[2,4,144,256]{3,2,1,0:T(8,128)(2,1)} %get-tuple-element.62), channel_id=1, source_target_pairs={{0,4},{1,5},{2,6},{3,7},{4,8},{5,9},{6,10},{7,11},{8,12},{9,13},{1... | collective-permute-start | bytes 1769480 | tf_op jit(solution)/shard_map/ppermute | solution.py:396
  99.9 41.0 %collective-permute-start.20 = (bf16[2,4,144,256]{3,2,1,0:T(8,128)(2,1)}, bf16[2,4,144,256]{3,2,1,0:T(8,128)(2,1)S(1)}, u32[]{:S(2)}, u32[]{:S(2)}) collective-permute-start(bf16[2,4,144,256]{3,2,1,0:T(8,128)(2,1)} %get-tuple-element.63), channel_id=1, source_target_pairs={{0,8},{1,9},{2,10},{3,11},{4,12},{5,13},{6,14},{7,15},{8,0},{9,1},... | collective-permute-start | bytes 1769480 | tf_op jit(solution)/shard_map/ppermute | solution.py:396
  101.8 39.1 %copy-start.1 = (bf16[2,4,144,256]{3,2,1,0:T(8,128)(2,1)S(1)}, bf16[2,4,144,256]{3,2,1,0:T(8,128)(2,1)}, u32[]{:S(2)}) copy-start(bf16[2,4,144,256]{3,2,1,0:T(8,128)(2,1)} %get-tuple-element.61) | copy-start | bytes 1769476
  101.8 39.1 %collective-permute-start.21 = (bf16[2,4,144,256]{3,2,1,0:T(8,128)(2,1)}, bf16[2,4,144,256]{3,2,1,0:T(8,128)(2,1)}, u32[]{:S(2)}, u32[]{:S(2)}) collective-permute-start(bf16[2,4,144,256]{3,2,1,0:T(8,128)(2,1)} %get-tuple-element.64), channel_id=1, source_target_pairs={{0,12},{1,13},{2,14},{3,15},{4,0},{5,1},{6,2},{7,3},{8,4},{9,5},{1... | collective-permute-start | bytes 1769480 | tf_op jit(solution)/shard_map/ppermute | solution.py:396
  136.6 23.9 %all-to-all-start.1 = ((bf16[16,4,32,128]{3,2,1,0:T(8,128)(2,1)}), bf16[16,4,32,128]{3,2,1,0:T(8,128)(2,1)S(1)}, u32[]{:S(2)}, u32[]{:S(2)}) async-start(bf16[16,4,32,128]{3,2,1,0:T(8,128)(2,1)} %block_strips.1), calls=%async_computation.1 | async-start | bytes 1048576 | tf_op jit(solution)/shard_map/all_to_all | solution.py:402
  142.3 12.0 %collective-permute-start.22 = (bf16[4,144,256]{2,1,0:T(8,128)(2,1)S(1)}, bf16[4,144,256]{2,1,0:T(8,128)(2,1)S(1)}, u32[]{:S(2)}, u32[]{:S(2)}) collective-permute-start(bf16[4,144,256]{2,1,0:T(8,128)(2,1)S(1)} %fusion.2), channel_id=1, source_target_pairs={{0,2},{1,3},{2,0},{3,1},{4,6},{5,7},{6,4},{7,5},{8,10},{9,11},{10,... | collective-permute-start | bytes 884744 | tf_op jit(solution)/shard_map/ppermute | solution.py:398
  154.4 10.6 %collective-permute-start.23 = (bf16[144,256]{1,0:T(8,128)(2,1)S(1)}, bf16[144,256]{1,0:T(8,128)(2,1)S(1)}, u32[]{:S(2)}, u32[]{:S(2)}) collective-permute-start(bf16[144,256]{1,0:T(8,128)(2,1)S(1)} %get-tuple-element.75), channel_id=1, source_target_pairs={{0,16},{16,0},{32,48},{48,32},{64,80},{80,64},{96,112},{112,96},{1... | collective-permute-start | bytes 221192 | tf_op jit(solution)/shard_map/ppermute | solution.py:401
  158.9 6.1 %collective-permute-start.24 = (bf16[144,256]{1,0:T(8,128)(2,1)S(1)}, bf16[144,256]{1,0:T(8,128)(2,1)S(1)}, u32[]{:S(2)}, u32[]{:S(2)}) collective-permute-start(bf16[144,256]{1,0:T(8,128)(2,1)S(1)} %get-tuple-element.74), channel_id=1, source_target_pairs={{0,32},{16,48},{32,0},{48,16},{64,96},{80,112},{96,64},{112,80},{1... | collective-permute-start | bytes 221192 | tf_op jit(solution)/shard_map/ppermute | solution.py:401
  160.4 6.8 %collective-permute-start.25 = (bf16[144,256]{1,0:T(8,128)(2,1)S(1)}, bf16[144,256]{1,0:T(8,128)(2,1)S(1)}, u32[]{:S(2)}, u32[]{:S(2)}) collective-permute-start(bf16[144,256]{1,0:T(8,128)(2,1)S(1)} %get-tuple-element.73), channel_id=1, source_target_pairs={{0,48},{16,32},{32,16},{48,0},{64,112},{80,96},{96,80},{112,64},{1... | collective-permute-start | bytes 221192 | tf_op jit(solution)/shard_map/ppermute | solution.py:401

commit v3 on v2

--- a/solution.py
+++ b/solution.py
@@ -109,31 +109,19 @@
     )(*args)
 
 
-def main_kernel(
-    pos, lq_in, lk_in, rope_in, og0, og1, og2, og3, w0, w1, w2, w3, w4, out, given_out, wq_out, wkv_out,
-    lq, lk, rope, og, wq3, wkv3, dq, dkv, drope, term, wq2, wkv2, w, row_sems, sems,
+def project_kernel(
+    pos, lq_in, lk_in, w0, w1, w2, w3, w4, query_out, keyval_out, wq_out, wkv_out, given_out,
+    lq, lk, w, wq3, wkv3, query, keyval, wq2, wkv2, sems,
 ):
     core, member, group = pos[0], pos[2], pos[3]
-    starts, at = [], 0
+    copies, at = [], 0
     for i, piece in enumerate((w0, w1, w2, w3, w4)):
-        starts.append(pltpu.make_async_copy(piece, w.at[pl.ds(at, piece.shape[0])], sems.at[i]))
+        copies.append(pltpu.make_async_copy(piece, w.at[pl.ds(at, piece.shape[0])], sems.at[i]))
         at += piece.shape[0]
-    for copy in starts:
+    rows_in = [pltpu.make_async_copy(lk_in, lk, sems.at[5]), pltpu.make_async_copy(lq_in, lq, sems.at[6])]
+    for copy in copies + rows_in:
         copy.start()
-
-    def row_copies(s):
-        part = pl.ds(256 * s, 256)
-        pairs = [(lq_in, lq), (lk_in, lk), (rope_in, rope)]
-        copies = [pltpu.make_async_copy(x.at[part], y.at[part], row_sems.at[s, i]) for i, (x, y) in enumerate(pairs)]
-        return copies + [pltpu.make_async_copy((og0, og1, og2, og3)[s], og.at[s], row_sems.at[s, 3])]
-
-    rows_in = [row_copies(s) for s in range(4)]
-    for copies in rows_in:
-        for copy in copies:
-            copy.start()
-    for copy in starts:
-        copy.wait()
-    for copy in rows_in[0]:
+    for copy in copies:
         copy.wait()
     for j, a in enumerate((0, 3, 1, 2)):
         for i in range(4):
@@ -143,6 +131,12 @@
             for t in range(4):
                 wkv3[d, :, 128 * t : 128 * t + 128] = w[4 * j + i, 288 + 32 * t : 320 + 32 * t, :]
     wq, wkv = wq3[...].reshape(1536, 384), wkv3[...].reshape(512, 512)
+    rows_in[0].wait()
+    keyval[...] = dot(lk[...], wkv, 1, 0).astype(BF16)
+    ends = [pltpu.make_async_copy(keyval, keyval_out, sems.at[7])]
+    ends[0].start()
+    rows_in[1].wait()
+    query[...] = dot(lq[...], wq, 1, 0).astype(BF16)
     wide = wkv.astype(F32)
     for h in range(16):
         side = (h % 2) ^ core
@@ -152,44 +146,88 @@
         if own:
             piece = jnp.concatenate([wide[36 * h : 36 * h + own, :], piece[own:]], axis=0)
         wkv2[side, 48 * (h // 2) : 48 * (h // 2) + 48, :] = piece.astype(BF16)
-    ends = [
-        pltpu.make_async_copy(wq2.at[0], wq_out, sems.at[7]),
-        pltpu.make_async_copy(wkv2.at[0], wkv_out, sems.at[8]),
-    ]
-    for i, (source, to, tiles) in enumerate(((wq2.at[1], 7680, 3), (wkv2.at[1], 9984, 4))):
+    last = [(query, query_out), (wq2.at[0], wq_out), (wkv2.at[0], wkv_out)]
+    for source, to, tiles in ((wq2.at[1], 0, 3), (wkv2.at[1], 2304, 4)):
         size = source.shape[0]
         for t in range(tiles):
-            part = given_out.at[pl.ds(to + size * t, size)]
-            ends.append(pltpu.make_async_copy(source.at[:, pl.ds(128 * t, 128)], part, sems.at[16 + 4 * i + t]))
+            last.append((source.at[:, pl.ds(128 * t, 128)], given_out.at[pl.ds(to + size * t, size)]))
+    for i, (source, to) in enumerate(last):
+        ends.append(pltpu.make_async_copy(source, to, sems.at[8 + i]))
+        ends[-1].start()
     for copy in ends:
+        copy.wait()
+
+
+def project_call(*args):
+    shape = jax.ShapeDtypeStruct
+    hbm = pl.BlockSpec(memory_space=pltpu.HBM)
+    shapes = [(1024, 384), (1024, 512), (768, 384), (384, 512), (3840, 128)]
+    return call(
+        project_kernel,
+        "projections",
+        [shape(x, BF16) for x in shapes],
+        WHOLE,
+        args,
+        scratch=[
+            pltpu.VMEM((1024, 1536), BF16),
+            pltpu.VMEM((1024, 512), BF16),
+            pltpu.VMEM((16, 416, 128), BF16),
+            pltpu.VMEM((16, 96, 384), BF16),
+            pltpu.VMEM((16, 32, 512), BF16),
+            pltpu.VMEM((1024, 384), BF16),
+            pltpu.VMEM((1024, 512), BF16),
+            pltpu.VMEM((2, 768, 384), BF16),
+            pltpu.VMEM((2, 384, 512), BF16),
+            pltpu.SemaphoreType.DMA((18,)),
+        ],
+        in_specs=[pl.BlockSpec(memory_space=pltpu.SMEM)] + [hbm] * 7,
+        out_specs=[hbm] * 5,
+        flops=1_800_000_000,
+        size=12_000_000,
+    )
+
+
+def main_kernel(
+    lq_in, lk_in, rope_in, og0, og1, og2, og3, query_in, keyval_in, out, given_out,
+    lq, lk, rope, og, dq, dkv, drope, term, row_sems, sems,
+):
+    whole = [pltpu.make_async_copy(lk_in, lk, sems.at[0]), pltpu.make_async_copy(lq_in, lq, sems.at[1])]
+    rows_in = []
+    for s, grad in enumerate((og0, og1, og2, og3)):
+        rows = pl.ds(256 * s, 256)
+        pairs = [(x.at[rows], y.at[rows]) for x, y in ((query_in, dq), (keyval_in, dkv), (rope_in, rope))]
+        pairs.append((grad, og.at[s]))
+        rows_in.append([pltpu.make_async_copy(x, y, row_sems.at[s, i]) for i, (x, y) in enumerate(pairs)])
+        for copy in rows_in[s]:
+            copy.start()
+    for copy in whole:
         copy.start()
 
-    causal = lax.broadcasted_iota(jnp.int32, (256, 256), 0) >= lax.broadcasted_iota(jnp.int32, (256, 256), 1)
-
+    causal = lax.broadcasted_iota(jnp.int32, (256, 256), 0) <= lax.broadcasted_iota(jnp.int32, (256, 256), 1)
+    ends = []
     for s in range(4):
-        if s:
-            for copy in rows_in[s]:
-                copy.wait()
         rows = pl.ds(256 * s, 256)
-        query = dot(lq[rows, :], wq, 1, 0)
-        keyval = dot(lk[rows, :], wkv, 1, 0).astype(BF16)
-        rope_key = rope[rows, :]
+        for copy in rows_in[s]:
+            copy.wait()
+        query, keyval, rope_key = dq[rows, :], dkv[rows, :], rope[rows, :]
         rope_sum = jnp.zeros((256, ROPE), F32)
         dq_parts = []
         for h in range(2):
-            q_h = query[:, QK * h : QK * h + QK].astype(BF16)
+            q_h = query[:, QK * h : QK * h + QK]
             key = jnp.concatenate([keyval[:, 256 * h : 256 * h + 128], rope_key], axis=1)
             value = keyval[:, 256 * h + 128 : 256 * h + 256]
             grad = og[s, 256 * h : 256 * h + 256, :]
-            weights = jnp.where(causal, jnp.exp2(dot(q_h, key, 1, 1) * (SCALE * LOG2E)), 0.0)
-            weights = weights / jnp.sum(weights, axis=1, keepdims=True)
+            weights = jnp.where(causal, jnp.exp2(dot(key, q_h, 1, 1) * (SCALE * LOG2E)), 0.0)
+            total = jnp.sum(weights, axis=0, keepdims=True)
+            shrink = jnp.where(total > 2.0**100, 2.0**-100, 1.0)
+            weights = (weights * shrink) * (1.0 / (total * shrink))
             probs = weights.astype(BF16)
-            dprob = dot(grad, value, 1, 1)
-            delta = jnp.sum(probs.astype(F32) * dprob, axis=1, keepdims=True)
+            dprob = dot(value, grad, 1, 1)
+            delta = jnp.sum(probs.astype(F32) * dprob, axis=0, keepdims=True)
             dscore = (weights * (dprob - delta) * SCALE).astype(BF16)
-            dvalue = dot(probs, grad, 0, 0).astype(BF16)
-            dq_parts.append(dot(dscore, key, 1, 0))
-            dkey = dot(dscore, q_h, 0, 0)
+            dvalue = dot(probs, grad, 1, 0).astype(BF16)
+            dkey = dot(dscore, q_h, 1, 0)
+            dq_parts.append(dot(dscore, key, 0, 0))
             dkv[rows, 256 * h : 256 * h + 128] = dkey[:, :NOPE].astype(BF16)
             dkv[rows, 256 * h + 128 : 256 * h + 256] = dvalue
             rope_sum = rope_sum + dkey[:, NOPE:].astype(BF16).astype(F32)
@@ -204,6 +242,8 @@
                 ends[-1].start()
                 to += size
 
+    for copy in whole:
+        copy.wait()
     for block in (3, 0, 1, 2):
         if block == 3:
             value = dot(lk[...], dkv[...], 0, 0).astype(BF16)
@@ -226,12 +266,7 @@
     return call(
         main_kernel,
         "mla_backward",
-        (
-            shape((16, 13, 32, 128), BF16),
-            shape((11520, 128), BF16),
-            shape((768, 384), BF16),
-            shape((384, 512), BF16),
-        ),
+        [shape((16, 13, 32, 128), BF16), shape((7680, 128), BF16)],
         WHOLE,
         args,
         scratch=[
@@ -239,21 +274,16 @@
             pltpu.VMEM((1024, 512), BF16),
             pltpu.VMEM((1024, ROPE), BF16),
             pltpu.VMEM((4, 512, 128), BF16),
-            pltpu.VMEM((16, 96, 384), BF16),
-            pltpu.VMEM((16, 32, 512), BF16),
             pltpu.VMEM((1024, 384), BF16),
             pltpu.VMEM((1024, 512), BF16),
             pltpu.VMEM((ROPE, 1024), BF16),
             pltpu.VMEM((16, 13, 32, 128), BF16),
-            pltpu.VMEM((2, 768, 384), BF16),
-            pltpu.VMEM((2, 384, 512), BF16),
-            pltpu.VMEM((16, 416, 128), BF16),
             pltpu.SemaphoreType.DMA((4, 4)),
             pltpu.SemaphoreType.DMA((64,)),
         ],
-        in_specs=[pl.BlockSpec(memory_space=pltpu.SMEM)] + [hbm] * 12,
-        out_specs=[hbm] * 4,
-        flops=4_500_000_000,
+        in_specs=[hbm] * 9,
+        out_specs=[hbm] * 2,
+        flops=2_700_000_000,
         size=12_000_000,
     )
 
@@ -274,34 +304,44 @@
     last = kv_term[336:384] + jnp.where(core == 0, on_0, on_1)
     q_term = q_term.astype(BF16)
     kv_term = jnp.concatenate([kv_term[:336], last], axis=0).astype(BF16)
+    along_x, (keep, give) = outs[:4], outs[4:]
     for x in range(4):
         for y in range(2):
             h = 2 * x + y
             to_x, to_y = (x - chip // 2 + 4) % 4, y ^ (chip % 2)
+            q_piece, kv_piece = q_term[96 * h : 96 * h + 96, :], kv_term[48 * h : 48 * h + 48, :]
             for k in range(4):
 
-                @pl.when(to_x == k)
+                @pl.when((pl.program_id(0) < 2) & (to_x == k))
                 def _():
-                    outs[k][to_y, 0, 0:96, :] = q_term[96 * h : 96 * h + 96, :]
-                    outs[k][to_y, 0, 96:144, :] = kv_term[48 * h : 48 * h + 48, :]
-
-
-def latent_grad_call(pos, mine, other, wq, wkv):
+                    along_x[k][to_y, 0, 0:96, :] = q_piece
+                    along_x[k][to_y, 0, 96:144, :] = kv_piece
+
+            for k, out in enumerate((keep, give)):
+
+                @pl.when((pl.program_id(0) >= 2) & (to_y == k))
+                def _():
+                    out[to_x, 0, 0:96, :] = q_piece
+                    out[to_x, 0, 96:144, :] = kv_piece
+
+
+def latent_grad_call(pos, mine, other, w_other, wq, wkv):
     def whole(x):
         return pl.BlockSpec(x.shape, lambda s: (0, 0))
 
     sequence = pl.BlockSpec((1920, 128), lambda s: (s, 0))
     return pl.pallas_call(
         latent_grad_kernel,
-        out_shape=[jax.ShapeDtypeStruct((2, 4, 144, 256), BF16)] * 4,
+        out_shape=[jax.ShapeDtypeStruct((2, 2, 144, 256), BF16)] * 4 + [jax.ShapeDtypeStruct((4, 2, 144, 256), BF16)] * 2,
         grid=(4,),
         in_specs=[pl.BlockSpec(memory_space=pltpu.SMEM)]
-        + [sequence, sequence, pl.BlockSpec((3840, 128), lambda s: (2, 0)), whole(wq), whole(wkv)],
-        out_specs=[pl.BlockSpec((2, 1, 144, 256), lambda s: (0, s, 0, 0))] * 4,
+        + [sequence, sequence, whole(w_other), whole(wq), whole(wkv)],
+        out_specs=[pl.BlockSpec((2, 1, 144, 256), lambda s: (0, jnp.minimum(s, 1), 0, 0))] * 4
+        + [pl.BlockSpec((4, 1, 144, 256), lambda s: (0, jnp.maximum(s - 2, 0), 0, 0))] * 2,
         compiler_params=pltpu.CompilerParams(vmem_limit_bytes=WHOLE * 1024 * 1024),
         cost_estimate=pl.CostEstimate(flops=1_800_000_000, bytes_accessed=12_000_000, transcendentals=0),
         name="latent_grads",
-    )(pos, mine, other, other, wq, wkv)
+    )(pos, mine, other, w_other, wq, wkv)
 
 
 def strip_kernel(terms, strips):
@@ -319,14 +359,16 @@
                 strips[block, u] = jnp.zeros((32, 128), BF16)
 
 
-def gram_kernel(strips, grad, left, right):
-    for d in range(16):
-        for u in range(4):
-            grad[32 * d : 32 * d + 32, 128 * u : 128 * u + 128] = strips[d, u].astype(F32)
-    g = grad[...]
-    highest = lax.Precision.HIGHEST
-    left[...] = lax.dot_general(g, g, (((1,), (1,)), ((), ())), precision=highest, preferred_element_type=F32)
-    right[...] = lax.dot_general(g, g, (((0,), (0,)), ((), ())), precision=highest, preferred_element_type=F32)
+def gram_kernel(strips, grad_out, left_out, right_out, grad, left, right, sems):
+    rows = [jnp.concatenate([strips[d, u] for u in range(4)], axis=1) for d in range(16)]
+    g = jnp.concatenate(rows, axis=0)
+    copies = []
+    for i, (value, out) in enumerate(((grad, grad_out), (left, left_out), (right, right_out))):
+        value[...] = g.astype(F32) if i == 0 else dot(g, g, 2 - i, 2 - i)
+        copies.append(pltpu.make_async_copy(value, out, sems.at[i]))
+        copies[-1].start()
+    for copy in copies:
+        copy.wait()
 
 
 PARTNER = [[(i, i ^ s) for i in range(16)] for s in range(4)]
@@ -388,23 +430,37 @@
         size=9_000_000,
         scalars=True,
     )
-    terms, mine, wq, wkv = main_call(pos, lq, lk, rope, *ogs, w, from_down, from_up, *far)
+    query, keyval, wq, wkv, w_given = project_call(pos, lq, lk, w, from_down, from_up, *far)
+    w_other = lax.ppermute(w_given, "head", OTHER_CORE)
+    terms, mine = main_call(lq, lk, rope, *ogs, query, keyval)
     terms = lax.all_to_all(terms, "dp", 0, 0, tiled=True)
 
     other = lax.ppermute(mine, "head", OTHER_CORE)
-    parts = latent_grad_call(pos, mine, other, wq, wkv)
+    *parts, keep, give = latent_grad_call(pos, mine, other, w_other, wq, wkv)
+    given = lax.ppermute(give, "head", ACROSS_Y)
     parts = [parts[0]] + [lax.ppermute(parts[k], "head", ALONG_X[k]) for k in (1, 2, 3)]
-    part = sum(p.astype(F32) for p in parts)
-    across = lax.ppermute(part[1].astype(BF16), "head", ACROSS_Y)
+    first = sum(p.astype(F32) for p in parts)
+    first = first[0] + lax.ppermute(first[1].astype(BF16), "head", ACROSS_Y).astype(F32)
+    parts = [(keep[k].astype(F32) + given[k].astype(F32)).astype(BF16) for k in range(4)]
+    parts = [parts[0]] + [lax.ppermute(parts[k], "head", ALONG_X[k]) for k in (1, 2, 3)]
+    second = sum(p.astype(F32) for p in parts)
+    part = jnp.concatenate([first, second], axis=0).astype(BF16)
+    parts = [part[0]] + [lax.ppermute(part[s], "dp", PARTNER[s]) for s in (1, 2, 3)]
     (strips,) = call(strip_kernel, "block_strips", (shape((16, 4, 32, 128), BF16),), 8, (terms,), size=3_000_000)
-    part = (part[0] + across.astype(F32)).astype(BF16)
-    parts = [part[0]] + [lax.ppermute(part[s], "dp", PARTNER[s]) for s in (1, 2, 3)]
     strips = lax.all_to_all(strips, "dp", 0, 0, tiled=True)
     block = shape((BLK, BLK), F32)
     owned, left, right = call(
-        gram_kernel, "owner_grams", (block, block, block), 16, (strips,), flops=3_200_000_000, size=4_000_000
-    )
-    parts, _ = lax.optimization_barrier((parts, left))
+        gram_kernel,
+        "owner_grams",
+        (block, block, block),
+        16,
+        (strips,),
+        scratch=[pltpu.VMEM((BLK, BLK), F32)] * 3 + [pltpu.SemaphoreType.DMA((3,))],
+        out_specs=[hbm] * 3,
+        flops=540_000_000,
+        size=4_000_000,
+    )
+    *parts, left = lax.optimization_barrier((*parts, left))
     part = sum(p.astype(F32) for p in parts)
     d_q = part[:96].T.astype(BF16)
     d_kv = part[96:132].T.astype(BF16)

time: 170 us -> 161 us (0.947)
  waiting for transfers between devices: 80.8 us -> 64.4 us
  starting transfers between devices: 47.2 us -> 53.8 us
  other arithmetic: 2.23 us -> 3.96 us
    all_to_all x1, waiting for transfers between devices: 33.6 us -> 6.32 us  [per_device(): terms = lax.all_to_all(terms, 'dp', 0, 0, tiled=True)]
    ppermute x3 -> x6, waiting for transfers between devices: 0.01 us -> 19 us  [per_device(): lax.ppermute(parts[k], 'head', ALONG_X[k])]
    ppermute x3, waiting for transfers between devices: 8.7 us -> 0.01 us  [per_device(): lax.ppermute(ogs[s - 1], 'dp', PARTNER[s])]
    ppermute x1, waiting for transfers between devices: 6.81 us -> 12.8 us  [per_device(): from_up = lax.ppermute(w, 'dp', GROUP_DOWN)]
    ppermute x1, waiting for transfers between devices: 8.87 us -> 3.83 us  [per_device(): from_down = lax.ppermute(w, 'dp', GROUP_UP)]
    ppermute x3 -> x6, starting transfers between devices: 3.19 us -> 7.78 us  [per_device(): lax.ppermute(parts[k], 'head', ALONG_X[k])]
    ppermute x1, waiting for transfers between devices: 0.01 us -> 4.25 us  [per_device(): lax.ppermute(from_down[:2], 'dp', GROUP_UP)]
    ppermute x1, starting transfers between devices: 3.35 us -> 0.01 us  [per_device(): from_down = lax.ppermute(w, 'dp', GROUP_UP)]
  transfers between devices with their start and end apart: 28 -> 33, of which waited for: 12 -> 14; matrix products, arithmetic and copies ran while one was open for 1% -> 3% of each run, Pallas kernels for 10% -> 14%
where the time goes in v3:
time: 161 us
  waiting for transfers between devices  64.4 us (40%)
  starting transfers between devices  53.8 us (33%)
  Pallas kernels  34.3 us (21%)
  other arithmetic  3.96 us (2%)
  local copies, waits for them, and re-layouts  3.11 us (2%)
    pallas_call x6, Pallas kernels, call(): pl.pallas_call(kernel, out_shape=out_shape, in_specs=specs if in_specs is...  26.8 us
    ppermute x6, waiting for transfers between devices, per_device(): lax.ppermute(parts[k], 'head', ALONG_X[k])  19 us
    ppermute x1, waiting for transfers between devices, per_device(): from_up = lax.ppermute(w, 'dp', GROUP_DOWN)  12.8 us
    ppermute x3, starting transfers between devices, per_device(): lax.ppermute(part[s], 'dp', PARTNER[s])  8.49 us
    ppermute x3, waiting for transfers between devices, per_device(): parts = [lax.ppermute(sends[s - 1], 'dp', PARTNER[s]) for s in (1, 2, 3)]  8.23 us
    ppermute x6, starting transfers between devices, per_device(): lax.ppermute(parts[k], 'head', ALONG_X[k])  7.78 us
    pallas_call x1, Pallas kernels, latent_grad_call(): pl.pallas_call(latent_grad_kernel, out_shape=[jax.ShapeDtypeStruct((2, 2,...  7.47 us
    all_to_all x1, waiting for transfers between devices, per_device(): terms = lax.all_to_all(terms, 'dp', 0, 0, tiled=True)  6.32 us
  transfers between devices with their start and end apart: 33, of which 14 were waited for; matrix products, arithmetic and copies ran while one was open for 3% of the time, Pallas kernels for 14%

profile of v3, /device:TPU:6, one launch (start us, length us, event | category | flops | bytes accessed | tf_op | source)
XLA Modules:
  0.0 160.5 jit_solution(10803654523778723707)
XLA Ops:
  0.7 0.7 pad_add_fusion.pos
  1.3 3.2 %send_rows.1 = (bf16[688,128]{1,0:T(8,128)(2,1)}, bf16[688,128]{1,0:T(8,128)(2,1)}, bf16[688,128]{1,0:T(8,128)(2,1)}, bf16[416,128]{1,0:T(8,128)(2,1)}, bf16[512...) custom-call(s32[4]{0:T(128)} %pad_add_fusion.pos, ...), custom_call_target="tpu_custom_call" | custom-call | bytes 4000000 | tf_op jit(solution)/shard_map/send_rows/pallas_call | solution.py:100
  4.6 3.3 %collective-permute-start = (bf16[688,128]{1,0:T(8,128)(2,1)}, bf16[688,128]{1,0:T(8,128)(2,1)S(1)}, u32[]{:S(2)}, u32[]{:S(2)}) collective-permute-start(bf16[688,128]{1,0:T(8,128)(2,1)} %get-tuple-element.46), channel_id=1, source_target_pairs={{0,16},{16,0},{32,48},{48,32},{64,80},{80,64},{96,112},{112,96},{1... | collective-permute-start | bytes 528392 | tf_op jit(solution)/shard_map/ppermute | solution.py:408
  7.8 1.9 %collective-permute-start.1 = (bf16[688,128]{1,0:T(8,128)(2,1)}, bf16[688,128]{1,0:T(8,128)(2,1)S(1)}, u32[]{:S(2)}, u32[]{:S(2)}) collective-permute-start(bf16[688,128]{1,0:T(8,128)(2,1)} %get-tuple-element.47), channel_id=1, source_target_pairs={{0,32},{16,48},{32,0},{48,16},{64,96},{80,112},{96,64},{112,80},{1... | collective-permute-start | bytes 528392 | tf_op jit(solution)/shard_map/ppermute | solution.py:408
  9.8 2.8 %collective-permute-done = bf16[688,128]{1,0:T(8,128)(2,1)S(1)} collective-permute-done((bf16[688,128]{1,0:T(8,128)(2,1)}, bf16[688,128]{1,0:T(8,128)(2,1)S(1)}, u32[]{:S(2)}, u32[]{:S(2)}) %collective-permute-start) | collective-permute-done | bytes 176160 | tf_op jit(solution)/shard_map/ppermute | solution.py:408
  12.6 2.8 %collective-permute-done.1 = bf16[688,128]{1,0:T(8,128)(2,1)S(1)} collective-permute-done((bf16[688,128]{1,0:T(8,128)(2,1)}, bf16[688,128]{1,0:T(8,128)(2,1)S(1)}, u32[]{:S(2)}, u32[]{:S(2)}) %collective-permute-start.1) | collective-permute-done | bytes 176160 | tf_op jit(solution)/shard_map/ppermute | solution.py:408
  15.4 2.6 %collective-permute-done.2 = bf16[688,128]{1,0:T(8,128)(2,1)S(1)} collective-permute-done((bf16[688,128]{1,0:T(8,128)(2,1)}, bf16[688,128]{1,0:T(8,128)(2,1)S(1)}, u32[]{:S(2)}, u32[]{:S(2)}) %collective-permute-start.2) | collective-permute-done | bytes 176160 | tf_op jit(solution)/shard_map/ppermute | solution.py:408
  18.0 1.3 collective-permute-start.3
  19.4 1.0 pad_maximum_fusion.w0
  20.4 6.2 %collective-permute-start.8 = (bf16[4,416,128]{2,1,0:T(8,128)(2,1)S(1)}, bf16[4,416,128]{2,1,0:T(8,128)(2,1)S(1)}, u32[]{:S(2)}, u32[]{:S(2)}) collective-permute-start(bf16[4,416,128]{2,1,0:T(8,128)(2,1)S(1)} %pad_maximum_fusion.w0), channel_id=1, source_target_pairs={{0,192},{16,208},{32,224},{48,240},{64,0},{80,16},{96,32},{112,48}... | collective-permute-start | bytes 1277960 | tf_op jit(solution)/shard_map/ppermute | solution.py:411
  26.7 0.0 copy-start
  26.7 0.9 collective-permute-start.6
  27.6 1.1 collective-permute-start.5
  28.7 2.1 %collective-permute-start.4 = (bf16[2,816,128]{2,1,0:T(8,128)(2,1)S(1)}, bf16[2,816,128]{2,1,0:T(8,128)(2,1)S(1)}, u32[]{:S(2)}, u32[]{:S(2)}) collective-permute-start(bf16[2,816,128]{2,1,0:T(8,128)(2,1)S(1)} %pad_maximum_fusion.1.refs_0_), channel_id=1, source_target_pairs={{0,4},{1,5},{2,6},{3,7},{4,8},{5,9},{6,10},{7,11},{8,12},{9,13},{1... | collective-permute-start | bytes 1253384 | tf_op jit(solution)/shard_map/ppermute | solution.py:417
  30.8 12.8 %collective-permute-done.8.w2 = bf16[4,416,128]{2,1,0:T(8,128)(2,1)S(1)} collective-permute-done((bf16[4,416,128]{2,1,0:T(8,128)(2,1)S(1)}, bf16[4,416,128]{2,1,0:T(8,128)(2,1)S(1)}, u32[]{:S(2)}, u32[]{:S(2)}) %collective-permute-start.8) | collective-permute-done | bytes 426016 | tf_op jit(solution)/shard_map/ppermute | solution.py:411
  43.5 3.8 %collective-permute-done.7.w1 = bf16[4,416,128]{2,1,0:T(8,128)(2,1)S(1)} collective-permute-done((bf16[4,416,128]{2,1,0:T(8,128)(2,1)S(1)}, bf16[4,416,128]{2,1,0:T(8,128)(2,1)S(1)}, u32[]{:S(2)}, u32[]{:S(2)}) %collective-permute-start.7) | collective-permute-done | bytes 426016 | tf_op jit(solution)/shard_map/ppermute | solution.py:410
  47.4 0.0 copy-start.5
  47.4 0.1 collective-permute-start.9
  47.5 0.5 collective-permute-start.10
  48.0 0.1 collective-permute-start.11
  48.1 0.4 collective-permute-start.12
  48.5 3.8 %collective-permute-start.17 = (bf16[2,416,128]{2,1,0:T(8,128)(2,1)S(1)}, bf16[2,416,128]{2,1,0:T(8,128)(2,1)}, u32[]{:S(2)}, u32[]{:S(2)}) collective-permute-start(bf16[2,416,128]{2,1,0:T(8,128)(2,1)S(1)} %slice.110), channel_id=1, source_target_pairs={{0,192},{16,208},{32,224},{48,240},{64,0},{80,16},{96,32},{112,48}... | collective-permute-start | bytes 638984 | tf_op jit(solution)/shard_map/ppermute | solution.py:412
  52.3 0.7 slice.109
  53.1 2.8 %collective-permute-start.13 = (bf16[512,128]{1,0:T(8,128)(2,1)}, bf16[512,128]{1,0:T(8,128)(2,1)}, u32[]{:S(2)}, u32[]{:S(2)}) collective-permute-start(bf16[512,128]{1,0:T(8,128)(2,1)} %get-tuple-element.61), channel_id=1, source_target_pairs={{0,16},{16,0},{32,48},{48,32},{64,80},{80,64},{96,112},{112,96},{1... | collective-permute-start | bytes 393224 | tf_op jit(solution)/shard_map/ppermute | solution.py:414
  55.9 1.0 collective-permute-start.14
  56.9 1.5 collective-permute-start.15
  58.5 4.5 %latent_rows.1 = (bf16[1024,1536]{1,0:T(8,128)(2,1)}, bf16[1024,512]{1,0:T(8,128)(2,1)}, bf16[1024,64]{1,0:T(8,128)(2,1)}) custom-call(s32[4]{0:T(128)} %pad_add_fusion.pos, bf16[256,1536]{1,0:T(8,128)(2,1)} %ql.1, bf16[256,576]{1,0:T(8,128)(2,1)} %get-tuple-element.45.kl, bf16[2,816,128]{2,1,0:T(8,128)(2,1)} %copy-done, bf16[2,816,128]{2,1,0:T(8,128)(2,1)} %copy-done.5, ...), custom_call_target="tpu_custom_call" | custom-call | bytes 9000000 | tf_op jit(solution)/shard_map/latent_rows/pallas_call | solution.py:100
  63.0 4.3 %collective-permute-done.16.w3 = bf16[2,416,128]{2,1,0:T(8,128)(2,1)} collective-permute-done((bf16[2,416,128]{2,1,0:T(8,128)(2,1)}, bf16[2,416,128]{2,1,0:T(8,128)(2,1)}, u32[]{:S(2)}, u32[]{:S(2)}) %collective-permute-start.16) | collective-permute-done | bytes 213024 | tf_op jit(solution)/shard_map/ppermute | solution.py:412
  67.2 7.0 %projections.1 = (bf16[1024,384]{1,0:T(8,128)(2,1)}, bf16[1024,512]{1,0:T(8,128)(2,1)}, bf16[768,384]{1,0:T(8,128)(2,1)}, bf16[384,512]{1,0:T(8,128)(2,1)}, bf16[3840,128]{1,0:T(8,128)(2,1)}) custom-call(s32[4]{0:T(128)} %pad_add_fusion.pos, bf16[1024,1536]{1,0:T(8,128)(2,1)} %get-tuple-element.54.lq_in, bf16[1024,512]{1,0:T(8,128)(2,1)} %get-tuple-element.55.lk_in, ...), custom_call_target="tpu_custom_call" | custom-call | flops 1800000000 | bytes 12000000 | tf_op jit(solution)/shard_map/projections/pallas_call | solution.py:100
  74.2 9.1 %mla_backward.1 = (bf16[16,13,32,128]{3,2,1,0:T(8,128)(2,1)}, bf16[7680,128]{1,0:T(8,128)(2,1)}) custom-call(bf16[1024,1536]{1,0:T(8,128)(2,1)} %get-tuple-element.54.lq_in, bf16[1024,512]{1,0:T(8,128)(2,1)} %get-tuple-element.55.lk_in, bf16[1024,64]{1,0:T(8,128)(2,1)} %get-tuple-element.56.rope_in, bf16[512,128]{1,0:T(8,128)(2,1)} %get-tuple-element.57.og0, ...), custom_call_target="tpu_custom_call" | custom-call | flops 2700000000 | bytes 12000000 | tf_op jit(solution)/shard_map/mla_backward/pallas_call | solution.py:100
  83.3 0.0 copy-start.12
  83.3 5.4 %all-to-all-start = ((bf16[16,13,32,128]{3,2,1,0:T(8,128)(2,1)}), bf16[16,13,32,128]{3,2,1,0:T(8,128)(2,1)S(1)}, u32[]{:S(2)}, u32[]{:S(2)}) async-start(bf16[16,13,32,128]{3,2,1,0:T(8,128)(2,1)} %get-tuple-element.76), calls=%async_computation | async-start | bytes 3407872 | tf_op jit(solution)/shard_map/all_to_all | solution.py:436
  88.7 0.1 collective-permute-start.18
  88.8 0.5 collective-permute-start.19
  89.3 4.6 %collective-permute-done.19.w_other = bf16[3840,128]{1,0:T(8,128)(2,1)S(1)} collective-permute-done((bf16[3840,128]{1,0:T(8,128)(2,1)S(1)}, bf16[3840,128]{1,0:T(8,128)(2,1)S(1)}, u32[]{:S(2)}, u32[]{:S(2)}) %collective-permute-start.19) | collective-permute-done | bytes 983072 | tf_op jit(solution)/shard_map/ppermute | solution.py:434
  93.9 0.6 collective-permute-done.18.other
  94.5 0.3 copy-done.13
  94.8 7.5 %latent_grads.1 = (bf16[2,2,144,256]{3,2,1,0:T(8,128)(2,1)}, bf16[2,2,144,256]{3,2,1,0:T(8,128)(2,1)}, bf16[2,2,144,256]{3,2,1,0:T(8,128)(2,1)}, bf16[2,2,144,25...) custom-call(s32[4]{0:T(128)} %pad_add_fusion.pos, ...), custom_call_target="tpu_custom_call" | custom-call | flops 1800000000 | bytes 12000000 | tf_op jit(solution)/shard_map/latent_grads/pallas_call | solution.py:333
  102.3 2.7 %collective-permute-start.20 = (bf16[2,2,144,256]{3,2,1,0:T(8,128)(2,1)}, bf16[2,2,144,256]{3,2,1,0:T(8,128)(2,1)S(1)}, u32[]{:S(2)}, u32[]{:S(2)}) collective-permute-start(bf16[2,2,144,256]{3,2,1,0:T(8,128)(2,1)} %get-tuple-element.71), channel_id=1, source_target_pairs={{0,4},{1,5},{2,6},{3,7},{4,8},{5,9},{6,10},{7,11},{8,12},{9,13},{1... | collective-permute-start | bytes 884744 | tf_op jit(solution)/shard_map/ppermute | solution.py:441
  105.0 0.2 collective-permute-start.21
  105.2 1.0 collective-permute-start.22
  106.1 0.1 collective-permute-start.25
  106.3 12.1 %collective-permute-done.20 = bf16[2,2,144,256]{3,2,1,0:T(8,128)(2,1)S(1)} collective-permute-done((bf16[2,2,144,256]{3,2,1,0:T(8,128)(2,1)}, bf16[2,2,144,256]{3,2,1,0:T(8,128)(2,1)S(1)}, u32[]{:S(2)}, u32[]{:S(2)}) %collective-permute-start.20) | collective-permute-done | bytes 294944 | tf_op jit(solution)/shard_map/ppermute | solution.py:441
  118.4 3.3 %collective-permute-done.22 = bf16[2,2,144,256]{3,2,1,0:T(8,128)(2,1)S(1)} collective-permute-done((bf16[2,2,144,256]{3,2,1,0:T(8,128)(2,1)}, bf16[2,2,144,256]{3,2,1,0:T(8,128)(2,1)S(1)}, u32[]{:S(2)}, u32[]{:S(2)}) %collective-permute-start.22) | collective-permute-done | bytes 294944 | tf_op jit(solution)/shard_map/ppermute | solution.py:441
  121.6 1.1 convert_add_fusion
  122.7 0.7 fusion.9
  123.4 0.1 collective-permute-start.23
  123.6 6.3 %all-to-all-done.terms = bf16[16,13,32,128]{3,2,1,0:T(8,128)(2,1)S(1)} async-done(((bf16[16,13,32,128]{3,2,1,0:T(8,128)(2,1)}), bf16[16,13,32,128]{3,2,1,0:T(8,128)(2,1)S(1)}, u32[]{:S(2)}, u32[]{:S(2)}) %all-to-all-start) | async-done | bytes 1703968 | tf_op jit(solution)/shard_map/all_to_all | solution.py:436
  129.9 1.0 block_strips.1
  130.9 4.2 %all-to-all-start.1 = ((bf16[16,4,32,128]{3,2,1,0:T(8,128)(2,1)}), bf16[16,4,32,128]{3,2,1,0:T(8,128)(2,1)S(1)}, u32[]{:S(2)}, u32[]{:S(2)}) async-start(bf16[16,4,32,128]{3,2,1,0:T(8,128)(2,1)} %block_strips.1), calls=%async_computation.1 | async-start | bytes 1048576 | tf_op jit(solution)/shard_map/all_to_all | solution.py:450
  135.1 3.7 %collective-permute-done.23 = bf16[2,144,256]{2,1,0:T(8,128)(2,1)} collective-permute-done((bf16[2,144,256]{2,1,0:T(8,128)(2,1)}, bf16[2,144,256]{2,1,0:T(8,128)(2,1)}, u32[]{:S(2)}, u32[]{:S(2)}) %collective-permute-start.23) | collective-permute-done | bytes 147488 | tf_op jit(solution)/shard_map/ppermute | solution.py:443
  138.8 0.9 fusion.1
  139.8 0.1 fusion.6
  139.9 2.4 %collective-permute-start.26 = (bf16[2,144,256]{2,1,0:T(8,128)(2,1)S(1)}, bf16[2,144,256]{2,1,0:T(8,128)(2,1)S(1)}, u32[]{:S(2)}, u32[]{:S(2)}) collective-permute-start(bf16[2,144,256]{2,1,0:T(8,128)(2,1)S(1)} %get-tuple-element.85), channel_id=1, source_target_pairs={{0,4},{1,5},{2,6},{3,7},{4,8},{5,9},{6,10},{7,11},{8,12},{9,13},{1... | collective-permute-start | bytes 442376 | tf_op jit(solution)/shard_map/ppermute | solution.py:445
  142.3 1.6 collective-permute-start.27
  143.8 3.5 %collective-permute-start.24 = (bf16[144,256]{1,0:T(8,128)(2,1)S(1)}, bf16[144,256]{1,0:T(8,128)(2,1)S(1)}, u32[]{:S(2)}, u32[]{:S(2)}) collective-permute-start(bf16[144,256]{1,0:T(8,128)(2,1)S(1)} %get-tuple-element.92), channel_id=1, source_target_pairs={{0,16},{16,0},{32,48},{48,32},{64,80},{80,64},{96,112},{112,96},{1... | collective-permute-start | bytes 221192 | tf_op jit(solution)/shard_map/ppermute | solution.py:448
  147.3 3.7 %collective-permute-done.28 = bf16[2,144,256]{2,1,0:T(8,128)(2,1)S(1)} collective-permute-done((bf16[2,144,256]{2,1,0:T(8,128)(2,1)S(1)}, bf16[2,144,256]{2,1,0:T(8,128)(2,1)S(1)}, u32[]{:S(2)}, u32[]{:S(2)}) %collective-permute-start.28) | collective-permute-done | bytes 147488 | tf_op jit(solution)/shard_map/ppermute | solution.py:445
  151.0 0.1 fusion.4
  151.2 3.7 %collective-permute-start.30 = (bf16[144,256]{1,0:T(8,128)(2,1)S(1)}, bf16[144,256]{1,0:T(8,128)(2,1)S(1)}, u32[]{:S(2)}, u32[]{:S(2)}) collective-permute-start(bf16[144,256]{1,0:T(8,128)(2,1)S(1)} %get-tuple-element.90), channel_id=1, source_target_pairs={{0,48},{16,32},{32,16},{48,0},{64,112},{80,96},{96,80},{112,64},{1... | collective-permute-start | bytes 221192 | tf_op jit(solution)/shard_map/ppermute | solution.py:448
  154.8 1.3 collective-permute-start.29
  156.1 2.1 %owner_grams.1 = (f32[512,512]{1,0:T(8,128)}, f32[512,512]{1,0:T(8,128)}, f32[512,512]{1,0:T(8,128)}) custom-call(bf16[16,4,32,128]{3,2,1,0:T(8,128)(2,1)S(1)} %all-to-all-done.1.strips), custom_call_target="tpu_custom_call" | custom-call | flops 540000000 | bytes 4000000 | tf_op jit(solution)/shard_map/owner_grams/pallas_call | solution.py:100
  158.3 1.0 collective-permute-done.29
  159.3 0.6 slice_bitcast_fusion.9
  159.9 0.6 slice_bitcast_fusion.8
  (61 shorter events, 0.3 us)
Async XLA Ops:
  4.6 8.0 %collective-permute-start = (bf16[688,128]{1,0:T(8,128)(2,1)}, bf16[688,128]{1,0:T(8,128)(2,1)S(1)}, u32[]{:S(2)}, u32[]{:S(2)}) collective-permute-start(bf16[688,128]{1,0:T(8,128)(2,1)} %get-tuple-element.46), channel_id=1, source_target_pairs={{0,16},{16,0},{32,48},{48,32},{64,80},{80,64},{96,112},{112,96},{1... | collective-permute-start | bytes 528392 | tf_op jit(solution)/shard_map/ppermute | solution.py:408
  7.8 7.6 %collective-permute-start.1 = (bf16[688,128]{1,0:T(8,128)(2,1)}, bf16[688,128]{1,0:T(8,128)(2,1)S(1)}, u32[]{:S(2)}, u32[]{:S(2)}) collective-permute-start(bf16[688,128]{1,0:T(8,128)(2,1)} %get-tuple-element.47), channel_id=1, source_target_pairs={{0,32},{16,48},{32,0},{48,16},{64,96},{80,112},{96,64},{112,80},{1... | collective-permute-start | bytes 528392 | tf_op jit(solution)/shard_map/ppermute | solution.py:408
  9.8 8.3 %collective-permute-start.2 = (bf16[688,128]{1,0:T(8,128)(2,1)}, bf16[688,128]{1,0:T(8,128)(2,1)S(1)}, u32[]{:S(2)}, u32[]{:S(2)}) collective-permute-start(bf16[688,128]{1,0:T(8,128)(2,1)} %get-tuple-element.48), channel_id=1, source_target_pairs={{0,48},{16,32},{32,16},{48,0},{64,112},{80,96},{96,80},{112,64},{1... | collective-permute-start | bytes 528392 | tf_op jit(solution)/shard_map/ppermute | solution.py:408
  15.4 41.5 %copy-start.14 = (bf16[512,128]{1,0:T(8,128)(2,1)S(1)}, bf16[512,128]{1,0:T(8,128)(2,1)}, u32[]{:S(2)}) copy-start(bf16[512,128]{1,0:T(8,128)(2,1)} %get-tuple-element.63) | copy-start | bytes 393220
  18.0 8.6 %collective-permute-start.3 = (bf16[816,128]{1,0:T(8,128)(2,1)S(1)}, bf16[816,128]{1,0:T(8,128)(2,1)S(1)}, u32[]{:S(2)}, u32[]{:S(2)}) collective-permute-start(bf16[816,128]{1,0:T(8,128)(2,1)S(1)} %get-tuple-element.89), channel_id=1, source_target_pairs={{0,2},{1,3},{2,0},{3,1},{4,6},{5,7},{6,4},{7,5},{8,10},{9,11},{10,... | collective-permute-start | bytes 626696 | tf_op jit(solution)/shard_map/ppermute | solution.py:416
  20.4 42.6 %copy-start.2 = (bf16[4,416,128]{2,1,0:T(8,128)(2,1)}, bf16[4,416,128]{2,1,0:T(8,128)(2,1)S(1)}, u32[]{:S(2)}) copy-start(bf16[4,416,128]{2,1,0:T(8,128)(2,1)S(1)} %pad_maximum_fusion.w0) | copy-start | bytes 1277956
  20.4 23.1 %collective-permute-start.8 = (bf16[4,416,128]{2,1,0:T(8,128)(2,1)S(1)}, bf16[4,416,128]{2,1,0:T(8,128)(2,1)S(1)}, u32[]{:S(2)}, u32[]{:S(2)}) collective-permute-start(bf16[4,416,128]{2,1,0:T(8,128)(2,1)S(1)} %pad_maximum_fusion.w0), channel_id=1, source_target_pairs={{0,192},{16,208},{32,224},{48,240},{64,0},{80,16},{96,32},{112,48}... | collective-permute-start | bytes 1277960 | tf_op jit(solution)/shard_map/ppermute | solution.py:411
  26.6 20.8 %collective-permute-start.7 = (bf16[4,416,128]{2,1,0:T(8,128)(2,1)S(1)}, bf16[4,416,128]{2,1,0:T(8,128)(2,1)S(1)}, u32[]{:S(2)}, u32[]{:S(2)}) collective-permute-start(bf16[4,416,128]{2,1,0:T(8,128)(2,1)S(1)} %pad_maximum_fusion.w0), channel_id=1, source_target_pairs={{0,64},{16,80},{32,96},{48,112},{64,128},{80,144},{96,160},{112,17... | collective-permute-start | bytes 1277960 | tf_op jit(solution)/shard_map/ppermute | solution.py:410
  26.7 31.8 %copy-start = (bf16[2,816,128]{2,1,0:T(8,128)(2,1)}, bf16[2,816,128]{2,1,0:T(8,128)(2,1)S(1)}, u32[]{:S(2)}) copy-start(bf16[2,816,128]{2,1,0:T(8,128)(2,1)S(1)} %pad_maximum_fusion.1.refs_0_) | copy-start | bytes 1253380
  26.7 20.7 %collective-permute-start.6 = (bf16[2,816,128]{2,1,0:T(8,128)(2,1)S(1)}, bf16[2,816,128]{2,1,0:T(8,128)(2,1)S(1)}, u32[]{:S(2)}, u32[]{:S(2)}) collective-permute-start(bf16[2,816,128]{2,1,0:T(8,128)(2,1)S(1)} %pad_maximum_fusion.1.refs_0_), channel_id=1, source_target_pairs={{0,12},{1,13},{2,14},{3,15},{4,0},{5,1},{6,2},{7,3},{8,4},{9,5},{1... | collective-permute-start | bytes 1253384 | tf_op jit(solution)/shard_map/ppermute | solution.py:417
  27.6 19.8 %collective-permute-start.5 = (bf16[2,816,128]{2,1,0:T(8,128)(2,1)S(1)}, bf16[2,816,128]{2,1,0:T(8,128)(2,1)S(1)}, u32[]{:S(2)}, u32[]{:S(2)}) collective-permute-start(bf16[2,816,128]{2,1,0:T(8,128)(2,1)S(1)} %pad_maximum_fusion.1.refs_0_), channel_id=1, source_target_pairs={{0,8},{1,9},{2,10},{3,11},{4,12},{5,13},{6,14},{7,15},{8,0},{9,1},... | collective-permute-start | bytes 1253384 | tf_op jit(solution)/shard_map/ppermute | solution.py:417
  28.7 18.7 %collective-permute-start.4 = (bf16[2,816,128]{2,1,0:T(8,128)(2,1)S(1)}, bf16[2,816,128]{2,1,0:T(8,128)(2,1)S(1)}, u32[]{:S(2)}, u32[]{:S(2)}) collective-permute-start(bf16[2,816,128]{2,1,0:T(8,128)(2,1)S(1)} %pad_maximum_fusion.1.refs_0_), channel_id=1, source_target_pairs={{0,4},{1,5},{2,6},{3,7},{4,8},{5,9},{6,10},{7,11},{8,12},{9,13},{1... | collective-permute-start | bytes 1253384 | tf_op jit(solution)/shard_map/ppermute | solution.py:417
  43.5 13.4 %copy-start.10 = (bf16[4,416,128]{2,1,0:T(8,128)(2,1)}, bf16[4,416,128]{2,1,0:T(8,128)(2,1)S(1)}, u32[]{:S(2)}) copy-start(bf16[4,416,128]{2,1,0:T(8,128)(2,1)S(1)} %collective-permute-done.8.w2) | copy-start | bytes 1277956
  47.4 11.1 %copy-start.11 = (bf16[4,416,128]{2,1,0:T(8,128)(2,1)}, bf16[4,416,128]{2,1,0:T(8,128)(2,1)S(1)}, u32[]{:S(2)}) copy-start(bf16[4,416,128]{2,1,0:T(8,128)(2,1)S(1)} %collective-permute-done.7.w1) | copy-start | bytes 1277956
  47.4 11.1 %copy-start.3 = (bf16[2,816,128]{2,1,0:T(8,128)(2,1)}, bf16[2,816,128]{2,1,0:T(8,128)(2,1)S(1)}, u32[]{:S(2)}) copy-start(bf16[2,816,128]{2,1,0:T(8,128)(2,1)S(1)} %collective-permute-done.6.refs_3_) | copy-start | bytes 1253380
  47.4 11.1 %copy-start.4 = (bf16[2,816,128]{2,1,0:T(8,128)(2,1)}, bf16[2,816,128]{2,1,0:T(8,128)(2,1)S(1)}, u32[]{:S(2)}) copy-start(bf16[2,816,128]{2,1,0:T(8,128)(2,1)S(1)} %collective-permute-done.5.refs_2_) | copy-start | bytes 1253380
  47.4 11.1 %copy-start.5 = (bf16[2,816,128]{2,1,0:T(8,128)(2,1)}, bf16[2,816,128]{2,1,0:T(8,128)(2,1)S(1)}, u32[]{:S(2)}) copy-start(bf16[2,816,128]{2,1,0:T(8,128)(2,1)S(1)} %collective-permute-done.4.refs_1_) | copy-start | bytes 1253380
  47.4 5.6 %collective-permute-start.9 = (bf16[2,816,128]{2,1,0:T(8,128)(2,1)S(1)}, bf16[2,816,128]{2,1,0:T(8,128)(2,1)S(1)}, u32[]{:S(2)}, u32[]{:S(2)}) collective-permute-start(bf16[2,816,128]{2,1,0:T(8,128)(2,1)S(1)} %pad_maximum_fusion.1.refs_0_), channel_id=1, source_target_pairs={{0,1},{1,0},{2,3},{3,2},{4,5},{5,4},{6,7},{7,6},{8,9},{9,8},{10,11... | collective-permute-start | bytes 1253384 | tf_op jit(solution)/shard_map/ppermute | solution.py:419
  47.5 5.5 %collective-permute-start.10 = (bf16[2,816,128]{2,1,0:T(8,128)(2,1)S(1)}, bf16[2,816,128]{2,1,0:T(8,128)(2,1)S(1)}, u32[]{:S(2)}, u32[]{:S(2)}) collective-permute-start(bf16[2,816,128]{2,1,0:T(8,128)(2,1)S(1)} %collective-permute-done.4.refs_1_), channel_id=1, source_target_pairs={{0,1},{1,0},{2,3},{3,2},{4,5},{5,4},{6,7},{7,6},{8,9},{9,8},{10,11... | collective-permute-start | bytes 1253384 | tf_op jit(solution)/shard_map/ppermute | solution.py:419
  48.0 7.9 %collective-permute-start.11 = (bf16[2,816,128]{2,1,0:T(8,128)(2,1)S(1)}, bf16[2,816,128]{2,1,0:T(8,128)(2,1)S(1)}, u32[]{:S(2)}, u32[]{:S(2)}) collective-permute-start(bf16[2,816,128]{2,1,0:T(8,128)(2,1)S(1)} %collective-permute-done.5.refs_2_), channel_id=1, source_target_pairs={{0,1},{1,0},{2,3},{3,2},{4,5},{5,4},{6,7},{7,6},{8,9},{9,8},{10,11... | collective-permute-start | bytes 1253384 | tf_op jit(solution)/shard_map/ppermute | solution.py:419
  48.1 8.8 %collective-permute-start.12 = (bf16[2,816,128]{2,1,0:T(8,128)(2,1)S(1)}, bf16[2,816,128]{2,1,0:T(8,128)(2,1)S(1)}, u32[]{:S(2)}, u32[]{:S(2)}) collective-permute-start(bf16[2,816,128]{2,1,0:T(8,128)(2,1)S(1)} %collective-permute-done.6.refs_3_), channel_id=1, source_target_pairs={{0,1},{1,0},{2,3},{3,2},{4,5},{5,4},{6,7},{7,6},{8,9},{9,8},{10,11... | collective-permute-start | bytes 1253384 | tf_op jit(solution)/shard_map/ppermute | solution.py:419
  48.5 14.4 %collective-permute-start.17 = (bf16[2,416,128]{2,1,0:T(8,128)(2,1)S(1)}, bf16[2,416,128]{2,1,0:T(8,128)(2,1)}, u32[]{:S(2)}, u32[]{:S(2)}) collective-permute-start(bf16[2,416,128]{2,1,0:T(8,128)(2,1)S(1)} %slice.110), channel_id=1, source_target_pairs={{0,192},{16,208},{32,224},{48,240},{64,0},{80,16},{96,32},{112,48}... | collective-permute-start | bytes 638984 | tf_op jit(solution)/shard_map/ppermute | solution.py:412
  53.0 5.4 %copy-start.6 = (bf16[2,816,128]{2,1,0:T(8,128)(2,1)}, bf16[2,816,128]{2,1,0:T(8,128)(2,1)S(1)}, u32[]{:S(2)}) copy-start(bf16[2,816,128]{2,1,0:T(8,128)(2,1)S(1)} %collective-permute-done.9.refs_4_) | copy-start | bytes 1253380
  53.0 14.2 %collective-permute-start.16 = (bf16[2,416,128]{2,1,0:T(8,128)(2,1)}, bf16[2,416,128]{2,1,0:T(8,128)(2,1)}, u32[]{:S(2)}, u32[]{:S(2)}) collective-permute-start(bf16[2,416,128]{2,1,0:T(8,128)(2,1)} %slice.109), channel_id=1, source_target_pairs={{0,64},{16,80},{32,96},{48,112},{64,128},{80,144},{96,160},{112,17... | collective-permute-start | bytes 638984 | tf_op jit(solution)/shard_map/ppermute | solution.py:412
  53.1 5.4 %copy-start.7 = (bf16[2,816,128]{2,1,0:T(8,128)(2,1)}, bf16[2,816,128]{2,1,0:T(8,128)(2,1)S(1)}, u32[]{:S(2)}) copy-start(bf16[2,816,128]{2,1,0:T(8,128)(2,1)S(1)} %collective-permute-done.10.refs_5_) | copy-start | bytes 1253380
  53.1 21.1 %collective-permute-start.13 = (bf16[512,128]{1,0:T(8,128)(2,1)}, bf16[512,128]{1,0:T(8,128)(2,1)}, u32[]{:S(2)}, u32[]{:S(2)}) collective-permute-start(bf16[512,128]{1,0:T(8,128)(2,1)} %get-tuple-element.61), channel_id=1, source_target_pairs={{0,16},{16,0},{32,48},{48,32},{64,80},{80,64},{96,112},{112,96},{1... | collective-permute-start | bytes 393224 | tf_op jit(solution)/shard_map/ppermute | solution.py:414
  55.9 2.6 %copy-start.8 = (bf16[2,816,128]{2,1,0:T(8,128)(2,1)}, bf16[2,816,128]{2,1,0:T(8,128)(2,1)S(1)}, u32[]{:S(2)}) copy-start(bf16[2,816,128]{2,1,0:T(8,128)(2,1)S(1)} %collective-permute-done.11.refs_6_) | copy-start | bytes 1253380
  55.9 18.3 %collective-permute-start.14 = (bf16[512,128]{1,0:T(8,128)(2,1)}, bf16[512,128]{1,0:T(8,128)(2,1)}, u32[]{:S(2)}, u32[]{:S(2)}) collective-permute-start(bf16[512,128]{1,0:T(8,128)(2,1)} %get-tuple-element.62), channel_id=1, source_target_pairs={{0,32},{16,48},{32,0},{48,16},{64,96},{80,112},{96,64},{112,80},{1... | collective-permute-start | bytes 393224 | tf_op jit(solution)/shard_map/ppermute | solution.py:414
  56.9 1.6 copy-start.9
  56.9 17.3 %collective-permute-start.15 = (bf16[512,128]{1,0:T(8,128)(2,1)S(1)}, bf16[512,128]{1,0:T(8,128)(2,1)}, u32[]{:S(2)}, u32[]{:S(2)}) collective-permute-start(bf16[512,128]{1,0:T(8,128)(2,1)S(1)} %copy-done.14), channel_id=1, source_target_pairs={{0,48},{16,32},{32,16},{48,0},{64,112},{80,96},{96,80},{112,64},{1... | collective-permute-start | bytes 393224 | tf_op jit(solution)/shard_map/ppermute | solution.py:414
  83.3 5.5 %copy-start.12 = (bf16[3840,128]{1,0:T(8,128)(2,1)S(1)}, bf16[3840,128]{1,0:T(8,128)(2,1)}, u32[]{:S(2)}) copy-start(bf16[3840,128]{1,0:T(8,128)(2,1)} %get-tuple-element.67) | copy-start | bytes 2949124
  83.3 46.5 %all-to-all-start = ((bf16[16,13,32,128]{3,2,1,0:T(8,128)(2,1)}), bf16[16,13,32,128]{3,2,1,0:T(8,128)(2,1)S(1)}, u32[]{:S(2)}, u32[]{:S(2)}) async-start(bf16[16,13,32,128]{3,2,1,0:T(8,128)(2,1)} %get-tuple-element.76), calls=%async_computation | async-start | bytes 3407872 | tf_op jit(solution)/shard_map/all_to_all | solution.py:436
  88.7 5.8 %collective-permute-start.18 = (bf16[7680,128]{1,0:T(8,128)(2,1)}, bf16[7680,128]{1,0:T(8,128)(2,1)}, u32[]{:S(2)}, u32[]{:S(2)}) collective-permute-start(bf16[7680,128]{1,0:T(8,128)(2,1)} %get-tuple-element.66.mine), channel_id=1, source_target_pairs={{0,1},{1,0},{2,3},{3,2},{4,5},{5,4},{6,7},{7,6},{8,9},{9,8},{10,11... | collective-permute-start | bytes 5898248 | tf_op jit(solution)/shard_map/ppermute | solution.py:438
  88.8 5.1 %collective-permute-start.19 = (bf16[3840,128]{1,0:T(8,128)(2,1)S(1)}, bf16[3840,128]{1,0:T(8,128)(2,1)S(1)}, u32[]{:S(2)}, u32[]{:S(2)}) collective-permute-start(bf16[3840,128]{1,0:T(8,128)(2,1)S(1)} %copy-done.12), channel_id=1, source_target_pairs={{0,1},{1,0},{2,3},{3,2},{4,5},{5,4},{6,7},{7,6},{8,9},{9,8},{10,11... | collective-permute-start | bytes 2949128 | tf_op jit(solution)/shard_map/ppermute | solution.py:434
  93.9 0.9 copy-start.13
  102.3 16.1 %collective-permute-start.20 = (bf16[2,2,144,256]{3,2,1,0:T(8,128)(2,1)}, bf16[2,2,144,256]{3,2,1,0:T(8,128)(2,1)S(1)}, u32[]{:S(2)}, u32[]{:S(2)}) collective-permute-start(bf16[2,2,144,256]{3,2,1,0:T(8,128)(2,1)} %get-tuple-element.71), channel_id=1, source_target_pairs={{0,4},{1,5},{2,6},{3,7},{4,8},{5,9},{6,10},{7,11},{8,12},{9,13},{1... | collective-permute-start | bytes 884744 | tf_op jit(solution)/shard_map/ppermute | solution.py:441
  105.0 13.4 %collective-permute-start.21 = (bf16[2,2,144,256]{3,2,1,0:T(8,128)(2,1)}, bf16[2,2,144,256]{3,2,1,0:T(8,128)(2,1)S(1)}, u32[]{:S(2)}, u32[]{:S(2)}) collective-permute-start(bf16[2,2,144,256]{3,2,1,0:T(8,128)(2,1)} %get-tuple-element.72), channel_id=1, source_target_pairs={{0,8},{1,9},{2,10},{3,11},{4,12},{5,13},{6,14},{7,15},{8,0},{9,1},... | collective-permute-start | bytes 884744 | tf_op jit(solution)/shard_map/ppermute | solution.py:441
  105.2 16.5 %collective-permute-start.22 = (bf16[2,2,144,256]{3,2,1,0:T(8,128)(2,1)}, bf16[2,2,144,256]{3,2,1,0:T(8,128)(2,1)S(1)}, u32[]{:S(2)}, u32[]{:S(2)}) collective-permute-start(bf16[2,2,144,256]{3,2,1,0:T(8,128)(2,1)} %get-tuple-element.73), channel_id=1, source_target_pairs={{0,12},{1,13},{2,14},{3,15},{4,0},{5,1},{6,2},{7,3},{8,4},{9,5},{1... | collective-permute-start | bytes 884744 | tf_op jit(solution)/shard_map/ppermute | solution.py:441
  106.1 33.6 %collective-permute-start.25 = (bf16[4,2,144,256]{3,2,1,0:T(8,128)(2,1)}, bf16[4,2,144,256]{3,2,1,0:T(8,128)(2,1)S(1)}, u32[]{:S(2)}, u32[]{:S(2)}) collective-permute-start(bf16[4,2,144,256]{3,2,1,0:T(8,128)(2,1)} %get-tuple-element.75), channel_id=1, source_target_pairs={{0,2},{1,3},{2,0},{3,1},{4,6},{5,7},{6,4},{7,5},{8,10},{9,11},{10,... | collective-permute-start | bytes 1769480 | tf_op jit(solution)/shard_map/ppermute | solution.py:440
  123.4 16.3 %copy-start.1 = (bf16[4,2,144,256]{3,2,1,0:T(8,128)(2,1)S(1)}, bf16[4,2,144,256]{3,2,1,0:T(8,128)(2,1)}, u32[]{:S(2)}) copy-start(bf16[4,2,144,256]{3,2,1,0:T(8,128)(2,1)} %get-tuple-element.74) | copy-start | bytes 1769476
  123.4 15.4 %collective-permute-start.23 = (bf16[2,144,256]{2,1,0:T(8,128)(2,1)}, bf16[2,144,256]{2,1,0:T(8,128)(2,1)}, u32[]{:S(2)}, u32[]{:S(2)}) collective-permute-start(bf16[2,144,256]{2,1,0:T(8,128)(2,1)} %fusion.9), channel_id=1, source_target_pairs={{0,2},{1,3},{2,0},{3,1},{4,6},{5,7},{6,4},{7,5},{8,10},{9,11},{10,... | collective-permute-start | bytes 442376 | tf_op jit(solution)/shard_map/ppermute | solution.py:443
  130.9 25.2 %all-to-all-start.1 = ((bf16[16,4,32,128]{3,2,1,0:T(8,128)(2,1)}), bf16[16,4,32,128]{3,2,1,0:T(8,128)(2,1)S(1)}, u32[]{:S(2)}, u32[]{:S(2)}) async-start(bf16[16,4,32,128]{3,2,1,0:T(8,128)(2,1)} %block_strips.1), calls=%async_computation.1 | async-start | bytes 1048576 | tf_op jit(solution)/shard_map/all_to_all | solution.py:450
  139.9 7.5 %collective-permute-start.26 = (bf16[2,144,256]{2,1,0:T(8,128)(2,1)S(1)}, bf16[2,144,256]{2,1,0:T(8,128)(2,1)S(1)}, u32[]{:S(2)}, u32[]{:S(2)}) collective-permute-start(bf16[2,144,256]{2,1,0:T(8,128)(2,1)S(1)} %get-tuple-element.85), channel_id=1, source_target_pairs={{0,4},{1,5},{2,6},{3,7},{4,8},{5,9},{6,10},{7,11},{8,12},{9,13},{1... | collective-permute-start | bytes 442376 | tf_op jit(solution)/shard_map/ppermute | solution.py:445
  142.2 8.8 %collective-permute-start.28 = (bf16[2,144,256]{2,1,0:T(8,128)(2,1)S(1)}, bf16[2,144,256]{2,1,0:T(8,128)(2,1)S(1)}, u32[]{:S(2)}, u32[]{:S(2)}) collective-permute-start(bf16[2,144,256]{2,1,0:T(8,128)(2,1)S(1)} %get-tuple-element.86), channel_id=1, source_target_pairs={{0,12},{1,13},{2,14},{3,15},{4,0},{5,1},{6,2},{7,3},{8,4},{9,5},{1... | collective-permute-start | bytes 442376 | tf_op jit(solution)/shard_map/ppermute | solution.py:445
  142.3 8.8 %collective-permute-start.27 = (bf16[2,144,256]{2,1,0:T(8,128)(2,1)S(1)}, bf16[2,144,256]{2,1,0:T(8,128)(2,1)S(1)}, u32[]{:S(2)}, u32[]{:S(2)}) collective-permute-start(bf16[2,144,256]{2,1,0:T(8,128)(2,1)S(1)} %get-tuple-element.87), channel_id=1, source_target_pairs={{0,8},{1,9},{2,10},{3,11},{4,12},{5,13},{6,14},{7,15},{8,0},{9,1},... | collective-permute-start | bytes 442376 | tf_op jit(solution)/shard_map/ppermute | solution.py:445
  143.8 14.4 %collective-permute-start.24 = (bf16[144,256]{1,0:T(8,128)(2,1)S(1)}, bf16[144,256]{1,0:T(8,128)(2,1)S(1)}, u32[]{:S(2)}, u32[]{:S(2)}) collective-permute-start(bf16[144,256]{1,0:T(8,128)(2,1)S(1)} %get-tuple-element.92), channel_id=1, source_target_pairs={{0,16},{16,0},{32,48},{48,32},{64,80},{80,64},{96,112},{112,96},{1... | collective-permute-start | bytes 221192 | tf_op jit(solution)/shard_map/ppermute | solution.py:448
  151.2 7.1 %collective-permute-start.30 = (bf16[144,256]{1,0:T(8,128)(2,1)S(1)}, bf16[144,256]{1,0:T(8,128)(2,1)S(1)}, u32[]{:S(2)}, u32[]{:S(2)}) collective-permute-start(bf16[144,256]{1,0:T(8,128)(2,1)S(1)} %get-tuple-element.90), channel_id=1, source_target_pairs={{0,48},{16,32},{32,16},{48,0},{64,112},{80,96},{96,80},{112,64},{1... | collective-permute-start | bytes 221192 | tf_op jit(solution)/shard_map/ppermute | solution.py:448
  154.8 4.4 %collective-permute-start.29 = (bf16[144,256]{1,0:T(8,128)(2,1)S(1)}, bf16[144,256]{1,0:T(8,128)(2,1)S(1)}, u32[]{:S(2)}, u32[]{:S(2)}) collective-permute-start(bf16[144,256]{1,0:T(8,128)(2,1)S(1)} %get-tuple-element.91), channel_id=1, source_target_pairs={{0,32},{16,48},{32,0},{48,16},{64,96},{80,112},{96,64},{112,80},{1... | collective-permute-start | bytes 221192 | tf_op jit(solution)/shard_map/ppermute | solution.py:448

commit v4 on v3

--- a/solution.py
+++ b/solution.py
@@ -19,6 +19,7 @@
 F32 = jnp.float32
 BF16 = jnp.bfloat16
 WHOLE = 60
+VMEM_MAIN = 16
 
 
 def dot(a, b, ca, cb):
@@ -64,12 +65,11 @@
 
 
 def latent_kernel(pos, ql, kl, *refs):
-    lats, outs, (lq, lk, rope, sems) = refs[:8], refs[8:11], refs[11:]
+    lats, (lq, lk, rope) = refs[:8], refs[8:]
     core, chip = pos[0], pos[1]
     lq[0:256, :] = ql[...]
     lk[0:256, :] = kl[:, :KVL]
     rope[0:256, :] = kl[:, KVL:]
-    copies = []
     for s in range(4):
         for side in range(2 if s else 0):
             base = 128 * (core ^ side)
@@ -84,12 +84,6 @@
                     for t in range(4):
                         lk[rows, 128 * t : 128 * t + 128] = lat[y, at + 192 + 16 * t : at + 208 + 16 * t, :]
                     rope[rows, :] = lat[y, at + 256 : at + 272, :ROPE]
-        part = pl.ds(256 * s, 256)
-        for i, (source, out) in enumerate(zip((lq, lk, rope), outs)):
-            copies.append(pltpu.make_async_copy(source.at[part], out.at[part], sems.at[s, i]))
-            copies[-1].start()
-    for copy in copies:
-        copy.wait()
 
 
 def call(kernel, name, out_shape, vmem_mib, args, scratch=(), out_specs=None, in_specs=None, flops=0, size=0, scalars=False):
@@ -110,16 +104,14 @@
 
 
 def project_kernel(
-    pos, lq_in, lk_in, w0, w1, w2, w3, w4, query_out, keyval_out, wq_out, wkv_out, given_out,
-    lq, lk, w, wq3, wkv3, query, keyval, wq2, wkv2, sems,
+    pos, lq, lk, w0, w1, w2, w3, w4, query, keyval, wq_out, wkv_out, given_out, w, wq3, wkv3, wq2, wkv2, sems,
 ):
     core, member, group = pos[0], pos[2], pos[3]
     copies, at = [], 0
     for i, piece in enumerate((w0, w1, w2, w3, w4)):
         copies.append(pltpu.make_async_copy(piece, w.at[pl.ds(at, piece.shape[0])], sems.at[i]))
         at += piece.shape[0]
-    rows_in = [pltpu.make_async_copy(lk_in, lk, sems.at[5]), pltpu.make_async_copy(lq_in, lq, sems.at[6])]
-    for copy in copies + rows_in:
+    for copy in copies:
         copy.start()
     for copy in copies:
         copy.wait()
@@ -131,11 +123,7 @@
             for t in range(4):
                 wkv3[d, :, 128 * t : 128 * t + 128] = w[4 * j + i, 288 + 32 * t : 320 + 32 * t, :]
     wq, wkv = wq3[...].reshape(1536, 384), wkv3[...].reshape(512, 512)
-    rows_in[0].wait()
     keyval[...] = dot(lk[...], wkv, 1, 0).astype(BF16)
-    ends = [pltpu.make_async_copy(keyval, keyval_out, sems.at[7])]
-    ends[0].start()
-    rows_in[1].wait()
     query[...] = dot(lq[...], wq, 1, 0).astype(BF16)
     wide = wkv.astype(F32)
     for h in range(16):
@@ -146,7 +134,7 @@
         if own:
             piece = jnp.concatenate([wide[36 * h : 36 * h + own, :], piece[own:]], axis=0)
         wkv2[side, 48 * (h // 2) : 48 * (h // 2) + 48, :] = piece.astype(BF16)
-    last = [(query, query_out), (wq2.at[0], wq_out), (wkv2.at[0], wkv_out)]
+    last, ends = [(wq2.at[0], wq_out), (wkv2.at[0], wkv_out)], []
     for source, to, tiles in ((wq2.at[1], 0, 3), (wkv2.at[1], 2304, 4)):
         size = source.shape[0]
         for t in range(tiles):
@@ -160,63 +148,44 @@
 
 def project_call(*args):
     shape = jax.ShapeDtypeStruct
-    hbm = pl.BlockSpec(memory_space=pltpu.HBM)
-    shapes = [(1024, 384), (1024, 512), (768, 384), (384, 512), (3840, 128)]
+    vmem, hbm = pl.BlockSpec(memory_space=pltpu.VMEM), pl.BlockSpec(memory_space=pltpu.HBM)
+    shapes = [(768, 384), (384, 512), (3840, 128)]
     return call(
         project_kernel,
         "projections",
-        [shape(x, BF16) for x in shapes],
-        WHOLE,
+        [shape((1024, 384), BF16), shape((1024, 512), BF16)] + [pltpu.HBM(x, BF16) for x in shapes],
+        24,
         args,
         scratch=[
-            pltpu.VMEM((1024, 1536), BF16),
-            pltpu.VMEM((1024, 512), BF16),
             pltpu.VMEM((16, 416, 128), BF16),
             pltpu.VMEM((16, 96, 384), BF16),
             pltpu.VMEM((16, 32, 512), BF16),
-            pltpu.VMEM((1024, 384), BF16),
-            pltpu.VMEM((1024, 512), BF16),
             pltpu.VMEM((2, 768, 384), BF16),
             pltpu.VMEM((2, 384, 512), BF16),
             pltpu.SemaphoreType.DMA((18,)),
         ],
-        in_specs=[pl.BlockSpec(memory_space=pltpu.SMEM)] + [hbm] * 7,
-        out_specs=[hbm] * 5,
+        in_specs=[pl.BlockSpec(memory_space=pltpu.SMEM)] + [vmem] * 2 + [hbm] * 5,
+        out_specs=[vmem] * 2 + [hbm] * 3,
         flops=1_800_000_000,
         size=12_000_000,
     )
 
 
 def main_kernel(
-    lq_in, lk_in, rope_in, og0, og1, og2, og3, query_in, keyval_in, out, given_out,
-    lq, lk, rope, og, dq, dkv, drope, term, row_sems, sems,
+    lq, lk, rope, og0, og1, og2, og3, queries, keyvals, out, given_out, dq, dkv, drope, term, sems
 ):
-    whole = [pltpu.make_async_copy(lk_in, lk, sems.at[0]), pltpu.make_async_copy(lq_in, lq, sems.at[1])]
-    rows_in = []
-    for s, grad in enumerate((og0, og1, og2, og3)):
-        rows = pl.ds(256 * s, 256)
-        pairs = [(x.at[rows], y.at[rows]) for x, y in ((query_in, dq), (keyval_in, dkv), (rope_in, rope))]
-        pairs.append((grad, og.at[s]))
-        rows_in.append([pltpu.make_async_copy(x, y, row_sems.at[s, i]) for i, (x, y) in enumerate(pairs)])
-        for copy in rows_in[s]:
-            copy.start()
-    for copy in whole:
-        copy.start()
-
     causal = lax.broadcasted_iota(jnp.int32, (256, 256), 0) <= lax.broadcasted_iota(jnp.int32, (256, 256), 1)
     ends = []
     for s in range(4):
         rows = pl.ds(256 * s, 256)
-        for copy in rows_in[s]:
-            copy.wait()
-        query, keyval, rope_key = dq[rows, :], dkv[rows, :], rope[rows, :]
+        query, keyval, rope_key = queries[rows, :], keyvals[rows, :], rope[rows, :]
         rope_sum = jnp.zeros((256, ROPE), F32)
         dq_parts = []
         for h in range(2):
             q_h = query[:, QK * h : QK * h + QK]
             key = jnp.concatenate([keyval[:, 256 * h : 256 * h + 128], rope_key], axis=1)
             value = keyval[:, 256 * h + 128 : 256 * h + 256]
-            grad = og[s, 256 * h : 256 * h + 256, :]
+            grad = (og0, og1, og2, og3)[s][256 * h : 256 * h + 256, :]
             weights = jnp.where(causal, jnp.exp2(dot(key, q_h, 1, 1) * (SCALE * LOG2E)), 0.0)
             total = jnp.sum(weights, axis=0, keepdims=True)
             shrink = jnp.where(total > 2.0**100, 2.0**-100, 1.0)
@@ -242,8 +211,6 @@
                 ends[-1].start()
                 to += size
 
-    for copy in whole:
-        copy.wait()
     for block in (3, 0, 1, 2):
         if block == 3:
             value = dot(lk[...], dkv[...], 0, 0).astype(BF16)
@@ -266,22 +233,17 @@
     return call(
         main_kernel,
         "mla_backward",
-        [shape((16, 13, 32, 128), BF16), shape((7680, 128), BF16)],
-        WHOLE,
+        [pltpu.HBM((16, 13, 32, 128), BF16), pltpu.HBM((7680, 128), BF16)],
+        VMEM_MAIN,
         args,
         scratch=[
-            pltpu.VMEM((1024, 1536), BF16),
-            pltpu.VMEM((1024, 512), BF16),
-            pltpu.VMEM((1024, ROPE), BF16),
-            pltpu.VMEM((4, 512, 128), BF16),
             pltpu.VMEM((1024, 384), BF16),
             pltpu.VMEM((1024, 512), BF16),
             pltpu.VMEM((ROPE, 1024), BF16),
             pltpu.VMEM((16, 13, 32, 128), BF16),
-            pltpu.SemaphoreType.DMA((4, 4)),
             pltpu.SemaphoreType.DMA((64,)),
         ],
-        in_specs=[hbm] * 9,
+        in_specs=None,
         out_specs=[hbm] * 2,
         flops=2_700_000_000,
         size=12_000_000,
@@ -423,10 +385,8 @@
         latent_kernel,
         "latent_rows",
         rows,
-        WHOLE,
+        20,
         (pos, q_latent, kl, *lats),
-        scratch=[pltpu.VMEM(x.shape, BF16) for x in rows] + [pltpu.SemaphoreType.DMA((4, 3))],
-        out_specs=[hbm] * 3,
         size=9_000_000,
         scalars=True,
     )

time: 161 us -> 156 us (0.969)
  Pallas kernels: 34.3 us -> 27.1 us
  waiting for transfers between devices: 64.4 us -> 67.5 us
    pallas_call x6, Pallas kernels: 26.8 us -> 19.7 us  [call(): pl.pallas_call(kernel, out_shape=out_shape, in_specs=specs if in_specs is...]
    ppermute x1, waiting for transfers between devices: 0.01 us -> 2.58 us  [per_device(): lax.ppermute(from_up[2:], 'dp', GROUP_DOWN)]
  transfers between devices with their start and end apart: 33 -> 33, of which waited for: 14 -> 15; matrix products, arithmetic and copies ran while one was open for 3% -> 3% of each run, Pallas kernels for 14% -> 11%
where the time goes in v4:
time: 156 us
  waiting for transfers between devices  67.5 us (43%)
  starting transfers between devices  53.8 us (34%)
  Pallas kernels  27.1 us (17%)
  other arithmetic  3.87 us (2%)
  local copies, waits for them, and re-layouts  2.36 us (2%)
    pallas_call x6, Pallas kernels, call(): pl.pallas_call(kernel, out_shape=out_shape, in_specs=specs if in_specs is...  19.7 us
    ppermute x6, waiting for transfers between devices, per_device(): lax.ppermute(parts[k], 'head', ALONG_X[k])  19.2 us
    ppermute x1, waiting for transfers between devices, per_device(): from_up = lax.ppermute(w, 'dp', GROUP_DOWN)  12.8 us
    ppermute x3, starting transfers between devices, per_device(): lax.ppermute(part[s], 'dp', PARTNER[s])  8.63 us
    ppermute x3, waiting for transfers between devices, per_device(): parts = [lax.ppermute(sends[s - 1], 'dp', PARTNER[s]) for s in (1, 2, 3)]  8.18 us
    ppermute x6, starting transfers between devices, per_device(): lax.ppermute(parts[k], 'head', ALONG_X[k])  7.69 us
    pallas_call x1, Pallas kernels, latent_grad_call(): pl.pallas_call(latent_grad_kernel, out_shape=[jax.ShapeDtypeStruct((2, 2,...  7.46 us
    all_to_all x1, waiting for transfers between devices, per_device(): terms = lax.all_to_all(terms, 'dp', 0, 0, tiled=True)  6.38 us
  transfers between devices with their start and end apart: 33, of which 15 were waited for; matrix products, arithmetic and copies ran while one was open for 3% of the time, Pallas kernels for 11%

profile of v4, /device:TPU:6, one launch (start us, length us, event | category | flops | bytes accessed | tf_op | source)
XLA Modules:
  0.0 155.7 jit_solution(17190704685942230554)
XLA Ops:
  0.7 0.6 pad_add_fusion.pos
  1.2 3.2 %send_rows.1 = (bf16[688,128]{1,0:T(8,128)(2,1)}, bf16[688,128]{1,0:T(8,128)(2,1)}, bf16[688,128]{1,0:T(8,128)(2,1)}, bf16[416,128]{1,0:T(8,128)(2,1)}, bf16[512...) custom-call(s32[4]{0:T(128)} %pad_add_fusion.pos, ...), custom_call_target="tpu_custom_call" | custom-call | bytes 4000000 | tf_op jit(solution)/shard_map/send_rows/pallas_call | solution.py:94
  4.5 3.3 %collective-permute-start = (bf16[688,128]{1,0:T(8,128)(2,1)}, bf16[688,128]{1,0:T(8,128)(2,1)S(1)}, u32[]{:S(2)}, u32[]{:S(2)}) collective-permute-start(bf16[688,128]{1,0:T(8,128)(2,1)} %get-tuple-element.46), channel_id=1, source_target_pairs={{0,16},{16,0},{32,48},{48,32},{64,80},{80,64},{96,112},{112,96},{1... | collective-permute-start | bytes 528392 | tf_op jit(solution)/shard_map/ppermute | solution.py:370
  7.7 1.9 %collective-permute-start.1 = (bf16[688,128]{1,0:T(8,128)(2,1)}, bf16[688,128]{1,0:T(8,128)(2,1)S(1)}, u32[]{:S(2)}, u32[]{:S(2)}) collective-permute-start(bf16[688,128]{1,0:T(8,128)(2,1)} %get-tuple-element.47), channel_id=1, source_target_pairs={{0,32},{16,48},{32,0},{48,16},{64,96},{80,112},{96,64},{112,80},{1... | collective-permute-start | bytes 528392 | tf_op jit(solution)/shard_map/ppermute | solution.py:370
  9.7 2.8 %collective-permute-done = bf16[688,128]{1,0:T(8,128)(2,1)S(1)} collective-permute-done((bf16[688,128]{1,0:T(8,128)(2,1)}, bf16[688,128]{1,0:T(8,128)(2,1)S(1)}, u32[]{:S(2)}, u32[]{:S(2)}) %collective-permute-start) | collective-permute-done | bytes 176160 | tf_op jit(solution)/shard_map/ppermute | solution.py:370
  12.5 2.8 %collective-permute-done.1 = bf16[688,128]{1,0:T(8,128)(2,1)S(1)} collective-permute-done((bf16[688,128]{1,0:T(8,128)(2,1)}, bf16[688,128]{1,0:T(8,128)(2,1)S(1)}, u32[]{:S(2)}, u32[]{:S(2)}) %collective-permute-start.1) | collective-permute-done | bytes 176160 | tf_op jit(solution)/shard_map/ppermute | solution.py:370
  15.4 0.0 copy-start
  15.4 0.0 copy-start.1
  15.4 2.5 %collective-permute-done.2 = bf16[688,128]{1,0:T(8,128)(2,1)S(1)} collective-permute-done((bf16[688,128]{1,0:T(8,128)(2,1)}, bf16[688,128]{1,0:T(8,128)(2,1)S(1)}, u32[]{:S(2)}, u32[]{:S(2)}) %collective-permute-start.2) | collective-permute-done | bytes 176160 | tf_op jit(solution)/shard_map/ppermute | solution.py:370
  18.0 1.3 collective-permute-start.3
  19.3 1.0 pad_maximum_fusion.w0
  20.3 6.2 %collective-permute-start.8 = (bf16[4,416,128]{2,1,0:T(8,128)(2,1)S(1)}, bf16[4,416,128]{2,1,0:T(8,128)(2,1)S(1)}, u32[]{:S(2)}, u32[]{:S(2)}) collective-permute-start(bf16[4,416,128]{2,1,0:T(8,128)(2,1)S(1)} %pad_maximum_fusion.w0), channel_id=1, source_target_pairs={{0,192},{16,208},{32,224},{48,240},{64,0},{80,16},{96,32},{112,48}... | collective-permute-start | bytes 1277960 | tf_op jit(solution)/shard_map/ppermute | solution.py:373
  26.6 0.9 collective-permute-start.6
  27.5 1.1 collective-permute-start.5
  28.6 2.1 %collective-permute-start.4 = (bf16[2,816,128]{2,1,0:T(8,128)(2,1)S(1)}, bf16[2,816,128]{2,1,0:T(8,128)(2,1)S(1)}, u32[]{:S(2)}, u32[]{:S(2)}) collective-permute-start(bf16[2,816,128]{2,1,0:T(8,128)(2,1)S(1)} %pad_maximum_fusion.1.refs_0_), channel_id=1, source_target_pairs={{0,4},{1,5},{2,6},{3,7},{4,8},{5,9},{6,10},{7,11},{8,12},{9,13},{1... | collective-permute-start | bytes 1253384 | tf_op jit(solution)/shard_map/ppermute | solution.py:379
  30.7 12.8 %collective-permute-done.8.w2 = bf16[4,416,128]{2,1,0:T(8,128)(2,1)S(1)} collective-permute-done((bf16[4,416,128]{2,1,0:T(8,128)(2,1)S(1)}, bf16[4,416,128]{2,1,0:T(8,128)(2,1)S(1)}, u32[]{:S(2)}, u32[]{:S(2)}) %collective-permute-start.8) | collective-permute-done | bytes 426016 | tf_op jit(solution)/shard_map/ppermute | solution.py:373
  43.4 3.8 %collective-permute-done.7.w1 = bf16[4,416,128]{2,1,0:T(8,128)(2,1)S(1)} collective-permute-done((bf16[4,416,128]{2,1,0:T(8,128)(2,1)S(1)}, bf16[4,416,128]{2,1,0:T(8,128)(2,1)S(1)}, u32[]{:S(2)}, u32[]{:S(2)}) %collective-permute-start.7) | collective-permute-done | bytes 426016 | tf_op jit(solution)/shard_map/ppermute | solution.py:372
  47.3 0.1 collective-permute-start.9
  47.4 0.5 collective-permute-start.10
  47.9 0.1 collective-permute-start.11
  48.0 0.4 collective-permute-start.12
  48.4 3.8 %collective-permute-start.17 = (bf16[2,416,128]{2,1,0:T(8,128)(2,1)S(1)}, bf16[2,416,128]{2,1,0:T(8,128)(2,1)S(1)}, u32[]{:S(2)}, u32[]{:S(2)}) collective-permute-start(bf16[2,416,128]{2,1,0:T(8,128)(2,1)S(1)} %slice.110), channel_id=1, source_target_pairs={{0,192},{16,208},{32,224},{48,240},{64,0},{80,16},{96,32},{112,48}... | collective-permute-start | bytes 638984 | tf_op jit(solution)/shard_map/ppermute | solution.py:374
  52.2 0.1 collective-permute-start.16
  52.3 2.8 %collective-permute-start.13 = (bf16[512,128]{1,0:T(8,128)(2,1)S(1)}, bf16[512,128]{1,0:T(8,128)(2,1)S(1)}, u32[]{:S(2)}, u32[]{:S(2)}) collective-permute-start(bf16[512,128]{1,0:T(8,128)(2,1)S(1)} %copy-done.9), channel_id=1, source_target_pairs={{0,16},{16,0},{32,48},{48,32},{64,80},{80,64},{96,112},{112,96},{1... | collective-permute-start | bytes 393224 | tf_op jit(solution)/shard_map/ppermute | solution.py:376
  55.1 1.0 collective-permute-start.14
  56.2 1.3 collective-permute-start.15
  57.4 1.2 latent_rows.1
  58.6 2.6 %collective-permute-done.17.w4 = bf16[2,416,128]{2,1,0:T(8,128)(2,1)S(1)} collective-permute-done((bf16[2,416,128]{2,1,0:T(8,128)(2,1)S(1)}, bf16[2,416,128]{2,1,0:T(8,128)(2,1)S(1)}, u32[]{:S(2)}, u32[]{:S(2)}) %collective-permute-start.17) | collective-permute-done | bytes 213024 | tf_op jit(solution)/shard_map/ppermute | solution.py:374
  61.2 4.8 %collective-permute-done.16.w3 = bf16[2,416,128]{2,1,0:T(8,128)(2,1)S(1)} collective-permute-done((bf16[2,416,128]{2,1,0:T(8,128)(2,1)S(1)}, bf16[2,416,128]{2,1,0:T(8,128)(2,1)S(1)}, u32[]{:S(2)}, u32[]{:S(2)}) %collective-permute-start.16) | collective-permute-done | bytes 213024 | tf_op jit(solution)/shard_map/ppermute | solution.py:374
  66.0 5.2 %projections.1 = (bf16[1024,384]{1,0:T(8,128)(2,1)S(1)}, bf16[1024,512]{1,0:T(8,128)(2,1)S(1)}, bf16[768,384]{1,0:T(8,128)(2,1)}, bf16[384,512]{1,0:T(8,128)(2,1)}, bf16[3840,128]{1,0:T(8,128)(2,1)}) custom-call(s32[4]{0:T(128)S(1)} %copy-done.2, bf16[1024,1536]{1,0:T(8,128)(2,1)S(1)} %get-tuple-element.54.lq, bf16[1024,512]{1,0:T(8,128)(2,1)S(1)} %get-tuple-element.55.lk, ...), custom_call_target="tpu_custom_call" | custom-call | flops 1800000000 | bytes 12000000 | tf_op jit(solution)/shard_map/projections/pallas_call | solution.py:94
  71.3 6.9 %mla_backward.1 = (bf16[16,13,32,128]{3,2,1,0:T(8,128)(2,1)}, bf16[7680,128]{1,0:T(8,128)(2,1)}) custom-call(bf16[1024,1536]{1,0:T(8,128)(2,1)S(1)} %get-tuple-element.54.lq, bf16[1024,512]{1,0:T(8,128)(2,1)S(1)} %get-tuple-element.55.lk, bf16[1024,64]{1,0:T(8,128)(2,1)S(1)} %get-tuple-element.56.rope, bf16[512,128]{1,0:T(8,128)(2,1)S(1)} %copy-done.3, ...), custom_call_target="tpu_custom_call" | custom-call | flops 2700000000 | bytes 12000000 | tf_op jit(solution)/shard_map/mla_backward/pallas_call | solution.py:94
  78.2 5.5 %all-to-all-start = ((bf16[16,13,32,128]{3,2,1,0:T(8,128)(2,1)}), bf16[16,13,32,128]{3,2,1,0:T(8,128)(2,1)S(1)}, u32[]{:S(2)}, u32[]{:S(2)}) async-start(bf16[16,13,32,128]{3,2,1,0:T(8,128)(2,1)} %get-tuple-element.76), calls=%async_computation | async-start | bytes 3407872 | tf_op jit(solution)/shard_map/all_to_all | solution.py:396
  83.7 0.1 collective-permute-start.18
  83.8 0.5 collective-permute-start.19
  84.3 4.6 %collective-permute-done.19.w_other = bf16[3840,128]{1,0:T(8,128)(2,1)S(1)} collective-permute-done((bf16[3840,128]{1,0:T(8,128)(2,1)S(1)}, bf16[3840,128]{1,0:T(8,128)(2,1)S(1)}, u32[]{:S(2)}, u32[]{:S(2)}) %collective-permute-start.19) | collective-permute-done | bytes 983072 | tf_op jit(solution)/shard_map/ppermute | solution.py:394
  88.9 0.6 collective-permute-done.18.other
  89.5 0.3 copy-done.6
  89.8 7.5 %latent_grads.1 = (bf16[2,2,144,256]{3,2,1,0:T(8,128)(2,1)}, bf16[2,2,144,256]{3,2,1,0:T(8,128)(2,1)}, bf16[2,2,144,256]{3,2,1,0:T(8,128)(2,1)}, bf16[2,2,144,25...) custom-call(s32[4]{0:T(128)} %pad_add_fusion.pos, ...), custom_call_target="tpu_custom_call" | custom-call | flops 1800000000 | bytes 12000000 | tf_op jit(solution)/shard_map/latent_grads/pallas_call | solution.py:295
  97.3 2.7 %collective-permute-start.20 = (bf16[2,2,144,256]{3,2,1,0:T(8,128)(2,1)}, bf16[2,2,144,256]{3,2,1,0:T(8,128)(2,1)S(1)}, u32[]{:S(2)}, u32[]{:S(2)}) collective-permute-start(bf16[2,2,144,256]{3,2,1,0:T(8,128)(2,1)} %get-tuple-element.71), channel_id=1, source_target_pairs={{0,4},{1,5},{2,6},{3,7},{4,8},{5,9},{6,10},{7,11},{8,12},{9,13},{1... | collective-permute-start | bytes 884744 | tf_op jit(solution)/shard_map/ppermute | solution.py:401
  100.0 0.2 collective-permute-start.21
  100.2 0.8 collective-permute-start.22
  100.9 0.1 collective-permute-start.25
  101.1 12.3 %collective-permute-done.20 = bf16[2,2,144,256]{3,2,1,0:T(8,128)(2,1)S(1)} collective-permute-done((bf16[2,2,144,256]{3,2,1,0:T(8,128)(2,1)}, bf16[2,2,144,256]{3,2,1,0:T(8,128)(2,1)S(1)}, u32[]{:S(2)}, u32[]{:S(2)}) %collective-permute-start.20) | collective-permute-done | bytes 294944 | tf_op jit(solution)/shard_map/ppermute | solution.py:401
  113.4 3.3 %collective-permute-done.22 = bf16[2,2,144,256]{3,2,1,0:T(8,128)(2,1)S(1)} collective-permute-done((bf16[2,2,144,256]{3,2,1,0:T(8,128)(2,1)}, bf16[2,2,144,256]{3,2,1,0:T(8,128)(2,1)S(1)}, u32[]{:S(2)}, u32[]{:S(2)}) %collective-permute-start.22) | collective-permute-done | bytes 294944 | tf_op jit(solution)/shard_map/ppermute | solution.py:401
  116.7 1.1 convert_add_fusion
  117.8 0.7 fusion.9
  118.4 0.1 collective-permute-start.23
  118.6 6.4 %all-to-all-done.terms = bf16[16,13,32,128]{3,2,1,0:T(8,128)(2,1)S(1)} async-done(((bf16[16,13,32,128]{3,2,1,0:T(8,128)(2,1)}), bf16[16,13,32,128]{3,2,1,0:T(8,128)(2,1)S(1)}, u32[]{:S(2)}, u32[]{:S(2)}) %all-to-all-start) | async-done | bytes 1703968 | tf_op jit(solution)/shard_map/all_to_all | solution.py:396
  125.0 1.0 block_strips.1
  126.0 4.2 %all-to-all-start.1 = ((bf16[16,4,32,128]{3,2,1,0:T(8,128)(2,1)}), bf16[16,4,32,128]{3,2,1,0:T(8,128)(2,1)S(1)}, u32[]{:S(2)}, u32[]{:S(2)}) async-start(bf16[16,4,32,128]{3,2,1,0:T(8,128)(2,1)} %block_strips.1), calls=%async_computation.1 | async-start | bytes 1048576 | tf_op jit(solution)/shard_map/all_to_all | solution.py:410
  130.2 3.6 %collective-permute-done.23 = bf16[2,144,256]{2,1,0:T(8,128)(2,1)} collective-permute-done((bf16[2,144,256]{2,1,0:T(8,128)(2,1)}, bf16[2,144,256]{2,1,0:T(8,128)(2,1)}, u32[]{:S(2)}, u32[]{:S(2)}) %collective-permute-start.23) | collective-permute-done | bytes 147488 | tf_op jit(solution)/shard_map/ppermute | solution.py:403
  133.7 0.9 fusion.1
  134.7 0.1 fusion.6
  134.8 2.5 %collective-permute-start.26 = (bf16[2,144,256]{2,1,0:T(8,128)(2,1)S(1)}, bf16[2,144,256]{2,1,0:T(8,128)(2,1)S(1)}, u32[]{:S(2)}, u32[]{:S(2)}) collective-permute-start(bf16[2,144,256]{2,1,0:T(8,128)(2,1)S(1)} %get-tuple-element.85), channel_id=1, source_target_pairs={{0,4},{1,5},{2,6},{3,7},{4,8},{5,9},{6,10},{7,11},{8,12},{9,13},{1... | collective-permute-start | bytes 442376 | tf_op jit(solution)/shard_map/ppermute | solution.py:405
  137.3 1.6 collective-permute-start.27
  138.9 3.6 %collective-permute-start.24 = (bf16[144,256]{1,0:T(8,128)(2,1)S(1)}, bf16[144,256]{1,0:T(8,128)(2,1)S(1)}, u32[]{:S(2)}, u32[]{:S(2)}) collective-permute-start(bf16[144,256]{1,0:T(8,128)(2,1)S(1)} %get-tuple-element.92), channel_id=1, source_target_pairs={{0,16},{16,0},{32,48},{48,32},{64,80},{80,64},{96,112},{112,96},{1... | collective-permute-start | bytes 221192 | tf_op jit(solution)/shard_map/ppermute | solution.py:408
  142.5 3.6 %collective-permute-done.28 = bf16[2,144,256]{2,1,0:T(8,128)(2,1)S(1)} collective-permute-done((bf16[2,144,256]{2,1,0:T(8,128)(2,1)S(1)}, bf16[2,144,256]{2,1,0:T(8,128)(2,1)S(1)}, u32[]{:S(2)}, u32[]{:S(2)}) %collective-permute-start.28) | collective-permute-done | bytes 147488 | tf_op jit(solution)/shard_map/ppermute | solution.py:405
  146.1 0.1 fusion.4
  146.2 3.7 %collective-permute-start.30 = (bf16[144,256]{1,0:T(8,128)(2,1)S(1)}, bf16[144,256]{1,0:T(8,128)(2,1)S(1)}, u32[]{:S(2)}, u32[]{:S(2)}) collective-permute-start(bf16[144,256]{1,0:T(8,128)(2,1)S(1)} %get-tuple-element.90), channel_id=1, source_target_pairs={{0,48},{16,32},{32,16},{48,0},{64,112},{80,96},{96,80},{112,64},{1... | collective-permute-start | bytes 221192 | tf_op jit(solution)/shard_map/ppermute | solution.py:408
  149.9 1.4 collective-permute-start.29
  151.3 2.1 %owner_grams.1 = (f32[512,512]{1,0:T(8,128)}, f32[512,512]{1,0:T(8,128)}, f32[512,512]{1,0:T(8,128)}) custom-call(bf16[16,4,32,128]{3,2,1,0:T(8,128)(2,1)S(1)} %all-to-all-done.1.strips), custom_call_target="tpu_custom_call" | custom-call | flops 540000000 | bytes 4000000 | tf_op jit(solution)/shard_map/owner_grams/pallas_call | solution.py:94
  153.4 1.0 collective-permute-done.29
  154.4 0.6 slice_bitcast_fusion.9
  155.0 0.6 slice_bitcast_fusion.8
  (51 shorter events, 0.3 us)
Async XLA Ops:
  4.5 8.0 %collective-permute-start = (bf16[688,128]{1,0:T(8,128)(2,1)}, bf16[688,128]{1,0:T(8,128)(2,1)S(1)}, u32[]{:S(2)}, u32[]{:S(2)}) collective-permute-start(bf16[688,128]{1,0:T(8,128)(2,1)} %get-tuple-element.46), channel_id=1, source_target_pairs={{0,16},{16,0},{32,48},{48,32},{64,80},{80,64},{96,112},{112,96},{1... | collective-permute-start | bytes 528392 | tf_op jit(solution)/shard_map/ppermute | solution.py:370
  7.7 7.6 %collective-permute-start.1 = (bf16[688,128]{1,0:T(8,128)(2,1)}, bf16[688,128]{1,0:T(8,128)(2,1)S(1)}, u32[]{:S(2)}, u32[]{:S(2)}) collective-permute-start(bf16[688,128]{1,0:T(8,128)(2,1)} %get-tuple-element.47), channel_id=1, source_target_pairs={{0,32},{16,48},{32,0},{48,16},{64,96},{80,112},{96,64},{112,80},{1... | collective-permute-start | bytes 528392 | tf_op jit(solution)/shard_map/ppermute | solution.py:370
  9.7 8.3 %collective-permute-start.2 = (bf16[688,128]{1,0:T(8,128)(2,1)}, bf16[688,128]{1,0:T(8,128)(2,1)S(1)}, u32[]{:S(2)}, u32[]{:S(2)}) collective-permute-start(bf16[688,128]{1,0:T(8,128)(2,1)} %get-tuple-element.48), channel_id=1, source_target_pairs={{0,48},{16,32},{32,16},{48,0},{64,112},{80,96},{96,80},{112,64},{1... | collective-permute-start | bytes 528392 | tf_op jit(solution)/shard_map/ppermute | solution.py:370
  15.3 37.0 %copy-start.9 = (bf16[512,128]{1,0:T(8,128)(2,1)S(1)}, bf16[512,128]{1,0:T(8,128)(2,1)}, u32[]{:S(2)}) copy-start(bf16[512,128]{1,0:T(8,128)(2,1)} %get-tuple-element.61) | copy-start | bytes 393220
  15.3 39.8 %copy-start.8 = (bf16[512,128]{1,0:T(8,128)(2,1)S(1)}, bf16[512,128]{1,0:T(8,128)(2,1)}, u32[]{:S(2)}) copy-start(bf16[512,128]{1,0:T(8,128)(2,1)} %get-tuple-element.62) | copy-start | bytes 393220
  15.3 40.8 %copy-start.7 = (bf16[512,128]{1,0:T(8,128)(2,1)S(1)}, bf16[512,128]{1,0:T(8,128)(2,1)}, u32[]{:S(2)}) copy-start(bf16[512,128]{1,0:T(8,128)(2,1)} %get-tuple-element.63) | copy-start | bytes 393220
  15.4 42.1 %copy-start = (bf16[256,1536]{1,0:T(8,128)(2,1)S(1)}, bf16[256,1536]{1,0:T(8,128)(2,1)}, u32[]{:S(2)}) copy-start(bf16[256,1536]{1,0:T(8,128)(2,1)} %ql.1) | copy-start | bytes 2359300
  15.4 42.1 %copy-start.1 = (bf16[256,576]{1,0:T(8,128)(2,1)S(1)}, bf16[256,576]{1,0:T(8,128)(2,1)}, u32[]{:S(2)}) copy-start(bf16[256,576]{1,0:T(8,128)(2,1)} %get-tuple-element.45.kl) | copy-start | bytes 884740
  15.4 42.0 %copy-start.2 = (s32[4]{0:T(128)S(1)}, s32[4]{0:T(128)}, u32[]{:S(2)}) copy-start(s32[4]{0:T(128)} %pad_add_fusion.pos) | copy-start | bytes 52
  18.0 8.6 %collective-permute-start.3 = (bf16[816,128]{1,0:T(8,128)(2,1)S(1)}, bf16[816,128]{1,0:T(8,128)(2,1)S(1)}, u32[]{:S(2)}, u32[]{:S(2)}) collective-permute-start(bf16[816,128]{1,0:T(8,128)(2,1)S(1)} %get-tuple-element.89), channel_id=1, source_target_pairs={{0,2},{1,3},{2,0},{3,1},{4,6},{5,7},{6,4},{7,5},{8,10},{9,11},{10,... | collective-permute-start | bytes 626696 | tf_op jit(solution)/shard_map/ppermute | solution.py:378
  20.3 23.1 %collective-permute-start.8 = (bf16[4,416,128]{2,1,0:T(8,128)(2,1)S(1)}, bf16[4,416,128]{2,1,0:T(8,128)(2,1)S(1)}, u32[]{:S(2)}, u32[]{:S(2)}) collective-permute-start(bf16[4,416,128]{2,1,0:T(8,128)(2,1)S(1)} %pad_maximum_fusion.w0), channel_id=1, source_target_pairs={{0,192},{16,208},{32,224},{48,240},{64,0},{80,16},{96,32},{112,48}... | collective-permute-start | bytes 1277960 | tf_op jit(solution)/shard_map/ppermute | solution.py:373
  26.5 20.8 %collective-permute-start.7 = (bf16[4,416,128]{2,1,0:T(8,128)(2,1)S(1)}, bf16[4,416,128]{2,1,0:T(8,128)(2,1)S(1)}, u32[]{:S(2)}, u32[]{:S(2)}) collective-permute-start(bf16[4,416,128]{2,1,0:T(8,128)(2,1)S(1)} %pad_maximum_fusion.w0), channel_id=1, source_target_pairs={{0,64},{16,80},{32,96},{48,112},{64,128},{80,144},{96,160},{112,17... | collective-permute-start | bytes 1277960 | tf_op jit(solution)/shard_map/ppermute | solution.py:372
  26.6 20.7 %collective-permute-start.6 = (bf16[2,816,128]{2,1,0:T(8,128)(2,1)S(1)}, bf16[2,816,128]{2,1,0:T(8,128)(2,1)S(1)}, u32[]{:S(2)}, u32[]{:S(2)}) collective-permute-start(bf16[2,816,128]{2,1,0:T(8,128)(2,1)S(1)} %pad_maximum_fusion.1.refs_0_), channel_id=1, source_target_pairs={{0,12},{1,13},{2,14},{3,15},{4,0},{5,1},{6,2},{7,3},{8,4},{9,5},{1... | collective-permute-start | bytes 1253384 | tf_op jit(solution)/shard_map/ppermute | solution.py:379
  27.5 19.8 %collective-permute-start.5 = (bf16[2,816,128]{2,1,0:T(8,128)(2,1)S(1)}, bf16[2,816,128]{2,1,0:T(8,128)(2,1)S(1)}, u32[]{:S(2)}, u32[]{:S(2)}) collective-permute-start(bf16[2,816,128]{2,1,0:T(8,128)(2,1)S(1)} %pad_maximum_fusion.1.refs_0_), channel_id=1, source_target_pairs={{0,8},{1,9},{2,10},{3,11},{4,12},{5,13},{6,14},{7,15},{8,0},{9,1},... | collective-permute-start | bytes 1253384 | tf_op jit(solution)/shard_map/ppermute | solution.py:379
  28.6 18.7 %collective-permute-start.4 = (bf16[2,816,128]{2,1,0:T(8,128)(2,1)S(1)}, bf16[2,816,128]{2,1,0:T(8,128)(2,1)S(1)}, u32[]{:S(2)}, u32[]{:S(2)}) collective-permute-start(bf16[2,816,128]{2,1,0:T(8,128)(2,1)S(1)} %pad_maximum_fusion.1.refs_0_), channel_id=1, source_target_pairs={{0,4},{1,5},{2,6},{3,7},{4,8},{5,9},{6,10},{7,11},{8,12},{9,13},{1... | collective-permute-start | bytes 1253384 | tf_op jit(solution)/shard_map/ppermute | solution.py:379
  47.3 4.9 %collective-permute-start.9 = (bf16[2,816,128]{2,1,0:T(8,128)(2,1)S(1)}, bf16[2,816,128]{2,1,0:T(8,128)(2,1)S(1)}, u32[]{:S(2)}, u32[]{:S(2)}) collective-permute-start(bf16[2,816,128]{2,1,0:T(8,128)(2,1)S(1)} %pad_maximum_fusion.1.refs_0_), channel_id=1, source_target_pairs={{0,1},{1,0},{2,3},{3,2},{4,5},{5,4},{6,7},{7,6},{8,9},{9,8},{10,11... | collective-permute-start | bytes 1253384 | tf_op jit(solution)/shard_map/ppermute | solution.py:381
  47.4 4.9 %collective-permute-start.10 = (bf16[2,816,128]{2,1,0:T(8,128)(2,1)S(1)}, bf16[2,816,128]{2,1,0:T(8,128)(2,1)S(1)}, u32[]{:S(2)}, u32[]{:S(2)}) collective-permute-start(bf16[2,816,128]{2,1,0:T(8,128)(2,1)S(1)} %collective-permute-done.4.refs_1_), channel_id=1, source_target_pairs={{0,1},{1,0},{2,3},{3,2},{4,5},{5,4},{6,7},{7,6},{8,9},{9,8},{10,11... | collective-permute-start | bytes 1253384 | tf_op jit(solution)/shard_map/ppermute | solution.py:381
  47.9 7.3 %collective-permute-start.11 = (bf16[2,816,128]{2,1,0:T(8,128)(2,1)S(1)}, bf16[2,816,128]{2,1,0:T(8,128)(2,1)S(1)}, u32[]{:S(2)}, u32[]{:S(2)}) collective-permute-start(bf16[2,816,128]{2,1,0:T(8,128)(2,1)S(1)} %collective-permute-done.5.refs_2_), channel_id=1, source_target_pairs={{0,1},{1,0},{2,3},{3,2},{4,5},{5,4},{6,7},{7,6},{8,9},{9,8},{10,11... | collective-permute-start | bytes 1253384 | tf_op jit(solution)/shard_map/ppermute | solution.py:381
  48.0 8.2 %collective-permute-start.12 = (bf16[2,816,128]{2,1,0:T(8,128)(2,1)S(1)}, bf16[2,816,128]{2,1,0:T(8,128)(2,1)S(1)}, u32[]{:S(2)}, u32[]{:S(2)}) collective-permute-start(bf16[2,816,128]{2,1,0:T(8,128)(2,1)S(1)} %collective-permute-done.6.refs_3_), channel_id=1, source_target_pairs={{0,1},{1,0},{2,3},{3,2},{4,5},{5,4},{6,7},{7,6},{8,9},{9,8},{10,11... | collective-permute-start | bytes 1253384 | tf_op jit(solution)/shard_map/ppermute | solution.py:381
  48.4 12.8 %collective-permute-start.17 = (bf16[2,416,128]{2,1,0:T(8,128)(2,1)S(1)}, bf16[2,416,128]{2,1,0:T(8,128)(2,1)S(1)}, u32[]{:S(2)}, u32[]{:S(2)}) collective-permute-start(bf16[2,416,128]{2,1,0:T(8,128)(2,1)S(1)} %slice.110), channel_id=1, source_target_pairs={{0,192},{16,208},{32,224},{48,240},{64,0},{80,16},{96,32},{112,48}... | collective-permute-start | bytes 638984 | tf_op jit(solution)/shard_map/ppermute | solution.py:374
  52.2 13.8 %collective-permute-start.16 = (bf16[2,416,128]{2,1,0:T(8,128)(2,1)S(1)}, bf16[2,416,128]{2,1,0:T(8,128)(2,1)S(1)}, u32[]{:S(2)}, u32[]{:S(2)}) collective-permute-start(bf16[2,416,128]{2,1,0:T(8,128)(2,1)S(1)} %slice.109), channel_id=1, source_target_pairs={{0,64},{16,80},{32,96},{48,112},{64,128},{80,144},{96,160},{112,17... | collective-permute-start | bytes 638984 | tf_op jit(solution)/shard_map/ppermute | solution.py:374
  52.3 18.9 %collective-permute-start.13 = (bf16[512,128]{1,0:T(8,128)(2,1)S(1)}, bf16[512,128]{1,0:T(8,128)(2,1)S(1)}, u32[]{:S(2)}, u32[]{:S(2)}) collective-permute-start(bf16[512,128]{1,0:T(8,128)(2,1)S(1)} %copy-done.9), channel_id=1, source_target_pairs={{0,16},{16,0},{32,48},{48,32},{64,80},{80,64},{96,112},{112,96},{1... | collective-permute-start | bytes 393224 | tf_op jit(solution)/shard_map/ppermute | solution.py:376
  55.1 16.1 %collective-permute-start.14 = (bf16[512,128]{1,0:T(8,128)(2,1)S(1)}, bf16[512,128]{1,0:T(8,128)(2,1)S(1)}, u32[]{:S(2)}, u32[]{:S(2)}) collective-permute-start(bf16[512,128]{1,0:T(8,128)(2,1)S(1)} %copy-done.8), channel_id=1, source_target_pairs={{0,32},{16,48},{32,0},{48,16},{64,96},{80,112},{96,64},{112,80},{1... | collective-permute-start | bytes 393224 | tf_op jit(solution)/shard_map/ppermute | solution.py:376
  56.2 15.1 %collective-permute-start.15 = (bf16[512,128]{1,0:T(8,128)(2,1)S(1)}, bf16[512,128]{1,0:T(8,128)(2,1)S(1)}, u32[]{:S(2)}, u32[]{:S(2)}) collective-permute-start(bf16[512,128]{1,0:T(8,128)(2,1)S(1)} %copy-done.7), channel_id=1, source_target_pairs={{0,48},{16,32},{32,16},{48,0},{64,112},{80,96},{96,80},{112,64},{1... | collective-permute-start | bytes 393224 | tf_op jit(solution)/shard_map/ppermute | solution.py:376
  66.0 5.3 %copy-start.3 = (bf16[512,128]{1,0:T(8,128)(2,1)S(1)}, bf16[512,128]{1,0:T(8,128)(2,1)}, u32[]{:S(2)}) copy-start(bf16[512,128]{1,0:T(8,128)(2,1)} %get-tuple-element.57.og0) | copy-start | bytes 393220
  78.2 5.7 %copy-start.5 = (bf16[3840,128]{1,0:T(8,128)(2,1)S(1)}, bf16[3840,128]{1,0:T(8,128)(2,1)}, u32[]{:S(2)}) copy-start(bf16[3840,128]{1,0:T(8,128)(2,1)} %get-tuple-element.67) | copy-start | bytes 2949124
  78.2 46.8 %all-to-all-start = ((bf16[16,13,32,128]{3,2,1,0:T(8,128)(2,1)}), bf16[16,13,32,128]{3,2,1,0:T(8,128)(2,1)S(1)}, u32[]{:S(2)}, u32[]{:S(2)}) async-start(bf16[16,13,32,128]{3,2,1,0:T(8,128)(2,1)} %get-tuple-element.76), calls=%async_computation | async-start | bytes 3407872 | tf_op jit(solution)/shard_map/all_to_all | solution.py:396
  83.7 5.8 %collective-permute-start.18 = (bf16[7680,128]{1,0:T(8,128)(2,1)}, bf16[7680,128]{1,0:T(8,128)(2,1)}, u32[]{:S(2)}, u32[]{:S(2)}) collective-permute-start(bf16[7680,128]{1,0:T(8,128)(2,1)} %get-tuple-element.66.mine), channel_id=1, source_target_pairs={{0,1},{1,0},{2,3},{3,2},{4,5},{5,4},{6,7},{7,6},{8,9},{9,8},{10,11... | collective-permute-start | bytes 5898248 | tf_op jit(solution)/shard_map/ppermute | solution.py:398
  83.8 5.1 %collective-permute-start.19 = (bf16[3840,128]{1,0:T(8,128)(2,1)S(1)}, bf16[3840,128]{1,0:T(8,128)(2,1)S(1)}, u32[]{:S(2)}, u32[]{:S(2)}) collective-permute-start(bf16[3840,128]{1,0:T(8,128)(2,1)S(1)} %copy-done.5), channel_id=1, source_target_pairs={{0,1},{1,0},{2,3},{3,2},{4,5},{5,4},{6,7},{7,6},{8,9},{9,8},{10,11... | collective-permute-start | bytes 2949128 | tf_op jit(solution)/shard_map/ppermute | solution.py:394
  88.9 0.9 copy-start.6
  97.3 16.1 %collective-permute-start.20 = (bf16[2,2,144,256]{3,2,1,0:T(8,128)(2,1)}, bf16[2,2,144,256]{3,2,1,0:T(8,128)(2,1)S(1)}, u32[]{:S(2)}, u32[]{:S(2)}) collective-permute-start(bf16[2,2,144,256]{3,2,1,0:T(8,128)(2,1)} %get-tuple-element.71), channel_id=1, source_target_pairs={{0,4},{1,5},{2,6},{3,7},{4,8},{5,9},{6,10},{7,11},{8,12},{9,13},{1... | collective-permute-start | bytes 884744 | tf_op jit(solution)/shard_map/ppermute | solution.py:401
  100.0 13.4 %collective-permute-start.21 = (bf16[2,2,144,256]{3,2,1,0:T(8,128)(2,1)}, bf16[2,2,144,256]{3,2,1,0:T(8,128)(2,1)S(1)}, u32[]{:S(2)}, u32[]{:S(2)}) collective-permute-start(bf16[2,2,144,256]{3,2,1,0:T(8,128)(2,1)} %get-tuple-element.72), channel_id=1, source_target_pairs={{0,8},{1,9},{2,10},{3,11},{4,12},{5,13},{6,14},{7,15},{8,0},{9,1},... | collective-permute-start | bytes 884744 | tf_op jit(solution)/shard_map/ppermute | solution.py:401
  100.2 16.5 %collective-permute-start.22 = (bf16[2,2,144,256]{3,2,1,0:T(8,128)(2,1)}, bf16[2,2,144,256]{3,2,1,0:T(8,128)(2,1)S(1)}, u32[]{:S(2)}, u32[]{:S(2)}) collective-permute-start(bf16[2,2,144,256]{3,2,1,0:T(8,128)(2,1)} %get-tuple-element.73), channel_id=1, source_target_pairs={{0,12},{1,13},{2,14},{3,15},{4,0},{5,1},{6,2},{7,3},{8,4},{9,5},{1... | collective-permute-start | bytes 884744 | tf_op jit(solution)/shard_map/ppermute | solution.py:401
  100.9 33.7 %collective-permute-start.25 = (bf16[4,2,144,256]{3,2,1,0:T(8,128)(2,1)}, bf16[4,2,144,256]{3,2,1,0:T(8,128)(2,1)S(1)}, u32[]{:S(2)}, u32[]{:S(2)}) collective-permute-start(bf16[4,2,144,256]{3,2,1,0:T(8,128)(2,1)} %get-tuple-element.75), channel_id=1, source_target_pairs={{0,2},{1,3},{2,0},{3,1},{4,6},{5,7},{6,4},{7,5},{8,10},{9,11},{10,... | collective-permute-start | bytes 1769480 | tf_op jit(solution)/shard_map/ppermute | solution.py:400
  118.4 16.3 %copy-start.4 = (bf16[4,2,144,256]{3,2,1,0:T(8,128)(2,1)S(1)}, bf16[4,2,144,256]{3,2,1,0:T(8,128)(2,1)}, u32[]{:S(2)}) copy-start(bf16[4,2,144,256]{3,2,1,0:T(8,128)(2,1)} %get-tuple-element.74) | copy-start | bytes 1769476
  118.4 15.3 %collective-permute-start.23 = (bf16[2,144,256]{2,1,0:T(8,128)(2,1)}, bf16[2,144,256]{2,1,0:T(8,128)(2,1)}, u32[]{:S(2)}, u32[]{:S(2)}) collective-permute-start(bf16[2,144,256]{2,1,0:T(8,128)(2,1)} %fusion.9), channel_id=1, source_target_pairs={{0,2},{1,3},{2,0},{3,1},{4,6},{5,7},{6,4},{7,5},{8,10},{9,11},{10,... | collective-permute-start | bytes 442376 | tf_op jit(solution)/shard_map/ppermute | solution.py:403
  126.0 25.3 %all-to-all-start.1 = ((bf16[16,4,32,128]{3,2,1,0:T(8,128)(2,1)}), bf16[16,4,32,128]{3,2,1,0:T(8,128)(2,1)S(1)}, u32[]{:S(2)}, u32[]{:S(2)}) async-start(bf16[16,4,32,128]{3,2,1,0:T(8,128)(2,1)} %block_strips.1), calls=%async_computation.1 | async-start | bytes 1048576 | tf_op jit(solution)/shard_map/all_to_all | solution.py:410
  134.8 7.6 %collective-permute-start.26 = (bf16[2,144,256]{2,1,0:T(8,128)(2,1)S(1)}, bf16[2,144,256]{2,1,0:T(8,128)(2,1)S(1)}, u32[]{:S(2)}, u32[]{:S(2)}) collective-permute-start(bf16[2,144,256]{2,1,0:T(8,128)(2,1)S(1)} %get-tuple-element.85), channel_id=1, source_target_pairs={{0,4},{1,5},{2,6},{3,7},{4,8},{5,9},{6,10},{7,11},{8,12},{9,13},{1... | collective-permute-start | bytes 442376 | tf_op jit(solution)/shard_map/ppermute | solution.py:405
  137.3 8.7 %collective-permute-start.28 = (bf16[2,144,256]{2,1,0:T(8,128)(2,1)S(1)}, bf16[2,144,256]{2,1,0:T(8,128)(2,1)S(1)}, u32[]{:S(2)}, u32[]{:S(2)}) collective-permute-start(bf16[2,144,256]{2,1,0:T(8,128)(2,1)S(1)} %get-tuple-element.86), channel_id=1, source_target_pairs={{0,12},{1,13},{2,14},{3,15},{4,0},{5,1},{6,2},{7,3},{8,4},{9,5},{1... | collective-permute-start | bytes 442376 | tf_op jit(solution)/shard_map/ppermute | solution.py:405
  137.3 8.7 %collective-permute-start.27 = (bf16[2,144,256]{2,1,0:T(8,128)(2,1)S(1)}, bf16[2,144,256]{2,1,0:T(8,128)(2,1)S(1)}, u32[]{:S(2)}, u32[]{:S(2)}) collective-permute-start(bf16[2,144,256]{2,1,0:T(8,128)(2,1)S(1)} %get-tuple-element.87), channel_id=1, source_target_pairs={{0,8},{1,9},{2,10},{3,11},{4,12},{5,13},{6,14},{7,15},{8,0},{9,1},... | collective-permute-start | bytes 442376 | tf_op jit(solution)/shard_map/ppermute | solution.py:405
  138.9 14.5 %collective-permute-start.24 = (bf16[144,256]{1,0:T(8,128)(2,1)S(1)}, bf16[144,256]{1,0:T(8,128)(2,1)S(1)}, u32[]{:S(2)}, u32[]{:S(2)}) collective-permute-start(bf16[144,256]{1,0:T(8,128)(2,1)S(1)} %get-tuple-element.92), channel_id=1, source_target_pairs={{0,16},{16,0},{32,48},{48,32},{64,80},{80,64},{96,112},{112,96},{1... | collective-permute-start | bytes 221192 | tf_op jit(solution)/shard_map/ppermute | solution.py:408
  146.2 7.2 %collective-permute-start.30 = (bf16[144,256]{1,0:T(8,128)(2,1)S(1)}, bf16[144,256]{1,0:T(8,128)(2,1)S(1)}, u32[]{:S(2)}, u32[]{:S(2)}) collective-permute-start(bf16[144,256]{1,0:T(8,128)(2,1)S(1)} %get-tuple-element.90), channel_id=1, source_target_pairs={{0,48},{16,32},{32,16},{48,0},{64,112},{80,96},{96,80},{112,64},{1... | collective-permute-start | bytes 221192 | tf_op jit(solution)/shard_map/ppermute | solution.py:408
  149.9 4.5 %collective-permute-start.29 = (bf16[144,256]{1,0:T(8,128)(2,1)S(1)}, bf16[144,256]{1,0:T(8,128)(2,1)S(1)}, u32[]{:S(2)}, u32[]{:S(2)}) collective-permute-start(bf16[144,256]{1,0:T(8,128)(2,1)S(1)} %get-tuple-element.91), channel_id=1, source_target_pairs={{0,32},{16,48},{32,0},{48,16},{64,96},{80,112},{96,64},{112,80},{1... | collective-permute-start | bytes 221192 | tf_op jit(solution)/shard_map/ppermute | solution.py:408

commit v5 on v4

--- a/solution.py
+++ b/solution.py
@@ -377,7 +377,7 @@
     near = jnp.concatenate([part[:272] for part in parts], axis=0)
     near = jnp.stack([near, lax.ppermute(near, "head", ACROSS_Y)])
     lats = [near] + [lax.ppermute(near, "head", ALONG_X[k]) for k in (1, 2, 3)]
-    lats, _ = lax.optimization_barrier((lats, (from_down, from_up)))
+    lats, far = lax.optimization_barrier((lats, far))
     lats = lats + [lax.ppermute(lat, "head", OTHER_CORE) for lat in lats]
 
     rows = (shape((1024, 1536), BF16), shape((1024, 512), BF16), shape((1024, ROPE), BF16))

time: 156 us -> 157 us (level)
    ppermute x1, waiting for transfers between devices: 3.83 us -> 0.01 us  [per_device(): from_down = lax.ppermute(w, 'dp', GROUP_UP)]
    all_to_all x1, waiting for transfers between devices: 6.38 us -> 10.1 us  [per_device(): terms = lax.all_to_all(terms, 'dp', 0, 0, tiled=True)]
    ppermute x1, waiting for transfers between devices: 2.58 us -> 6.03 us  [per_device(): lax.ppermute(from_up[2:], 'dp', GROUP_DOWN)]
where the time goes in v5:
time: 157 us
  waiting for transfers between devices  68 us (43%)
  starting transfers between devices  54.5 us (35%)
  Pallas kernels  27.2 us (17%)
  other arithmetic  3.87 us (2%)
  local copies, waits for them, and re-layouts  2.36 us (2%)
    pallas_call x6, Pallas kernels, call(): pl.pallas_call(kernel, out_shape=out_shape, in_specs=specs if in_specs is...  19.7 us
    ppermute x6, waiting for transfers between devices, per_device(): lax.ppermute(parts[k], 'head', ALONG_X[k])  17.7 us
    ppermute x1, waiting for transfers between devices, per_device(): from_up = lax.ppermute(w, 'dp', GROUP_DOWN)  12.8 us
    all_to_all x1, waiting for transfers between devices, per_device(): terms = lax.all_to_all(terms, 'dp', 0, 0, tiled=True)  10.1 us
    ppermute x3, waiting for transfers between devices, per_device(): parts = [lax.ppermute(sends[s - 1], 'dp', PARTNER[s]) for s in (1, 2, 3)]  8.18 us
    ppermute x3, starting transfers between devices, per_device(): lax.ppermute(part[s], 'dp', PARTNER[s])  8.06 us
    ppermute x6, starting transfers between devices, per_device(): lax.ppermute(parts[k], 'head', ALONG_X[k])  7.58 us
    pallas_call x1, Pallas kernels, latent_grad_call(): pl.pallas_call(latent_grad_kernel, out_shape=[jax.ShapeDtypeStruct((2, 2,...  7.46 us
  transfers between devices with their start and end apart: 33, of which 15 were waited for; matrix products, arithmetic and copies ran while one was open for 3% of the time, Pallas kernels for 11%

profile of v5, /device:TPU:6, one launch (start us, length us, event | category | flops | bytes accessed | tf_op | source)
XLA Modules:
  0.0 156.9 jit_solution(11921547397343694230)
XLA Ops:
  0.7 0.6 pad_add_fusion.pos
  1.2 3.2 %send_rows.1 = (bf16[688,128]{1,0:T(8,128)(2,1)}, bf16[688,128]{1,0:T(8,128)(2,1)}, bf16[688,128]{1,0:T(8,128)(2,1)}, bf16[416,128]{1,0:T(8,128)(2,1)}, bf16[512...) custom-call(s32[4]{0:T(128)} %pad_add_fusion.pos, ...), custom_call_target="tpu_custom_call" | custom-call | bytes 4000000 | tf_op jit(solution)/shard_map/send_rows/pallas_call | solution.py:94
  4.5 3.3 %collective-permute-start = (bf16[688,128]{1,0:T(8,128)(2,1)}, bf16[688,128]{1,0:T(8,128)(2,1)S(1)}, u32[]{:S(2)}, u32[]{:S(2)}) collective-permute-start(bf16[688,128]{1,0:T(8,128)(2,1)} %get-tuple-element.48), channel_id=1, source_target_pairs={{0,16},{16,0},{32,48},{48,32},{64,80},{80,64},{96,112},{112,96},{1... | collective-permute-start | bytes 528392 | tf_op jit(solution)/shard_map/ppermute | solution.py:370
  7.7 1.9 %collective-permute-start.1 = (bf16[688,128]{1,0:T(8,128)(2,1)}, bf16[688,128]{1,0:T(8,128)(2,1)S(1)}, u32[]{:S(2)}, u32[]{:S(2)}) collective-permute-start(bf16[688,128]{1,0:T(8,128)(2,1)} %get-tuple-element.49), channel_id=1, source_target_pairs={{0,32},{16,48},{32,0},{48,16},{64,96},{80,112},{96,64},{112,80},{1... | collective-permute-start | bytes 528392 | tf_op jit(solution)/shard_map/ppermute | solution.py:370
  9.7 2.8 %collective-permute-done = bf16[688,128]{1,0:T(8,128)(2,1)S(1)} collective-permute-done((bf16[688,128]{1,0:T(8,128)(2,1)}, bf16[688,128]{1,0:T(8,128)(2,1)S(1)}, u32[]{:S(2)}, u32[]{:S(2)}) %collective-permute-start) | collective-permute-done | bytes 176160 | tf_op jit(solution)/shard_map/ppermute | solution.py:370
  12.5 2.8 %collective-permute-done.1 = bf16[688,128]{1,0:T(8,128)(2,1)S(1)} collective-permute-done((bf16[688,128]{1,0:T(8,128)(2,1)}, bf16[688,128]{1,0:T(8,128)(2,1)S(1)}, u32[]{:S(2)}, u32[]{:S(2)}) %collective-permute-start.1) | collective-permute-done | bytes 176160 | tf_op jit(solution)/shard_map/ppermute | solution.py:370
  15.4 0.0 copy-start
  15.4 0.0 copy-start.1
  15.4 2.5 %collective-permute-done.2 = bf16[688,128]{1,0:T(8,128)(2,1)S(1)} collective-permute-done((bf16[688,128]{1,0:T(8,128)(2,1)}, bf16[688,128]{1,0:T(8,128)(2,1)S(1)}, u32[]{:S(2)}, u32[]{:S(2)}) %collective-permute-start.2) | collective-permute-done | bytes 176160 | tf_op jit(solution)/shard_map/ppermute | solution.py:370
  18.0 1.3 collective-permute-start.3
  19.3 1.0 pad_maximum_fusion.w0
  20.3 6.2 %collective-permute-start.9 = (bf16[4,416,128]{2,1,0:T(8,128)(2,1)S(1)}, bf16[4,416,128]{2,1,0:T(8,128)(2,1)S(1)}, u32[]{:S(2)}, u32[]{:S(2)}) collective-permute-start(bf16[4,416,128]{2,1,0:T(8,128)(2,1)S(1)} %pad_maximum_fusion.w0), channel_id=1, source_target_pairs={{0,192},{16,208},{32,224},{48,240},{64,0},{80,16},{96,32},{112,48}... | collective-permute-start | bytes 1277960 | tf_op jit(solution)/shard_map/ppermute | solution.py:373
  26.6 0.9 collective-permute-start.6
  27.5 1.1 collective-permute-start.5
  28.6 2.1 %collective-permute-start.4 = (bf16[2,816,128]{2,1,0:T(8,128)(2,1)S(1)}, bf16[2,816,128]{2,1,0:T(8,128)(2,1)S(1)}, u32[]{:S(2)}, u32[]{:S(2)}) collective-permute-start(bf16[2,816,128]{2,1,0:T(8,128)(2,1)S(1)} %pad_maximum_fusion.1.refs_0_), channel_id=1, source_target_pairs={{0,4},{1,5},{2,6},{3,7},{4,8},{5,9},{6,10},{7,11},{8,12},{9,13},{1... | collective-permute-start | bytes 1253384 | tf_op jit(solution)/shard_map/ppermute | solution.py:379
  30.7 12.8 %collective-permute-done.9.w2 = bf16[4,416,128]{2,1,0:T(8,128)(2,1)S(1)} collective-permute-done((bf16[4,416,128]{2,1,0:T(8,128)(2,1)S(1)}, bf16[4,416,128]{2,1,0:T(8,128)(2,1)S(1)}, u32[]{:S(2)}, u32[]{:S(2)}) %collective-permute-start.9) | collective-permute-done | bytes 426016 | tf_op jit(solution)/shard_map/ppermute | solution.py:373
  43.5 4.7 %collective-permute-start.10 = (bf16[2,416,128]{2,1,0:T(8,128)(2,1)S(1)}, bf16[2,416,128]{2,1,0:T(8,128)(2,1)S(1)}, u32[]{:S(2)}, u32[]{:S(2)}) collective-permute-start(bf16[2,416,128]{2,1,0:T(8,128)(2,1)S(1)} %slice.110), channel_id=1, source_target_pairs={{0,192},{16,208},{32,224},{48,240},{64,0},{80,16},{96,32},{112,48}... | collective-permute-start | bytes 638984 | tf_op jit(solution)/shard_map/ppermute | solution.py:374
  48.2 0.1 collective-permute-start.8
  48.3 6.0 %collective-permute-done.10.w4 = bf16[2,416,128]{2,1,0:T(8,128)(2,1)S(1)} collective-permute-done((bf16[2,416,128]{2,1,0:T(8,128)(2,1)S(1)}, bf16[2,416,128]{2,1,0:T(8,128)(2,1)S(1)}, u32[]{:S(2)}, u32[]{:S(2)}) %collective-permute-start.10) | collective-permute-done | bytes 213024 | tf_op jit(solution)/shard_map/ppermute | solution.py:374
  54.4 4.7 %collective-permute-done.8.w3 = bf16[2,416,128]{2,1,0:T(8,128)(2,1)S(1)} collective-permute-done((bf16[2,416,128]{2,1,0:T(8,128)(2,1)S(1)}, bf16[2,416,128]{2,1,0:T(8,128)(2,1)S(1)}, u32[]{:S(2)}, u32[]{:S(2)}) %collective-permute-start.8) | collective-permute-done | bytes 213024 | tf_op jit(solution)/shard_map/ppermute | solution.py:374
  59.1 0.5 collective-permute-start.12
  59.6 0.0 collective-permute-start.13
  59.6 0.5 collective-permute-start.14
  60.1 3.3 %collective-permute-start.15 = (bf16[512,128]{1,0:T(8,128)(2,1)S(1)}, bf16[512,128]{1,0:T(8,128)(2,1)S(1)}, u32[]{:S(2)}, u32[]{:S(2)}) collective-permute-start(bf16[512,128]{1,0:T(8,128)(2,1)S(1)} %copy-done.9), channel_id=1, source_target_pairs={{0,16},{16,0},{32,48},{48,32},{64,80},{80,64},{96,112},{112,96},{1... | collective-permute-start | bytes 393224 | tf_op jit(solution)/shard_map/ppermute | solution.py:376
  63.4 2.2 %collective-permute-start.17 = (bf16[512,128]{1,0:T(8,128)(2,1)S(1)}, bf16[512,128]{1,0:T(8,128)(2,1)S(1)}, u32[]{:S(2)}, u32[]{:S(2)}) collective-permute-start(bf16[512,128]{1,0:T(8,128)(2,1)S(1)} %copy-done.7), channel_id=1, source_target_pairs={{0,48},{16,32},{32,16},{48,0},{64,112},{80,96},{96,80},{112,64},{1... | collective-permute-start | bytes 393224 | tf_op jit(solution)/shard_map/ppermute | solution.py:376
  65.6 1.2 latent_rows.1
  66.9 5.2 %projections.1 = (bf16[1024,384]{1,0:T(8,128)(2,1)S(1)}, bf16[1024,512]{1,0:T(8,128)(2,1)S(1)}, bf16[768,384]{1,0:T(8,128)(2,1)}, bf16[384,512]{1,0:T(8,128)(2,1)}, bf16[3840,128]{1,0:T(8,128)(2,1)}) custom-call(s32[4]{0:T(128)S(1)} %copy-done.2, bf16[1024,1536]{1,0:T(8,128)(2,1)S(1)} %get-tuple-element.56.lq, bf16[1024,512]{1,0:T(8,128)(2,1)S(1)} %get-tuple-element.57.lk, ...), custom_call_target="tpu_custom_call" | custom-call | flops 1800000000 | bytes 12000000 | tf_op jit(solution)/shard_map/projections/pallas_call | solution.py:94
  72.2 6.9 %mla_backward.1 = (bf16[16,13,32,128]{3,2,1,0:T(8,128)(2,1)}, bf16[7680,128]{1,0:T(8,128)(2,1)}) custom-call(bf16[1024,1536]{1,0:T(8,128)(2,1)S(1)} %get-tuple-element.56.lq, bf16[1024,512]{1,0:T(8,128)(2,1)S(1)} %get-tuple-element.57.lk, bf16[1024,64]{1,0:T(8,128)(2,1)S(1)} %get-tuple-element.58.rope, bf16[512,128]{1,0:T(8,128)(2,1)S(1)} %copy-done.3, ...), custom_call_target="tpu_custom_call" | custom-call | flops 2700000000 | bytes 12000000 | tf_op jit(solution)/shard_map/mla_backward/pallas_call | solution.py:94
  79.1 0.0 copy-start.5
  79.1 6.2 %all-to-all-start = ((bf16[16,13,32,128]{3,2,1,0:T(8,128)(2,1)}), bf16[16,13,32,128]{3,2,1,0:T(8,128)(2,1)S(1)}, u32[]{:S(2)}, u32[]{:S(2)}) async-start(bf16[16,13,32,128]{3,2,1,0:T(8,128)(2,1)} %get-tuple-element.80), calls=%async_computation | async-start | bytes 3407872 | tf_op jit(solution)/shard_map/all_to_all | solution.py:396
  85.3 0.1 collective-permute-start.18
  85.4 0.5 collective-permute-start.19
  85.9 4.6 %collective-permute-done.19.w_other = bf16[3840,128]{1,0:T(8,128)(2,1)S(1)} collective-permute-done((bf16[3840,128]{1,0:T(8,128)(2,1)S(1)}, bf16[3840,128]{1,0:T(8,128)(2,1)S(1)}, u32[]{:S(2)}, u32[]{:S(2)}) %collective-permute-start.19) | collective-permute-done | bytes 983072 | tf_op jit(solution)/shard_map/ppermute | solution.py:394
  90.5 0.6 collective-permute-done.18.other
  91.1 0.3 copy-done.6
  91.5 7.5 %latent_grads.1 = (bf16[2,2,144,256]{3,2,1,0:T(8,128)(2,1)}, bf16[2,2,144,256]{3,2,1,0:T(8,128)(2,1)}, bf16[2,2,144,256]{3,2,1,0:T(8,128)(2,1)}, bf16[2,2,144,25...) custom-call(s32[4]{0:T(128)} %pad_add_fusion.pos, ...), custom_call_target="tpu_custom_call" | custom-call | flops 1800000000 | bytes 12000000 | tf_op jit(solution)/shard_map/latent_grads/pallas_call | solution.py:295
  98.9 0.5 collective-permute-start.20
  99.5 2.4 %collective-permute-start.21 = (bf16[2,2,144,256]{3,2,1,0:T(8,128)(2,1)}, bf16[2,2,144,256]{3,2,1,0:T(8,128)(2,1)S(1)}, u32[]{:S(2)}, u32[]{:S(2)}) collective-permute-start(bf16[2,2,144,256]{3,2,1,0:T(8,128)(2,1)} %get-tuple-element.76), channel_id=1, source_target_pairs={{0,8},{1,9},{2,10},{3,11},{4,12},{5,13},{6,14},{7,15},{8,0},{9,1},... | collective-permute-start | bytes 884744 | tf_op jit(solution)/shard_map/ppermute | solution.py:401
  101.9 0.1 collective-permute-start.25
  102.0 7.0 %collective-permute-done.20 = bf16[2,2,144,256]{3,2,1,0:T(8,128)(2,1)S(1)} collective-permute-done((bf16[2,2,144,256]{3,2,1,0:T(8,128)(2,1)}, bf16[2,2,144,256]{3,2,1,0:T(8,128)(2,1)S(1)}, u32[]{:S(2)}, u32[]{:S(2)}) %collective-permute-start.20) | collective-permute-done | bytes 294944 | tf_op jit(solution)/shard_map/ppermute | solution.py:401
  109.0 2.1 %collective-permute-done.21 = bf16[2,2,144,256]{3,2,1,0:T(8,128)(2,1)S(1)} collective-permute-done((bf16[2,2,144,256]{3,2,1,0:T(8,128)(2,1)}, bf16[2,2,144,256]{3,2,1,0:T(8,128)(2,1)S(1)}, u32[]{:S(2)}, u32[]{:S(2)}) %collective-permute-start.21) | collective-permute-done | bytes 294944 | tf_op jit(solution)/shard_map/ppermute | solution.py:401
  111.1 5.3 %collective-permute-done.22 = bf16[2,2,144,256]{3,2,1,0:T(8,128)(2,1)S(1)} collective-permute-done((bf16[2,2,144,256]{3,2,1,0:T(8,128)(2,1)}, bf16[2,2,144,256]{3,2,1,0:T(8,128)(2,1)S(1)}, u32[]{:S(2)}, u32[]{:S(2)}) %collective-permute-start.22) | collective-permute-done | bytes 294944 | tf_op jit(solution)/shard_map/ppermute | solution.py:401
  116.4 1.1 convert_add_fusion
  117.5 0.7 fusion.9
  118.2 0.1 collective-permute-start.23
  118.3 10.1 %all-to-all-done.terms = bf16[16,13,32,128]{3,2,1,0:T(8,128)(2,1)S(1)} async-done(((bf16[16,13,32,128]{3,2,1,0:T(8,128)(2,1)}), bf16[16,13,32,128]{3,2,1,0:T(8,128)(2,1)S(1)}, u32[]{:S(2)}, u32[]{:S(2)}) %all-to-all-start) | async-done | bytes 1703968 | tf_op jit(solution)/shard_map/all_to_all | solution.py:396
  128.5 1.0 block_strips.1
  129.5 3.6 %all-to-all-start.1 = ((bf16[16,4,32,128]{3,2,1,0:T(8,128)(2,1)}), bf16[16,4,32,128]{3,2,1,0:T(8,128)(2,1)S(1)}, u32[]{:S(2)}, u32[]{:S(2)}) async-start(bf16[16,4,32,128]{3,2,1,0:T(8,128)(2,1)} %block_strips.1), calls=%async_computation.1 | async-start | bytes 1048576 | tf_op jit(solution)/shard_map/all_to_all | solution.py:410
  133.1 2.1 %collective-permute-done.23 = bf16[2,144,256]{2,1,0:T(8,128)(2,1)} collective-permute-done((bf16[2,144,256]{2,1,0:T(8,128)(2,1)}, bf16[2,144,256]{2,1,0:T(8,128)(2,1)}, u32[]{:S(2)}, u32[]{:S(2)}) %collective-permute-start.23) | collective-permute-done | bytes 147488 | tf_op jit(solution)/shard_map/ppermute | solution.py:403
  135.2 0.9 fusion.1
  136.2 0.1 fusion.6
  136.3 2.0 %collective-permute-start.26 = (bf16[2,144,256]{2,1,0:T(8,128)(2,1)S(1)}, bf16[2,144,256]{2,1,0:T(8,128)(2,1)S(1)}, u32[]{:S(2)}, u32[]{:S(2)}) collective-permute-start(bf16[2,144,256]{2,1,0:T(8,128)(2,1)S(1)} %get-tuple-element.89), channel_id=1, source_target_pairs={{0,4},{1,5},{2,6},{3,7},{4,8},{5,9},{6,10},{7,11},{8,12},{9,13},{1... | collective-permute-start | bytes 442376 | tf_op jit(solution)/shard_map/ppermute | solution.py:405
  138.3 0.1 collective-permute-start.28
  138.4 2.5 %collective-permute-start.27 = (bf16[2,144,256]{2,1,0:T(8,128)(2,1)S(1)}, bf16[2,144,256]{2,1,0:T(8,128)(2,1)S(1)}, u32[]{:S(2)}, u32[]{:S(2)}) collective-permute-start(bf16[2,144,256]{2,1,0:T(8,128)(2,1)S(1)} %get-tuple-element.91), channel_id=1, source_target_pairs={{0,8},{1,9},{2,10},{3,11},{4,12},{5,13},{6,14},{7,15},{8,0},{9,1},... | collective-permute-start | bytes 442376 | tf_op jit(solution)/shard_map/ppermute | solution.py:405
  140.9 3.4 %collective-permute-start.24 = (bf16[144,256]{1,0:T(8,128)(2,1)S(1)}, bf16[144,256]{1,0:T(8,128)(2,1)S(1)}, u32[]{:S(2)}, u32[]{:S(2)}) collective-permute-start(bf16[144,256]{1,0:T(8,128)(2,1)S(1)} %get-tuple-element.96), channel_id=1, source_target_pairs={{0,16},{16,0},{32,48},{48,32},{64,80},{80,64},{96,112},{112,96},{1... | collective-permute-start | bytes 221192 | tf_op jit(solution)/shard_map/ppermute | solution.py:408
  144.3 3.3 %collective-permute-done.28 = bf16[2,144,256]{2,1,0:T(8,128)(2,1)S(1)} collective-permute-done((bf16[2,144,256]{2,1,0:T(8,128)(2,1)S(1)}, bf16[2,144,256]{2,1,0:T(8,128)(2,1)S(1)}, u32[]{:S(2)}, u32[]{:S(2)}) %collective-permute-start.28) | collective-permute-done | bytes 147488 | tf_op jit(solution)/shard_map/ppermute | solution.py:405
  147.6 0.1 fusion.4
  147.7 3.5 %collective-permute-start.30 = (bf16[144,256]{1,0:T(8,128)(2,1)S(1)}, bf16[144,256]{1,0:T(8,128)(2,1)S(1)}, u32[]{:S(2)}, u32[]{:S(2)}) collective-permute-start(bf16[144,256]{1,0:T(8,128)(2,1)S(1)} %get-tuple-element.94), channel_id=1, source_target_pairs={{0,48},{16,32},{32,16},{48,0},{64,112},{80,96},{96,80},{112,64},{1... | collective-permute-start | bytes 221192 | tf_op jit(solution)/shard_map/ppermute | solution.py:408
  151.3 1.2 collective-permute-start.29
  152.4 2.1 %owner_grams.1 = (f32[512,512]{1,0:T(8,128)}, f32[512,512]{1,0:T(8,128)}, f32[512,512]{1,0:T(8,128)}) custom-call(bf16[16,4,32,128]{3,2,1,0:T(8,128)(2,1)S(1)} %all-to-all-done.1.strips), custom_call_target="tpu_custom_call" | custom-call | flops 540000000 | bytes 4000000 | tf_op jit(solution)/shard_map/owner_grams/pallas_call | solution.py:94
  154.6 0.0 collective-permute-done.30
  154.6 1.0 collective-permute-done.29
  155.7 0.6 slice_bitcast_fusion.9
  156.3 0.6 slice_bitcast_fusion.8
  (51 shorter events, 0.3 us)
Async XLA Ops:
  4.5 8.0 %collective-permute-start = (bf16[688,128]{1,0:T(8,128)(2,1)}, bf16[688,128]{1,0:T(8,128)(2,1)S(1)}, u32[]{:S(2)}, u32[]{:S(2)}) collective-permute-start(bf16[688,128]{1,0:T(8,128)(2,1)} %get-tuple-element.48), channel_id=1, source_target_pairs={{0,16},{16,0},{32,48},{48,32},{64,80},{80,64},{96,112},{112,96},{1... | collective-permute-start | bytes 528392 | tf_op jit(solution)/shard_map/ppermute | solution.py:370
  7.7 7.6 %collective-permute-start.1 = (bf16[688,128]{1,0:T(8,128)(2,1)}, bf16[688,128]{1,0:T(8,128)(2,1)S(1)}, u32[]{:S(2)}, u32[]{:S(2)}) collective-permute-start(bf16[688,128]{1,0:T(8,128)(2,1)} %get-tuple-element.49), channel_id=1, source_target_pairs={{0,32},{16,48},{32,0},{48,16},{64,96},{80,112},{96,64},{112,80},{1... | collective-permute-start | bytes 528392 | tf_op jit(solution)/shard_map/ppermute | solution.py:370
  9.7 8.3 %collective-permute-start.2 = (bf16[688,128]{1,0:T(8,128)(2,1)}, bf16[688,128]{1,0:T(8,128)(2,1)S(1)}, u32[]{:S(2)}, u32[]{:S(2)}) collective-permute-start(bf16[688,128]{1,0:T(8,128)(2,1)} %get-tuple-element.50), channel_id=1, source_target_pairs={{0,48},{16,32},{32,16},{48,0},{64,112},{80,96},{96,80},{112,64},{1... | collective-permute-start | bytes 528392 | tf_op jit(solution)/shard_map/ppermute | solution.py:370
  15.3 44.8 %copy-start.9 = (bf16[512,128]{1,0:T(8,128)(2,1)S(1)}, bf16[512,128]{1,0:T(8,128)(2,1)}, u32[]{:S(2)}) copy-start(bf16[512,128]{1,0:T(8,128)(2,1)} %get-tuple-element.63) | copy-start | bytes 393220
  15.3 48.1 %copy-start.8 = (bf16[512,128]{1,0:T(8,128)(2,1)S(1)}, bf16[512,128]{1,0:T(8,128)(2,1)}, u32[]{:S(2)}) copy-start(bf16[512,128]{1,0:T(8,128)(2,1)} %get-tuple-element.64) | copy-start | bytes 393220
  15.3 48.1 %copy-start.7 = (bf16[512,128]{1,0:T(8,128)(2,1)S(1)}, bf16[512,128]{1,0:T(8,128)(2,1)}, u32[]{:S(2)}) copy-start(bf16[512,128]{1,0:T(8,128)(2,1)} %get-tuple-element.65) | copy-start | bytes 393220
  15.4 50.3 %copy-start = (bf16[256,1536]{1,0:T(8,128)(2,1)S(1)}, bf16[256,1536]{1,0:T(8,128)(2,1)}, u32[]{:S(2)}) copy-start(bf16[256,1536]{1,0:T(8,128)(2,1)} %ql.1) | copy-start | bytes 2359300
  15.4 50.3 %copy-start.1 = (bf16[256,576]{1,0:T(8,128)(2,1)S(1)}, bf16[256,576]{1,0:T(8,128)(2,1)}, u32[]{:S(2)}) copy-start(bf16[256,576]{1,0:T(8,128)(2,1)} %get-tuple-element.47.kl) | copy-start | bytes 884740
  15.4 50.2 %copy-start.2 = (s32[4]{0:T(128)S(1)}, s32[4]{0:T(128)}, u32[]{:S(2)}) copy-start(s32[4]{0:T(128)} %pad_add_fusion.pos) | copy-start | bytes 52
  18.0 8.6 %collective-permute-start.3 = (bf16[816,128]{1,0:T(8,128)(2,1)S(1)}, bf16[816,128]{1,0:T(8,128)(2,1)S(1)}, u32[]{:S(2)}, u32[]{:S(2)}) collective-permute-start(bf16[816,128]{1,0:T(8,128)(2,1)S(1)} %get-tuple-element.93), channel_id=1, source_target_pairs={{0,2},{1,3},{2,0},{3,1},{4,6},{5,7},{6,4},{7,5},{8,10},{9,11},{10,... | collective-permute-start | bytes 626696 | tf_op jit(solution)/shard_map/ppermute | solution.py:378
  20.3 23.1 %collective-permute-start.9 = (bf16[4,416,128]{2,1,0:T(8,128)(2,1)S(1)}, bf16[4,416,128]{2,1,0:T(8,128)(2,1)S(1)}, u32[]{:S(2)}, u32[]{:S(2)}) collective-permute-start(bf16[4,416,128]{2,1,0:T(8,128)(2,1)S(1)} %pad_maximum_fusion.w0), channel_id=1, source_target_pairs={{0,192},{16,208},{32,224},{48,240},{64,0},{80,16},{96,32},{112,48}... | collective-permute-start | bytes 1277960 | tf_op jit(solution)/shard_map/ppermute | solution.py:373
  26.5 21.7 %collective-permute-start.7 = (bf16[4,416,128]{2,1,0:T(8,128)(2,1)S(1)}, bf16[4,416,128]{2,1,0:T(8,128)(2,1)S(1)}, u32[]{:S(2)}, u32[]{:S(2)}) collective-permute-start(bf16[4,416,128]{2,1,0:T(8,128)(2,1)S(1)} %pad_maximum_fusion.w0), channel_id=1, source_target_pairs={{0,64},{16,80},{32,96},{48,112},{64,128},{80,144},{96,160},{112,17... | collective-permute-start | bytes 1277960 | tf_op jit(solution)/shard_map/ppermute | solution.py:372
  26.6 21.8 %collective-permute-start.6 = (bf16[2,816,128]{2,1,0:T(8,128)(2,1)S(1)}, bf16[2,816,128]{2,1,0:T(8,128)(2,1)S(1)}, u32[]{:S(2)}, u32[]{:S(2)}) collective-permute-start(bf16[2,816,128]{2,1,0:T(8,128)(2,1)S(1)} %pad_maximum_fusion.1.refs_0_), channel_id=1, source_target_pairs={{0,12},{1,13},{2,14},{3,15},{4,0},{5,1},{6,2},{7,3},{8,4},{9,5},{1... | collective-permute-start | bytes 1253384 | tf_op jit(solution)/shard_map/ppermute | solution.py:379
  27.5 20.9 %collective-permute-start.5 = (bf16[2,816,128]{2,1,0:T(8,128)(2,1)S(1)}, bf16[2,816,128]{2,1,0:T(8,128)(2,1)S(1)}, u32[]{:S(2)}, u32[]{:S(2)}) collective-permute-start(bf16[2,816,128]{2,1,0:T(8,128)(2,1)S(1)} %pad_maximum_fusion.1.refs_0_), channel_id=1, source_target_pairs={{0,8},{1,9},{2,10},{3,11},{4,12},{5,13},{6,14},{7,15},{8,0},{9,1},... | collective-permute-start | bytes 1253384 | tf_op jit(solution)/shard_map/ppermute | solution.py:379
  28.6 19.8 %collective-permute-start.4 = (bf16[2,816,128]{2,1,0:T(8,128)(2,1)S(1)}, bf16[2,816,128]{2,1,0:T(8,128)(2,1)S(1)}, u32[]{:S(2)}, u32[]{:S(2)}) collective-permute-start(bf16[2,816,128]{2,1,0:T(8,128)(2,1)S(1)} %pad_maximum_fusion.1.refs_0_), channel_id=1, source_target_pairs={{0,4},{1,5},{2,6},{3,7},{4,8},{5,9},{6,10},{7,11},{8,12},{9,13},{1... | collective-permute-start | bytes 1253384 | tf_op jit(solution)/shard_map/ppermute | solution.py:379
  43.5 10.9 %collective-permute-start.10 = (bf16[2,416,128]{2,1,0:T(8,128)(2,1)S(1)}, bf16[2,416,128]{2,1,0:T(8,128)(2,1)S(1)}, u32[]{:S(2)}, u32[]{:S(2)}) collective-permute-start(bf16[2,416,128]{2,1,0:T(8,128)(2,1)S(1)} %slice.110), channel_id=1, source_target_pairs={{0,192},{16,208},{32,224},{48,240},{64,0},{80,16},{96,32},{112,48}... | collective-permute-start | bytes 638984 | tf_op jit(solution)/shard_map/ppermute | solution.py:374
  48.2 10.9 %collective-permute-start.8 = (bf16[2,416,128]{2,1,0:T(8,128)(2,1)S(1)}, bf16[2,416,128]{2,1,0:T(8,128)(2,1)S(1)}, u32[]{:S(2)}, u32[]{:S(2)}) collective-permute-start(bf16[2,416,128]{2,1,0:T(8,128)(2,1)S(1)} %slice.109), channel_id=1, source_target_pairs={{0,64},{16,80},{32,96},{48,112},{64,128},{80,144},{96,160},{112,17... | collective-permute-start | bytes 638984 | tf_op jit(solution)/shard_map/ppermute | solution.py:374
  59.1 4.3 %collective-permute-start.11 = (bf16[2,816,128]{2,1,0:T(8,128)(2,1)S(1)}, bf16[2,816,128]{2,1,0:T(8,128)(2,1)S(1)}, u32[]{:S(2)}, u32[]{:S(2)}) collective-permute-start(bf16[2,816,128]{2,1,0:T(8,128)(2,1)S(1)} %pad_maximum_fusion.1.refs_0_), channel_id=1, source_target_pairs={{0,1},{1,0},{2,3},{3,2},{4,5},{5,4},{6,7},{7,6},{8,9},{9,8},{10,11... | collective-permute-start | bytes 1253384 | tf_op jit(solution)/shard_map/ppermute | solution.py:381
  59.1 4.3 %collective-permute-start.12 = (bf16[2,816,128]{2,1,0:T(8,128)(2,1)S(1)}, bf16[2,816,128]{2,1,0:T(8,128)(2,1)S(1)}, u32[]{:S(2)}, u32[]{:S(2)}) collective-permute-start(bf16[2,816,128]{2,1,0:T(8,128)(2,1)S(1)} %collective-permute-done.4.refs_1_), channel_id=1, source_target_pairs={{0,1},{1,0},{2,3},{3,2},{4,5},{5,4},{6,7},{7,6},{8,9},{9,8},{10,11... | collective-permute-start | bytes 1253384 | tf_op jit(solution)/shard_map/ppermute | solution.py:381
  59.6 6.0 %collective-permute-start.13 = (bf16[2,816,128]{2,1,0:T(8,128)(2,1)S(1)}, bf16[2,816,128]{2,1,0:T(8,128)(2,1)S(1)}, u32[]{:S(2)}, u32[]{:S(2)}) collective-permute-start(bf16[2,816,128]{2,1,0:T(8,128)(2,1)S(1)} %collective-permute-done.5.refs_2_), channel_id=1, source_target_pairs={{0,1},{1,0},{2,3},{3,2},{4,5},{5,4},{6,7},{7,6},{8,9},{9,8},{10,11... | collective-permute-start | bytes 1253384 | tf_op jit(solution)/shard_map/ppermute | solution.py:381
  59.6 6.0 %collective-permute-start.14 = (bf16[2,816,128]{2,1,0:T(8,128)(2,1)S(1)}, bf16[2,816,128]{2,1,0:T(8,128)(2,1)S(1)}, u32[]{:S(2)}, u32[]{:S(2)}) collective-permute-start(bf16[2,816,128]{2,1,0:T(8,128)(2,1)S(1)} %collective-permute-done.6.refs_3_), channel_id=1, source_target_pairs={{0,1},{1,0},{2,3},{3,2},{4,5},{5,4},{6,7},{7,6},{8,9},{9,8},{10,11... | collective-permute-start | bytes 1253384 | tf_op jit(solution)/shard_map/ppermute | solution.py:381
  60.1 12.0 %collective-permute-start.15 = (bf16[512,128]{1,0:T(8,128)(2,1)S(1)}, bf16[512,128]{1,0:T(8,128)(2,1)S(1)}, u32[]{:S(2)}, u32[]{:S(2)}) collective-permute-start(bf16[512,128]{1,0:T(8,128)(2,1)S(1)} %copy-done.9), channel_id=1, source_target_pairs={{0,16},{16,0},{32,48},{48,32},{64,80},{80,64},{96,112},{112,96},{1... | collective-permute-start | bytes 393224 | tf_op jit(solution)/shard_map/ppermute | solution.py:376
  63.4 8.7 %collective-permute-start.16 = (bf16[512,128]{1,0:T(8,128)(2,1)S(1)}, bf16[512,128]{1,0:T(8,128)(2,1)S(1)}, u32[]{:S(2)}, u32[]{:S(2)}) collective-permute-start(bf16[512,128]{1,0:T(8,128)(2,1)S(1)} %copy-done.8), channel_id=1, source_target_pairs={{0,32},{16,48},{32,0},{48,16},{64,96},{80,112},{96,64},{112,80},{1... | collective-permute-start | bytes 393224 | tf_op jit(solution)/shard_map/ppermute | solution.py:376
  63.4 8.7 %collective-permute-start.17 = (bf16[512,128]{1,0:T(8,128)(2,1)S(1)}, bf16[512,128]{1,0:T(8,128)(2,1)S(1)}, u32[]{:S(2)}, u32[]{:S(2)}) collective-permute-start(bf16[512,128]{1,0:T(8,128)(2,1)S(1)} %copy-done.7), channel_id=1, source_target_pairs={{0,48},{16,32},{32,16},{48,0},{64,112},{80,96},{96,80},{112,64},{1... | collective-permute-start | bytes 393224 | tf_op jit(solution)/shard_map/ppermute | solution.py:376
  66.9 5.3 %copy-start.3 = (bf16[512,128]{1,0:T(8,128)(2,1)S(1)}, bf16[512,128]{1,0:T(8,128)(2,1)}, u32[]{:S(2)}) copy-start(bf16[512,128]{1,0:T(8,128)(2,1)} %get-tuple-element.59.og0) | copy-start | bytes 393220
  79.1 6.4 %copy-start.5 = (bf16[3840,128]{1,0:T(8,128)(2,1)S(1)}, bf16[3840,128]{1,0:T(8,128)(2,1)}, u32[]{:S(2)}) copy-start(bf16[3840,128]{1,0:T(8,128)(2,1)} %get-tuple-element.71) | copy-start | bytes 2949124
  79.1 49.4 %all-to-all-start = ((bf16[16,13,32,128]{3,2,1,0:T(8,128)(2,1)}), bf16[16,13,32,128]{3,2,1,0:T(8,128)(2,1)S(1)}, u32[]{:S(2)}, u32[]{:S(2)}) async-start(bf16[16,13,32,128]{3,2,1,0:T(8,128)(2,1)} %get-tuple-element.80), calls=%async_computation | async-start | bytes 3407872 | tf_op jit(solution)/shard_map/all_to_all | solution.py:396
  85.3 5.8 %collective-permute-start.18 = (bf16[7680,128]{1,0:T(8,128)(2,1)}, bf16[7680,128]{1,0:T(8,128)(2,1)}, u32[]{:S(2)}, u32[]{:S(2)}) collective-permute-start(bf16[7680,128]{1,0:T(8,128)(2,1)} %get-tuple-element.70.mine), channel_id=1, source_target_pairs={{0,1},{1,0},{2,3},{3,2},{4,5},{5,4},{6,7},{7,6},{8,9},{9,8},{10,11... | collective-permute-start | bytes 5898248 | tf_op jit(solution)/shard_map/ppermute | solution.py:398
  85.4 5.1 %collective-permute-start.19 = (bf16[3840,128]{1,0:T(8,128)(2,1)S(1)}, bf16[3840,128]{1,0:T(8,128)(2,1)S(1)}, u32[]{:S(2)}, u32[]{:S(2)}) collective-permute-start(bf16[3840,128]{1,0:T(8,128)(2,1)S(1)} %copy-done.5), channel_id=1, source_target_pairs={{0,1},{1,0},{2,3},{3,2},{4,5},{5,4},{6,7},{7,6},{8,9},{9,8},{10,11... | collective-permute-start | bytes 2949128 | tf_op jit(solution)/shard_map/ppermute | solution.py:394
  90.5 0.9 copy-start.6
  98.9 10.1 %collective-permute-start.20 = (bf16[2,2,144,256]{3,2,1,0:T(8,128)(2,1)}, bf16[2,2,144,256]{3,2,1,0:T(8,128)(2,1)S(1)}, u32[]{:S(2)}, u32[]{:S(2)}) collective-permute-start(bf16[2,2,144,256]{3,2,1,0:T(8,128)(2,1)} %get-tuple-element.75), channel_id=1, source_target_pairs={{0,4},{1,5},{2,6},{3,7},{4,8},{5,9},{6,10},{7,11},{8,12},{9,13},{1... | collective-permute-start | bytes 884744 | tf_op jit(solution)/shard_map/ppermute | solution.py:401
  99.5 11.6 %collective-permute-start.21 = (bf16[2,2,144,256]{3,2,1,0:T(8,128)(2,1)}, bf16[2,2,144,256]{3,2,1,0:T(8,128)(2,1)S(1)}, u32[]{:S(2)}, u32[]{:S(2)}) collective-permute-start(bf16[2,2,144,256]{3,2,1,0:T(8,128)(2,1)} %get-tuple-element.76), channel_id=1, source_target_pairs={{0,8},{1,9},{2,10},{3,11},{4,12},{5,13},{6,14},{7,15},{8,0},{9,1},... | collective-permute-start | bytes 884744 | tf_op jit(solution)/shard_map/ppermute | solution.py:401
  101.9 14.5 %collective-permute-start.22 = (bf16[2,2,144,256]{3,2,1,0:T(8,128)(2,1)}, bf16[2,2,144,256]{3,2,1,0:T(8,128)(2,1)S(1)}, u32[]{:S(2)}, u32[]{:S(2)}) collective-permute-start(bf16[2,2,144,256]{3,2,1,0:T(8,128)(2,1)} %get-tuple-element.77), channel_id=1, source_target_pairs={{0,12},{1,13},{2,14},{3,15},{4,0},{5,1},{6,2},{7,3},{8,4},{9,5},{1... | collective-permute-start | bytes 884744 | tf_op jit(solution)/shard_map/ppermute | solution.py:401
  101.9 34.3 %collective-permute-start.25 = (bf16[4,2,144,256]{3,2,1,0:T(8,128)(2,1)}, bf16[4,2,144,256]{3,2,1,0:T(8,128)(2,1)S(1)}, u32[]{:S(2)}, u32[]{:S(2)}) collective-permute-start(bf16[4,2,144,256]{3,2,1,0:T(8,128)(2,1)} %get-tuple-element.79), channel_id=1, source_target_pairs={{0,2},{1,3},{2,0},{3,1},{4,6},{5,7},{6,4},{7,5},{8,10},{9,11},{10,... | collective-permute-start | bytes 1769480 | tf_op jit(solution)/shard_map/ppermute | solution.py:400
  118.2 18.0 %copy-start.4 = (bf16[4,2,144,256]{3,2,1,0:T(8,128)(2,1)S(1)}, bf16[4,2,144,256]{3,2,1,0:T(8,128)(2,1)}, u32[]{:S(2)}) copy-start(bf16[4,2,144,256]{3,2,1,0:T(8,128)(2,1)} %get-tuple-element.78) | copy-start | bytes 1769476
  118.2 17.0 %collective-permute-start.23 = (bf16[2,144,256]{2,1,0:T(8,128)(2,1)}, bf16[2,144,256]{2,1,0:T(8,128)(2,1)}, u32[]{:S(2)}, u32[]{:S(2)}) collective-permute-start(bf16[2,144,256]{2,1,0:T(8,128)(2,1)} %fusion.9), channel_id=1, source_target_pairs={{0,2},{1,3},{2,0},{3,1},{4,6},{5,7},{6,4},{7,5},{8,10},{9,11},{10,... | collective-permute-start | bytes 442376 | tf_op jit(solution)/shard_map/ppermute | solution.py:403
  129.5 23.0 %all-to-all-start.1 = ((bf16[16,4,32,128]{3,2,1,0:T(8,128)(2,1)}), bf16[16,4,32,128]{3,2,1,0:T(8,128)(2,1)S(1)}, u32[]{:S(2)}, u32[]{:S(2)}) async-start(bf16[16,4,32,128]{3,2,1,0:T(8,128)(2,1)} %block_strips.1), calls=%async_computation.1 | async-start | bytes 1048576 | tf_op jit(solution)/shard_map/all_to_all | solution.py:410
  136.3 8.0 %collective-permute-start.26 = (bf16[2,144,256]{2,1,0:T(8,128)(2,1)S(1)}, bf16[2,144,256]{2,1,0:T(8,128)(2,1)S(1)}, u32[]{:S(2)}, u32[]{:S(2)}) collective-permute-start(bf16[2,144,256]{2,1,0:T(8,128)(2,1)S(1)} %get-tuple-element.89), channel_id=1, source_target_pairs={{0,4},{1,5},{2,6},{3,7},{4,8},{5,9},{6,10},{7,11},{8,12},{9,13},{1... | collective-permute-start | bytes 442376 | tf_op jit(solution)/shard_map/ppermute | solution.py:405
  138.3 9.3 %collective-permute-start.28 = (bf16[2,144,256]{2,1,0:T(8,128)(2,1)S(1)}, bf16[2,144,256]{2,1,0:T(8,128)(2,1)S(1)}, u32[]{:S(2)}, u32[]{:S(2)}) collective-permute-start(bf16[2,144,256]{2,1,0:T(8,128)(2,1)S(1)} %get-tuple-element.90), channel_id=1, source_target_pairs={{0,12},{1,13},{2,14},{3,15},{4,0},{5,1},{6,2},{7,3},{8,4},{9,5},{1... | collective-permute-start | bytes 442376 | tf_op jit(solution)/shard_map/ppermute | solution.py:405
  138.4 9.2 %collective-permute-start.27 = (bf16[2,144,256]{2,1,0:T(8,128)(2,1)S(1)}, bf16[2,144,256]{2,1,0:T(8,128)(2,1)S(1)}, u32[]{:S(2)}, u32[]{:S(2)}) collective-permute-start(bf16[2,144,256]{2,1,0:T(8,128)(2,1)S(1)} %get-tuple-element.91), channel_id=1, source_target_pairs={{0,8},{1,9},{2,10},{3,11},{4,12},{5,13},{6,14},{7,15},{8,0},{9,1},... | collective-permute-start | bytes 442376 | tf_op jit(solution)/shard_map/ppermute | solution.py:405
  140.9 13.6 %collective-permute-start.24 = (bf16[144,256]{1,0:T(8,128)(2,1)S(1)}, bf16[144,256]{1,0:T(8,128)(2,1)S(1)}, u32[]{:S(2)}, u32[]{:S(2)}) collective-permute-start(bf16[144,256]{1,0:T(8,128)(2,1)S(1)} %get-tuple-element.96), channel_id=1, source_target_pairs={{0,16},{16,0},{32,48},{48,32},{64,80},{80,64},{96,112},{112,96},{1... | collective-permute-start | bytes 221192 | tf_op jit(solution)/shard_map/ppermute | solution.py:408
  147.7 6.8 %collective-permute-start.30 = (bf16[144,256]{1,0:T(8,128)(2,1)S(1)}, bf16[144,256]{1,0:T(8,128)(2,1)S(1)}, u32[]{:S(2)}, u32[]{:S(2)}) collective-permute-start(bf16[144,256]{1,0:T(8,128)(2,1)S(1)} %get-tuple-element.94), channel_id=1, source_target_pairs={{0,48},{16,32},{32,16},{48,0},{64,112},{80,96},{96,80},{112,64},{1... | collective-permute-start | bytes 221192 | tf_op jit(solution)/shard_map/ppermute | solution.py:408
  151.3 4.4 %collective-permute-start.29 = (bf16[144,256]{1,0:T(8,128)(2,1)S(1)}, bf16[144,256]{1,0:T(8,128)(2,1)S(1)}, u32[]{:S(2)}, u32[]{:S(2)}) collective-permute-start(bf16[144,256]{1,0:T(8,128)(2,1)S(1)} %get-tuple-element.95), channel_id=1, source_target_pairs={{0,32},{16,48},{32,0},{48,16},{64,96},{80,112},{96,64},{112,80},{1... | collective-permute-start | bytes 221192 | tf_op jit(solution)/shard_map/ppermute | solution.py:408
